TPU v7x, 32 devices: a whole 2x2x4 slice. The times are simulated.
32 devices in a mesh: groups: 2 (over y), side: 4 (over x, core), tp: 4 (over z).
Axes of the slice: x: 2, y: 2, z: 4, core: 2. Of those that a mesh axis runs over, the one named last changes fastest.
Arguments:
- tokens: bfloat16 [128, 6144], P(('groups', 'side', 'tp')), parts along dimension 0, may hold values from -6 to 6
- queries: bfloat16 [128, 6144], P(('groups', 'side', 'tp')), parts along dimension 0, may hold values from -120 to 120
- stored_keys: bfloat16 [128, 128, 1024], P(('groups', 'side', 'tp')), parts along dimension 0, may hold values from -4 to 4
- stored_values: bfloat16 [128, 128, 1024], P(('groups', 'side', 'tp')), parts along dimension 0, may hold values from -6 to 6
- lengths: int32 [128], P(('groups', 'side', 'tp')), parts along dimension 0, may hold values from 2 to 128, as said below
- norm_gain: float32 [6144], replicated, may hold values from 0.1 to 1.9
- routes: int32 [128, 2], P(('groups', 'side', 'tp')), parts along dimension 0, may hold values from 0 to 3, all different within a row; in each aligned block of 2 rows (0 to 1, 2 to 3, ...) at most 2 rows name the same one
- route_weights: float32 [128, 2], P(('groups', 'side', 'tp')), parts along dimension 0, may hold values from 0.2 to 1
- gate_up: bfloat16 [4, 2, 5376, 6144], P('side', None, 'tp'), may hold values from -0.078125 to 0.078125
- down_proj: bfloat16 [4, 5376, 6144], P('side', 'tp'), may hold values from -0.078125 to 0.078125
Outputs:
- mixed: bfloat16 [128, 6144], P(('groups', 'side', 'tp')), parts along dimension 0
There are 2 independent parts, one for each index of `groups`. A program takes and returns all parts, laid end to end along the dimension named above; an argument that names none is the same for every part. Nothing has to cross between parts.
Inputs may be any that keep to these rules, and one draw needn't show every extreme that they name: `routes`: each row names 2 different experts; in each aligned block of 2 rows no expert is named by more than 2 rows, and in some blocks one is named by exactly 2. `lengths`: some sequences use all 128 positions.
All inputs are finite; a program needn't handle non-finite values.
Results may differ from a plain program's by a relative error of at most 0.0051.
Values may be sent and summed in bfloat16 or wider, within the bound.
No kernel may reach another device: no remote copies, remote signals or barrier semaphores. Data moves between devices by JAX's collectives and lax.ppermute only.
A program may use at most 128 MiB of HBM per device.

v0:
```python
import math

import jax
import jax.numpy as jnp
from jax import lax
from jax.sharding import PartitionSpec as P

QUERY_HEADS = 48
KEY_VALUE_HEADS = 8
HEAD_SIZE = 128
MICRO = 2
CAP = 2


def attend_norm(tokens, queries, stored_keys, stored_values, lengths, norm_gain):
    local_rows = tokens.shape[0]
    cache_positions = stored_keys.shape[1]
    query_head_rows = queries.reshape(
        local_rows, KEY_VALUE_HEADS, QUERY_HEADS // KEY_VALUE_HEADS, HEAD_SIZE
    )
    key_head_rows = stored_keys.reshape(local_rows, cache_positions, KEY_VALUE_HEADS, HEAD_SIZE)
    value_head_rows = stored_values.reshape(local_rows, cache_positions, KEY_VALUE_HEADS, HEAD_SIZE)
    scores = jnp.einsum(
        "tkgd,tlkd->tkgl", query_head_rows, key_head_rows, preferred_element_type=jnp.float32
    ) / math.sqrt(HEAD_SIZE)
    alive_mask = (jnp.arange(cache_positions)[None, :] < lengths[:, None])[:, None, None, :]
    scores = jnp.where(alive_mask, scores, jnp.float32(-1e30))
    peak = jnp.max(scores, axis=-1, keepdims=True)
    expo = jnp.where(alive_mask, jnp.exp(scores - peak), jnp.float32(0.0))
    probabilities = (expo / jnp.sum(expo, axis=-1, keepdims=True)).astype(jnp.bfloat16)
    attended = jnp.einsum(
        "tkgl,tlkd->tkgd", probabilities, value_head_rows, preferred_element_type=jnp.float32
    )
    resid = tokens.astype(jnp.float32) + attended.reshape(local_rows, QUERY_HEADS * HEAD_SIZE)
    scale = lax.rsqrt(jnp.mean(resid * resid, axis=-1, keepdims=True) + 1e-05)
    normed = (resid * scale * norm_gain[None, :]).astype(jnp.bfloat16)
    return (resid, normed)


def shards(
    tokens,
    queries,
    stored_keys,
    stored_values,
    lengths,
    norm_gain,
    routes,
    route_weights,
    gate_up,
    down_proj,
):
    n_side = lax.axis_size("side")
    n_tensor = lax.axis_size("tp")
    width = tokens.shape[1]
    choose = routes.shape[1]
    micro_rows = tokens.shape[0] // MICRO
    local_gu = gate_up[0]
    local_down = down_proj[0]
    pieces = []
    for micro_index in range(MICRO):
        lower = micro_index * micro_rows
        upper = lower + micro_rows
        resid, normed = attend_norm(
            tokens[lower:upper],
            queries[lower:upper],
            stored_keys[lower:upper],
            stored_values[lower:upper],
            lengths[lower:upper],
            norm_gain,
        )
        chosen = routes[lower:upper]
        flat_routes = chosen.reshape(1, micro_rows * choose)
        onehot = (
            flat_routes[:, :, None] == jnp.arange(n_side, dtype=jnp.int32)[None, None, :]
        ).astype(jnp.int32)
        before = jnp.cumsum(onehot, axis=1) - onehot
        slot_index = jnp.sum(before * onehot, axis=-1).reshape(micro_rows, choose)
        destination = chosen * CAP + slot_index
        selector = jnp.any(
            destination[:, :, None] == jnp.arange(n_side * CAP, dtype=jnp.int32)[None, None, :],
            axis=1,
        )
        outgoing = jnp.dot(
            selector.astype(jnp.bfloat16).T, normed, preferred_element_type=jnp.float32
        ).astype(jnp.bfloat16)
        repeated = jnp.broadcast_to(
            outgoing.reshape(n_side, 1, CAP, width), (n_side, n_tensor, CAP, width)
        )
        repeated = repeated.reshape(n_side * n_tensor * CAP, width)
        arrived = lax.all_to_all(repeated, ("side", "tp"), split_axis=0, concat_axis=0, tiled=True)
        both = jnp.einsum("rd,cfd->rcf", arrived, local_gu, preferred_element_type=jnp.float32)
        hidden = (jax.nn.silu(both[:, 0]) * both[:, 1]).astype(jnp.bfloat16)
        partial_value = jnp.dot(hidden, local_down, preferred_element_type=jnp.float32).astype(
            jnp.bfloat16
        )
        gathered = lax.all_to_all(
            partial_value, ("side", "tp"), split_axis=0, concat_axis=0, tiled=True
        )
        summed = jnp.sum(gathered.reshape(n_side, n_tensor, CAP, width).astype(jnp.float32), axis=1)
        returned = summed.astype(jnp.bfloat16).reshape(n_side * CAP, width)
        picked_rows = returned[destination].astype(jnp.float32)
        weights_here = route_weights[lower:upper]
        mixed_part = resid + jnp.sum(weights_here[:, :, None] * picked_rows, axis=1)
        pieces.append(mixed_part.astype(jnp.bfloat16))
    return jnp.concatenate(pieces, axis=0)


def solution(mesh):
    placed = (
        P(("groups", "side", "tp"), None),
        P(("groups", "side", "tp"), None),
        P(("groups", "side", "tp"), None, None),
        P(("groups", "side", "tp"), None, None),
        P(("groups", "side", "tp")),
        P(),
        P(("groups", "side", "tp"), None),
        P(("groups", "side", "tp"), None),
        P("side", None, "tp", None),
        P("side", "tp", None),
    )
    return jax.shard_map(
        shards,
        mesh=mesh,
        in_specs=placed,
        out_specs=P(("groups", "side", "tp"), None),
        check_vma=False,
    )
```

profile of v0, /device:TPU:0, one launch (start us, length us, event | category | flops | bytes accessed | tf_op | source)
XLA Modules:
  0.0 113.7 jit_solution(14230670013273550609)
XLA Ops:
  0.0 0.8 fusion.45
  0.8 0.8 fusion.44
  2.3 0.9 fusion.42
  3.3 1.3 %fusion.40 = (bf16[2,128,1024]{2,1,0:T(8,128)(2,1)S(1)}, bf16[2,128,1024]{2,1,0:T(8,128)(2,1)S(1)}) fusion(bf16[4,128,1024]{2,1,0:T(8,128)(2,1)} %param.12), kind=kLoop, calls=%fused_computation.73 | loop fusion | bytes 2097152 | tf_op jit(solution)/shard_map/slice | solution.py:66
  6.1 1.3 %fusion.41 = (bf16[2,128,1024]{2,1,0:T(8,128)(2,1)S(1)}, bf16[2,128,1024]{2,1,0:T(8,128)(2,1)S(1)}) fusion(bf16[4,128,1024]{2,1,0:T(8,128)(2,1)} %param.13), kind=kLoop, calls=%fused_computation.74 | loop fusion | bytes 2097152 | tf_op jit(solution)/shard_map/slice | solution.py:67
  8.9 1.1 multiply_reduce_fusion.3
  10.0 1.1 convolution_convert_fusion.1
  11.1 1.0 broadcast_in_dim.74
  12.1 7.4 %all-to-all-start = ((bf16[16,2,6144]{2,1,0:T(2,128)(2,1)}), bf16[16,2,6144]{2,1,0:T(2,128)(2,1)S(1)}, u32[]{:S(2)}, u32[]{:S(2)}) async-start(bf16[16,2,6144]{2,1,0:T(2,128)(2,1)} %bitcast.2), calls=%async_computation | async-start | bytes 786432 | tf_op jit(solution)/shard_map/all_to_all | solution.py:90
  20.1 1.0 convolution_convert_fusion
  21.2 11.1 %all-to-all-done = bf16[16,2,6144]{2,1,0:T(2,128)(2,1)S(1)} async-done(((bf16[16,2,6144]{2,1,0:T(2,128)(2,1)}), bf16[16,2,6144]{2,1,0:T(2,128)(2,1)S(1)}, u32[]{:S(2)}, u32[]{:S(2)}) %all-to-all-start) | async-done | bytes 393248 | tf_op jit(solution)/shard_map/all_to_all | solution.py:90
  32.3 1.0 broadcast_in_dim.78
  33.3 3.6 %all-to-all-start.2 = ((bf16[16,2,6144]{2,1,0:T(2,128)(2,1)}), bf16[16,2,6144]{2,1,0:T(2,128)(2,1)S(1)}, u32[]{:S(2)}, u32[]{:S(2)}) async-start(bf16[16,2,6144]{2,1,0:T(2,128)(2,1)} %bitcast.9), calls=%async_computation.2 | async-start | bytes 786432 | tf_op jit(solution)/shard_map/all_to_all | solution.py:90
  37.0 15.0 %fusion.4 = f32[32,2,1344]{2,0,1:T(8,128)S(1)} fusion(bf16[32,6144,1]{1,0,2:T(8,128)(2,1)S(1)} %reshape.343, bf16[1,2,1344,6144]{3,2,1,0:T(8,128)(2,1)} %param.18), kind=kOutput, calls=%fused_computation.6 | convolution fusion | flops 1056964608 | bytes 33767424 | tf_op jit(solution)/shard_map/rd,cfd->rcf/dot_general | solution.py:91
  52.0 8.6 %fusion.10 = bf16[32,6144]{1,0:T(8,128)(2,1)S(1)} fusion(bf16[1,1344,6144]{2,1,0:T(8,128)(2,1)} %param.19, f32[32,2,1344]{2,0,1:T(8,128)S(1)} %fusion.4), kind=kOutput, calls=%fused_computation.12 | convolution fusion | flops 528936960 | bytes 17252352 | tf_op jit(solution)/shard_map/dot_general | solution.py:93
  60.6 1.0 all_to_all.31
  61.7 6.0 %all-to-all-start.1 = ((bf16[16,2,6144]{2,1,0:T(2,128)(2,1)}), bf16[16,2,6144]{2,1,0:T(2,128)(2,1)S(1)}, u32[]{:S(2)}, u32[]{:S(2)}) async-start(bf16[16,2,6144]{2,1,0:T(2,128)(2,1)} %all_to_all.31), calls=%async_computation.1 | async-start | bytes 786432 | tf_op jit(solution)/shard_map/all_to_all | solution.py:96
  67.8 15.0 %fusion.2 = f32[32,2,1344]{2,0,1:T(8,128)S(1)} fusion(bf16[32,6144,1]{1,0,2:T(8,128)(2,1)S(1)} %reshape.344, bf16[1,2,1344,6144]{3,2,1,0:T(8,128)(2,1)} %param.18), kind=kOutput, calls=%fused_computation.4 | convolution fusion | flops 1056964608 | bytes 33767424 | tf_op jit(solution)/shard_map/rd,cfd->rcf/dot_general | solution.py:91
  82.8 8.6 %fusion.13 = bf16[32,6144]{1,0:T(8,128)(2,1)S(1)} fusion(bf16[1,1344,6144]{2,1,0:T(8,128)(2,1)} %param.19, f32[32,2,1344]{2,0,1:T(8,128)S(1)} %fusion.2), kind=kOutput, calls=%fused_computation.13 | convolution fusion | flops 528936960 | bytes 17252352 | tf_op jit(solution)/shard_map/dot_general | solution.py:93
  91.5 1.0 all_to_all.36
  92.5 6.0 %all-to-all-start.3 = ((bf16[16,2,6144]{2,1,0:T(2,128)(2,1)}), bf16[16,2,6144]{2,1,0:T(2,128)(2,1)S(1)}, u32[]{:S(2)}, u32[]{:S(2)}) async-start(bf16[16,2,6144]{2,1,0:T(2,128)(2,1)} %all_to_all.36), calls=%async_computation.3 | async-start | bytes 786432 | tf_op jit(solution)/shard_map/all_to_all | solution.py:96
  99.4 0.6 gather_fusion
  100.1 11.3 %all-to-all-done.3 = bf16[16,2,6144]{2,1,0:T(2,128)(2,1)S(1)} async-done(((bf16[16,2,6144]{2,1,0:T(2,128)(2,1)}), bf16[16,2,6144]{2,1,0:T(2,128)(2,1)S(1)}, u32[]{:S(2)}, u32[]{:S(2)}) %all-to-all-start.3) | async-done | bytes 393248 | tf_op jit(solution)/shard_map/all_to_all | solution.py:96
  113.1 0.6 copy-done.2
  (62 shorter events, 7.4 us)
Async XLA Ops:
  12.1 20.2 %all-to-all-start = ((bf16[16,2,6144]{2,1,0:T(2,128)(2,1)}), bf16[16,2,6144]{2,1,0:T(2,128)(2,1)S(1)}, u32[]{:S(2)}, u32[]{:S(2)}) async-start(bf16[16,2,6144]{2,1,0:T(2,128)(2,1)} %bitcast.2), calls=%async_computation | async-start | bytes 786432 | tf_op jit(solution)/shard_map/all_to_all | solution.py:90
  33.3 28.4 %all-to-all-start.2 = ((bf16[16,2,6144]{2,1,0:T(2,128)(2,1)}), bf16[16,2,6144]{2,1,0:T(2,128)(2,1)S(1)}, u32[]{:S(2)}, u32[]{:S(2)}) async-start(bf16[16,2,6144]{2,1,0:T(2,128)(2,1)} %bitcast.9), calls=%async_computation.2 | async-start | bytes 786432 | tf_op jit(solution)/shard_map/all_to_all | solution.py:90
  61.7 30.8 %all-to-all-start.1 = ((bf16[16,2,6144]{2,1,0:T(2,128)(2,1)}), bf16[16,2,6144]{2,1,0:T(2,128)(2,1)S(1)}, u32[]{:S(2)}, u32[]{:S(2)}) async-start(bf16[16,2,6144]{2,1,0:T(2,128)(2,1)} %all_to_all.31), calls=%async_computation.1 | async-start | bytes 786432 | tf_op jit(solution)/shard_map/all_to_all | solution.py:96
  67.6 31.1 %copy-start.1 = (f32[4,2]{0,1:T(2,128)S(1)}, f32[4,2]{0,1:T(2,128)}, u32[]{:S(2)}) copy-start(f32[4,2]{0,1:T(2,128)} %param.17) | copy-start | bytes 100
  67.8 45.1 %copy-start = (bf16[4,6144]{1,0:T(4,128)(2,1)S(1)}, bf16[4,6144]{1,0:T(4,128)(2,1)}, u32[]{:S(2)}) copy-start(bf16[4,6144]{1,0:T(4,128)(2,1)} %param.10) | copy-start | bytes 147460
  92.5 18.9 %all-to-all-start.3 = ((bf16[16,2,6144]{2,1,0:T(2,128)(2,1)}), bf16[16,2,6144]{2,1,0:T(2,128)(2,1)S(1)}, u32[]{:S(2)}, u32[]{:S(2)}) async-start(bf16[16,2,6144]{2,1,0:T(2,128)(2,1)} %all_to_all.36), calls=%async_computation.3 | async-start | bytes 786432 | tf_op jit(solution)/shard_map/all_to_all | solution.py:96
  113.0 0.6 copy-start.2
where the time goes:
time: 115 us; the launch traced here: 114 us
  matrix products  50.7 us (44%)
  starting transfers between devices  22.9 us (20%)
  waiting for transfers between devices  22.4 us (19%)
  local copies, waits for them, and re-layouts  13.7 us (12%)
  other arithmetic  3.7 us (3%)
    dot_general x2, matrix products, shards(): jnp.einsum('rd,cfd->rcf', arrived, local_gu, preferred_element_type=jnp.f...  30.1 us
    dot_general x2, matrix products, shards(): jnp.dot(hidden, local_down, preferred_element_type=jnp.float32)  17.2 us
    all_to_all x2, starting transfers between devices, shards(): lax.all_to_all(partial_value, ('side', 'tp'), split_axis=0, concat_axis=0...  11.9 us
    all_to_all x2, waiting for transfers between devices, shards(): lax.all_to_all(partial_value, ('side', 'tp'), split_axis=0, concat_axis=0...  11.3 us
    all_to_all x2, waiting for transfers between devices, shards(): lax.all_to_all(repeated, ('side', 'tp'), split_axis=0, concat_axis=0, til...  11.1 us
    all_to_all x2, starting transfers between devices, shards(): lax.all_to_all(repeated, ('side', 'tp'), split_axis=0, concat_axis=0, til...  10.9 us
  transfers between devices with their start and end apart: 4, of which 2 were waited for; matrix products, arithmetic and copies ran while one was open for 45% of the time, Pallas kernels for 0%

commit v1 on v0

v1 whole, which is shorter than its diff:
```python
import functools
import math

import jax
import jax.numpy as jnp
from jax import lax
from jax.experimental import pallas as pl
from jax.experimental.pallas import tpu as pltpu
from jax.sharding import PartitionSpec as P

HEAD_SIZE = 128
LANES = 128
F32 = jnp.float32
BF16 = jnp.bfloat16


def attend_kernel(
    lengths, routes, weights, tokens, queries, gain, keys_hbm, values_hbm,
    resid_ref, row_ref, keys, values, key_sems, value_sems,
):
    rows, positions, kv_width = keys_hbm.shape
    width = tokens.shape[1]
    n_kv = kv_width // HEAD_SIZE
    per = width // kv_width
    key_copies = [
        pltpu.make_async_copy(keys_hbm.at[t], keys.at[t], key_sems.at[t]) for t in range(rows)
    ]
    value_copies = [
        pltpu.make_async_copy(values_hbm.at[t], values.at[t], value_sems.at[t])
        for t in range(rows)
    ]
    for copy in key_copies + value_copies:
        copy.start()
    block = per * rows
    owner = lax.broadcasted_iota(jnp.int32, (block, 1), 0) % rows
    length = jnp.zeros((block, 1), jnp.int32)
    for t in range(rows):
        length = jnp.where(owner == t, lengths[t], length)
    alive = lax.broadcasted_iota(jnp.int32, (block, positions), 1) < length
    q = queries[...].astype(F32)
    stacked = []
    for g in range(n_kv):
        heads = [
            q[:, (g * per + j) * HEAD_SIZE : (g * per + j + 1) * HEAD_SIZE] for j in range(per)
        ]
        stacked.append(jnp.concatenate(heads, axis=0))
    for copy in key_copies:
        copy.wait()
    scores = []
    for g in range(n_kv):
        total = jnp.zeros((block, positions), F32)
        for t in range(rows):
            mine = jnp.where(owner == t, stacked[g], 0.0).astype(BF16)
            total += lax.dot_general(
                mine, keys[t, :, g * HEAD_SIZE : (g + 1) * HEAD_SIZE],
                (((1,), (1,)), ((), ())), preferred_element_type=F32,
            )
        scores.append(total)
    probs = []
    for g in range(n_kv):
        s = jnp.where(alive, scores[g] / math.sqrt(HEAD_SIZE), -1e30)
        peak = jnp.max(s, axis=1, keepdims=True)
        e = jnp.where(alive, jnp.exp(s - peak), 0.0)
        probs.append((e / jnp.sum(e, axis=1, keepdims=True)).astype(BF16).astype(F32))
    for copy in value_copies:
        copy.wait()
    squares = jnp.zeros((rows, HEAD_SIZE), F32)
    for g in range(n_kv):
        total = jnp.zeros((block, HEAD_SIZE), F32)
        for t in range(rows):
            mine = jnp.where(owner == t, probs[g], 0.0).astype(BF16)
            total += jnp.dot(
                mine, values[t, :, g * HEAD_SIZE : (g + 1) * HEAD_SIZE],
                preferred_element_type=F32,
            )
        for j in range(per):
            at = slice((g * per + j) * HEAD_SIZE, (g * per + j + 1) * HEAD_SIZE)
            piece = tokens[:, at].astype(F32) + total[j * rows : (j + 1) * rows]
            resid_ref[:, at] = piece
            squares += piece * piece
    mean = jnp.sum(squares, axis=1, keepdims=True) / width
    scale = lax.rsqrt(mean + 1e-05)
    row_ref[:, :width] = (resid_ref[...] * scale * gain[...]).astype(BF16)
    row_at = lax.broadcasted_iota(jnp.int32, (rows, LANES), 0)
    lane = lax.broadcasted_iota(jnp.int32, (rows, LANES), 1)
    high = jnp.zeros((rows, LANES), F32)
    low = jnp.zeros((rows, LANES), F32)
    for t in range(rows):
        for k in range(routes.shape[0]):
            hit = row_at == t
            high += jnp.where(hit & (lane == routes[k, t]), weights[k, t], 0.0)
            low += jnp.where(hit & (lane == routes[k, t] + LANES // 2), weights[k, t], 0.0)
    low = low - low.astype(BF16).astype(F32)
    row_ref[:, width:] = (high.astype(BF16).astype(F32) + low).astype(BF16)


def attend(tokens, queries, keys, values, lengths, gain, routes, weights):
    rows, width = tokens.shape
    smem = pl.BlockSpec(memory_space=pltpu.SMEM)
    vmem = pl.BlockSpec(memory_space=pltpu.VMEM)
    hbm = pl.BlockSpec(memory_space=pl.ANY)
    return pl.pallas_call(
        attend_kernel,
        in_specs=[smem, smem, smem, vmem, vmem, vmem, hbm, hbm],
        out_specs=[vmem, vmem],
        out_shape=[
            jax.ShapeDtypeStruct((rows, width), F32),
            jax.ShapeDtypeStruct((rows, width + LANES), BF16),
        ],
        scratch_shapes=[
            pltpu.VMEM(keys.shape, BF16),
            pltpu.VMEM(values.shape, BF16),
            pltpu.SemaphoreType.DMA((rows,)),
            pltpu.SemaphoreType.DMA((rows,)),
        ],
        name="attend",
    )(lengths, routes.T, weights.T, tokens, queries, gain.reshape(1, width), keys, values)


def expert_kernel(n_pieces, chunk, wide, expert, *refs):
    pieces = refs[:n_pieces]
    gate_up_hbm, down_hbm = refs[n_pieces : n_pieces + 2]
    outs = refs[n_pieces + 2 : 2 * n_pieces + 2]
    x, gate_up, down, hidden, gate_sems, down_sems = refs[2 * n_pieces + 2 :]
    hidden_units, width = down_hbm.shape
    n_chunks = hidden_units // chunk
    n_wide = width // wide
    gate_copies = [
        pltpu.make_async_copy(
            gate_up_hbm.at[:, c * chunk : (c + 1) * chunk],
            gate_up.at[:, c * chunk : (c + 1) * chunk],
            gate_sems.at[c],
        )
        for c in range(n_chunks)
    ]
    down_copies = [
        pltpu.make_async_copy(
            down_hbm.at[c * chunk : (c + 1) * chunk],
            down.at[c * chunk : (c + 1) * chunk],
            down_sems.at[c],
        )
        for c in range(n_chunks)
    ]
    for copy in gate_copies + down_copies:
        copy.start()
    size = pieces[0].shape[0]
    factors = []
    for i in range(n_pieces):
        x[i * size : (i + 1) * size] = pieces[i][:, :width]
        meta = pieces[i][:, width:].astype(F32)
        lane = lax.broadcasted_iota(jnp.int32, meta.shape, 1)
        mine = lane % (LANES // 2) == expert[0]
        factors.append(jnp.sum(jnp.where(mine, meta, 0.0), axis=1, keepdims=True))
    for c in range(n_chunks):
        gate_copies[c].wait()
        at = slice(c * chunk, (c + 1) * chunk)
        both = [
            lax.dot_general(
                gate_up[i, at], x[...], (((1,), (1,)), ((), ())), preferred_element_type=F32
            )
            for i in range(2)
        ]
        hidden[at] = both[0] / (1.0 + jnp.exp(-both[0])) * both[1]
    turned = jnp.transpose(hidden[...]).astype(BF16)
    for copy in down_copies:
        copy.wait()
    for c in range(n_wide):
        at = slice(c * wide, (c + 1) * wide)
        total = jnp.dot(turned, down[:, at], preferred_element_type=F32)
        for i in range(n_pieces):
            part = total[i * size : (i + 1) * size] * factors[i]
            outs[i][:, at] = part.astype(BF16)


def experts(pieces, gate_up, down, expert):
    n_pieces = len(pieces)
    size, width = pieces[0].shape[0], pieces[0].shape[1] - LANES
    hidden_units = down.shape[0]
    chunk = next((c for c in (192, 96, 64, 32, 16) if hidden_units % c == 0), hidden_units)
    vmem = pl.BlockSpec(memory_space=pltpu.VMEM)
    hbm = pl.BlockSpec(memory_space=pl.ANY)
    return pl.pallas_call(
        functools.partial(expert_kernel, n_pieces, chunk, 768),
        in_specs=[pl.BlockSpec(memory_space=pltpu.SMEM)] + [vmem] * n_pieces + [hbm, hbm],
        out_specs=[vmem] * n_pieces,
        out_shape=[jax.ShapeDtypeStruct((size, width), BF16)] * n_pieces,
        scratch_shapes=[
            pltpu.VMEM((n_pieces * size, width), BF16),
            pltpu.VMEM(gate_up.shape, BF16),
            pltpu.VMEM(down.shape, BF16),
            pltpu.VMEM((hidden_units, n_pieces * size), F32),
            pltpu.SemaphoreType.DMA((hidden_units // chunk,)),
            pltpu.SemaphoreType.DMA((hidden_units // chunk,)),
        ],
        compiler_params=pltpu.CompilerParams(vmem_limit_bytes=60 * 2**20),
        name="experts",
    )(expert, *pieces, gate_up, down)


def swap(value, axis, bits):
    n = lax.axis_size(axis)
    return lax.ppermute(value, axis, [(i, i ^ bits) for i in range(n)])


def strides(size):
    steps, stride = [], 1
    while stride < size:
        radix = 4 if size // stride >= 4 else 2
        steps.append((stride, radix))
        stride *= radix
    return steps


def added(*parts):
    total = parts[0].astype(F32)
    for part in parts[1:]:
        total = total + part.astype(F32)
    return total.astype(BF16)


def shards(
    tokens, queries, stored_keys, stored_values, lengths, norm_gain, routes, route_weights,
    gate_up, down_proj,
):
    n_side = lax.axis_size("side")
    rows = tokens.shape[0]
    resid, row = attend(
        tokens, queries, stored_keys, stored_values, lengths, norm_gain, routes, route_weights
    )
    tp_steps = strides(lax.axis_size("tp"))
    held = row
    for stride, radix in tp_steps:
        held = jnp.concatenate(
            [held] + [swap(held, "tp", stride * k) for k in range(1, radix)], axis=0
        )
    pieces = [held]
    side_bits = []
    bit = n_side // 2
    while bit:
        side_bits.append(bit)
        pieces = pieces + [swap(piece, "side", bit) for piece in pieces]
        bit //= 2
    expert = lax.axis_index("side").astype(jnp.int32).reshape(1)
    parts = list(experts(pieces, gate_up[0], down_proj[0], expert))
    for bit in reversed(side_bits):
        half = len(parts) // 2
        parts = [
            added(parts[i], swap(parts[half + i], "side", bit)) for i in range(half)
        ]
    total = parts[0]
    for stride, radix in reversed(tp_steps):
        size = total.shape[0] // radix
        own = total[:size]
        other = [
            swap(total[k * size : (k + 1) * size], "tp", stride * k) for k in range(1, radix)
        ]
        if size == rows:
            mixed = resid + own.astype(F32)
            for part in other:
                mixed = mixed + part.astype(F32)
            return mixed.astype(BF16)
        total = added(own, *other)


def solution(mesh):
    rows = ("groups", "side", "tp")
    placed = (
        P(rows, None),
        P(rows, None),
        P(rows, None, None),
        P(rows, None, None),
        P(rows),
        P(),
        P(rows, None),
        P(rows, None),
        P("side", None, "tp", None),
        P("side", "tp", None),
    )
    return jax.shard_map(
        shards, mesh=mesh, in_specs=placed, out_specs=P(rows, None), check_vma=False
    )
```

time: 115 us -> 65.2 us (0.57)
  matrix products: 50.7 us -> 0 us
  Pallas kernels: 0 us -> 25.6 us
  local copies, waits for them, and re-layouts: 13.7 us -> 0.75 us
  starting transfers between devices: 22.9 us -> 13 us
    dot_general x10 -> x0, matrix products: 50.7 us -> none  [the longest x2 30.1 us: shards(): jnp.einsum('rd,cfd->rcf', arrived, local_gu, preferred_element_type=jnp.f...]
    pallas_call x0 -> x2, Pallas kernels: none -> 25.6 us  [the longest x1 21.3 us: experts(): pl.pallas_call(functools.partial(expert_kernel, n_pieces, chunk, 768), in...]
    all_to_all x4 -> x0, starting transfers between devices: 22.9 us -> none  [the longest x2 11.9 us: shards(): lax.all_to_all(partial_value, ('side', 'tp'), split_axis=0, concat_axis=0...]
    all_to_all x4 -> x0, waiting for transfers between devices: 22.4 us -> none  [the longest x2 11.3 us: shards(): lax.all_to_all(partial_value, ('side', 'tp'), split_axis=0, concat_axis=0...]
    ppermute x0 -> x12, waiting for transfers between devices: none -> 21.8 us  [swap(): return lax.ppermute(value, axis, [(i, i ^ bits) for i in range(n)])]
    ppermute x0 -> x12, starting transfers between devices: none -> 13 us  [swap(): return lax.ppermute(value, axis, [(i, i ^ bits) for i in range(n)])]
    slice x8 -> x1, local copies, waits for them, and re-layouts: 5.35 us -> 0.06 us  [shards(): total[k * size:(k + 1) * size]]
    reduce_sum x7 -> x0, other arithmetic: 2.7 us -> none  [the longest x1 1.09 us: attend_norm(): scale = lax.rsqrt(jnp.mean(resid * resid, axis=-1, keepdims=True) + 1e-05)]
  transfers between devices with their start and end apart: 4 -> 12, of which waited for: 2 -> 9; matrix products, arithmetic and copies ran while one was open for 45% -> 2% of each run, Pallas kernels for 0% -> 0%
where the time goes in v1:
time: 65.2 us; the launch traced here: 64.8 us
  Pallas kernels  25.6 us (39%)
  waiting for transfers between devices  21.8 us (33%)
  starting transfers between devices  13 us (20%)
  other arithmetic  3.6 us (6%)
  local copies, waits for them, and re-layouts  0.75 us (1%)
    ppermute x12, waiting for transfers between devices, swap(): return lax.ppermute(value, axis, [(i, i ^ bits) for i in range(n)])  21.8 us
    pallas_call x1, Pallas kernels, experts(): pl.pallas_call(functools.partial(expert_kernel, n_pieces, chunk, 768), in...  21.3 us
    ppermute x12, starting transfers between devices, swap(): return lax.ppermute(value, axis, [(i, i ^ bits) for i in range(n)])  13 us
    pallas_call x1, Pallas kernels, attend(): pl.pallas_call(attend_kernel, in_specs=[smem, smem, smem, vmem, vmem, vme...  4.3 us
    convert_element_type x2, other arithmetic, added(): return total.astype(BF16)  1.99 us
  transfers between devices with their start and end apart: 12, of which 9 were waited for; matrix products, arithmetic and copies ran while one was open for 2% of the time, Pallas kernels for 0%

profile of v1, /device:TPU:0, one launch (start us, length us, event | category | flops | bytes accessed | tf_op | source)
XLA Modules:
  0.0 64.8 jit_solution(6094691387671199583)
XLA Ops:
  0.0 4.3 %attend.1 = (f32[4,6144]{1,0:T(4,128)}, bf16[4,6272]{1,0:T(4,128)(2,1)}) custom-call(s32[4]{0:T(128)} %lengths.1, s32[2,4]{1,0:T(2,128)} %bitcast.9, f32[2,4]{1,0:T(2,128)} %bitcast.10, bf16[4,6144]{1,0:T(4,128)(2,1)} %tokens.1, bf16[4,6144]{1,0:T(4,128)(2,1)} %queries.1, f32[1,6144]{1,0:T(1,128)} %bitcast.8, bf16[4,128,1024]{2,1,0:T(8,128)(2,1)} %keys_hbm.1, ...), custom_call_target="tpu_custom_call" | custom-call | tf_op jit(solution)/shard_map/attend/pallas_call | solution.py:102
  4.3 5.1 %collective-permute-start.2 = (bf16[4,6272]{1,0:T(4,128)(2,1)}, bf16[4,6272]{1,0:T(4,128)(2,1)S(1)}, u32[]{:S(2)}, u32[]{:S(2)}) collective-permute-start(bf16[4,6272]{1,0:T(4,128)(2,1)} %get-tuple-element.12), channel_id=1, source_target_pairs={{0,3},{1,2},{2,1},{3,0},{4,7},{5,6},{6,5},{7,4},{8,11},{9,10},{10,... | collective-permute-start | bytes 150536 | tf_op jit(solution)/shard_map/ppermute | solution.py:202
  9.4 0.6 collective-permute-start
  10.1 1.8 %collective-permute-done.2 = bf16[4,6272]{1,0:T(4,128)(2,1)S(1)} collective-permute-done((bf16[4,6272]{1,0:T(4,128)(2,1)}, bf16[4,6272]{1,0:T(4,128)(2,1)S(1)}, u32[]{:S(2)}, u32[]{:S(2)}) %collective-permute-start.2) | collective-permute-done | bytes 50208 | tf_op jit(solution)/shard_map/ppermute | solution.py:202
  11.9 2.7 %collective-permute-done.1 = bf16[4,6272]{1,0:T(4,128)(2,1)S(1)} collective-permute-done((bf16[4,6272]{1,0:T(4,128)(2,1)}, bf16[4,6272]{1,0:T(4,128)(2,1)S(1)}, u32[]{:S(2)}, u32[]{:S(2)}) %collective-permute-start.1) | collective-permute-done | bytes 50208 | tf_op jit(solution)/shard_map/ppermute | solution.py:202
  14.7 0.9 %pad_maximum_fusion.refs_0_ = bf16[16,6272]{1,0:T(8,128)(2,1)S(1)} fusion(bf16[4,6272]{1,0:T(4,128)(2,1)S(1)} %collective-permute-done.2, bf16[4,6272]{1,0:T(4,128)(2,1)S(1)} %collective-permute-done.1, bf16[4,6272]{1,0:T(4,128)(2,1)S(1)} %collective-permute-done, bf16[4,6272]{1,0:T(4,128)(2,1)} %get-tuple-element.12), kind=kLoop, calls=%fused_computation.3 | loop fusion | flops 802816 | bytes 401408 | tf_op jit(solution)/shard_map/concatenate | solution.py:233
  15.6 1.6 %collective-permute-start.3 = (bf16[16,6272]{1,0:T(8,128)(2,1)S(1)}, bf16[16,6272]{1,0:T(8,128)(2,1)S(1)}, u32[]{:S(2)}, u32[]{:S(2)}) collective-permute-start(bf16[16,6272]{1,0:T(8,128)(2,1)S(1)} %pad_maximum_fusion.refs_0_), channel_id=1, source_target_pairs={{0,8},{4,12},{8,0},{12,4},{1,9},{5,13},{9,1},{13,5},{2,10},{6,14},... | collective-permute-start | bytes 602120 | tf_op jit(solution)/shard_map/ppermute | solution.py:202
  17.1 4.4 %collective-permute-done.3.refs_1_ = bf16[16,6272]{1,0:T(8,128)(2,1)S(1)} collective-permute-done((bf16[16,6272]{1,0:T(8,128)(2,1)S(1)}, bf16[16,6272]{1,0:T(8,128)(2,1)S(1)}, u32[]{:S(2)}, u32[]{:S(2)}) %collective-permute-start.3) | collective-permute-done | bytes 200736 | tf_op jit(solution)/shard_map/ppermute | solution.py:202
  21.5 1.4 %collective-permute-done.5.refs_3_ = bf16[16,6272]{1,0:T(8,128)(2,1)S(1)} collective-permute-done((bf16[16,6272]{1,0:T(8,128)(2,1)S(1)}, bf16[16,6272]{1,0:T(8,128)(2,1)S(1)}, u32[]{:S(2)}, u32[]{:S(2)}) %collective-permute-start.5) | collective-permute-done | bytes 200736 | tf_op jit(solution)/shard_map/ppermute | solution.py:202
  23.0 0.7 %copy-done.3 = bf16[16,6272]{1,0:T(8,128)(2,1)} copy-done((bf16[16,6272]{1,0:T(8,128)(2,1)}, bf16[16,6272]{1,0:T(8,128)(2,1)S(1)}, u32[]{:S(2)}) %copy-start.3) | copy-done | bytes 200728
  23.6 21.3 %experts.1 = (bf16[16,6144]{1,0:T(8,128)(2,1)}, bf16[16,6144]{1,0:T(8,128)(2,1)}, bf16[16,6144]{1,0:T(8,128)(2,1)}, bf16[16,6144]{1,0:T(8,128)(2,1)}) custom-call(s32[1]{0:T(128)} %bitcast.3.expert, bf16[16,6272]{1,0:T(8,128)(2,1)} %copy-done, bf16[16,6272]{1,0:T(8,128)(2,1)} %copy-done.1, bf16[16,6272]{1,0:T(8,128)(2,1)} %copy-done.2, ...), custom_call_target="tpu_custom_call" | custom-call | tf_op jit(solution)/shard_map/experts/pallas_call | solution.py:182
  45.0 0.2 collective-permute-start.7
  45.2 0.4 collective-permute-start.6
  45.5 1.1 %collective-permute-done.7 = bf16[16,6144]{1,0:T(8,128)(2,1)S(1)} collective-permute-done((bf16[16,6144]{1,0:T(8,128)(2,1)}, bf16[16,6144]{1,0:T(8,128)(2,1)S(1)}, u32[]{:S(2)}, u32[]{:S(2)}) %collective-permute-start.7) | collective-permute-done | bytes 196640 | tf_op jit(solution)/shard_map/ppermute | solution.py:202
  46.7 1.0 %add_convert_fusion.1 = bf16[16,6144]{1,0:T(8,128)(2,1)S(1)} fusion(bf16[16,6144]{1,0:T(8,128)(2,1)S(1)} %collective-permute-done.7, bf16[16,6144]{1,0:T(8,128)(2,1)} %get-tuple-element.15), kind=kLoop, calls=%fused_computation.1 | loop fusion | flops 393216 | bytes 589824 | tf_op jit(solution)/shard_map/convert_element_type | solution.py:218
  47.7 1.6 %collective-permute-start.8 = (bf16[16,6144]{1,0:T(8,128)(2,1)S(1)}, bf16[16,6144]{1,0:T(8,128)(2,1)S(1)}, u32[]{:S(2)}, u32[]{:S(2)}) collective-permute-start(bf16[16,6144]{1,0:T(8,128)(2,1)S(1)} %add_convert_fusion.1), channel_id=1, source_target_pairs={{0,8},{4,12},{8,0},{12,4},{1,9},{5,13},{9,1},{13,5},{2,10},{6,14},... | collective-permute-start | bytes 589832 | tf_op jit(solution)/shard_map/ppermute | solution.py:202
  49.2 5.4 %collective-permute-done.8 = bf16[16,6144]{1,0:T(8,128)(2,1)S(1)} collective-permute-done((bf16[16,6144]{1,0:T(8,128)(2,1)S(1)}, bf16[16,6144]{1,0:T(8,128)(2,1)S(1)}, u32[]{:S(2)}, u32[]{:S(2)}) %collective-permute-start.8) | collective-permute-done | bytes 196640 | tf_op jit(solution)/shard_map/ppermute | solution.py:202
  54.7 1.0 %add_convert_fusion = bf16[16,6144]{1,0:T(8,128)(2,1)S(1)} fusion(bf16[16,6144]{1,0:T(8,128)(2,1)S(1)} %collective-permute-done.8, bf16[16,6144]{1,0:T(8,128)(2,1)S(1)} %collective-permute-done.6, bf16[16,6144]{1,0:T(8,128)(2,1)} %get-tuple-element.13), kind=kLoop, calls=%fused_computation | loop fusion | flops 786432 | bytes 786432 | tf_op jit(solution)/shard_map/convert_element_type | solution.py:218
  55.7 0.8 %collective-permute-start.9 = (bf16[4,6144]{1,0:T(4,128)(2,1)S(1)}, bf16[4,6144]{1,0:T(4,128)(2,1)S(1)}, u32[]{:S(2)}, u32[]{:S(2)}) collective-permute-start(bf16[4,6144]{1,0:T(4,128)(2,1)S(1)} %get-tuple-element.17), channel_id=1, source_target_pairs={{0,1},{1,0},{2,3},{3,2},{4,5},{5,4},{6,7},{7,6},{8,9},{9,8},{10,11... | collective-permute-start | bytes 147464 | tf_op jit(solution)/shard_map/ppermute | solution.py:202
  56.5 2.6 %collective-permute-start.11 = (bf16[4,6144]{1,0:T(4,128)(2,1)S(1)}, bf16[4,6144]{1,0:T(4,128)(2,1)S(1)}, u32[]{:S(2)}, u32[]{:S(2)}) collective-permute-start(bf16[4,6144]{1,0:T(4,128)(2,1)S(1)} %get-tuple-element.18), channel_id=1, source_target_pairs={{0,3},{1,2},{2,1},{3,0},{4,7},{5,6},{6,5},{7,4},{8,11},{9,10},{10,... | collective-permute-start | bytes 147464 | tf_op jit(solution)/shard_map/ppermute | solution.py:202
  59.3 0.6 collective-permute-done.9
  59.9 2.6 %collective-permute-done.11 = bf16[4,6144]{1,0:T(4,128)(2,1)S(1)} collective-permute-done((bf16[4,6144]{1,0:T(4,128)(2,1)S(1)}, bf16[4,6144]{1,0:T(4,128)(2,1)S(1)}, u32[]{:S(2)}, u32[]{:S(2)}) %collective-permute-start.11) | collective-permute-done | bytes 49184 | tf_op jit(solution)/shard_map/ppermute | solution.py:202
  62.5 1.6 %collective-permute-done.10 = bf16[4,6144]{1,0:T(4,128)(2,1)S(1)} collective-permute-done((bf16[4,6144]{1,0:T(4,128)(2,1)S(1)}, bf16[4,6144]{1,0:T(4,128)(2,1)S(1)}, u32[]{:S(2)}, u32[]{:S(2)}) %collective-permute-start.10) | collective-permute-done | bytes 49184 | tf_op jit(solution)/shard_map/ppermute | solution.py:202
  64.2 0.7 %add_convert_fusion.3 = bf16[4,6144]{1,0:T(4,128)(2,1)} fusion(bf16[4,6144]{1,0:T(4,128)(2,1)S(1)} %collective-permute-done.11, bf16[4,6144]{1,0:T(4,128)(2,1)S(1)} %collective-permute-done.10, bf16[4,6144]{1,0:T(4,128)(2,1)S(1)} %collective-permute-done.9, f32[4,6144]{1,0:T(4,128)S(1)} %copy-done.4, bf16[16,6144]{1,0:T(8,128)(2,1)S(1)} %add_convert_fusion), kind=kLoop, calls=%fused_computation.4 | loop fusion | flops 221184 | bytes 344064 | tf_op jit(solution)/shard_map/convert_element_type | solution.py:261
  (17 shorter events, 0.2 us)
Async XLA Ops:
  4.3 59.8 %copy-start.4 = (f32[4,6144]{1,0:T(4,128)S(1)}, f32[4,6144]{1,0:T(4,128)}, u32[]{:S(2)}) copy-start(f32[4,6144]{1,0:T(4,128)} %get-tuple-element.11) | copy-start | bytes 294916
  4.3 7.6 %collective-permute-start.2 = (bf16[4,6272]{1,0:T(4,128)(2,1)}, bf16[4,6272]{1,0:T(4,128)(2,1)S(1)}, u32[]{:S(2)}, u32[]{:S(2)}) collective-permute-start(bf16[4,6272]{1,0:T(4,128)(2,1)} %get-tuple-element.12), channel_id=1, source_target_pairs={{0,3},{1,2},{2,1},{3,0},{4,7},{5,6},{6,5},{7,4},{8,11},{9,10},{10,... | collective-permute-start | bytes 150536 | tf_op jit(solution)/shard_map/ppermute | solution.py:202
  9.4 5.2 %collective-permute-start.1 = (bf16[4,6272]{1,0:T(4,128)(2,1)}, bf16[4,6272]{1,0:T(4,128)(2,1)S(1)}, u32[]{:S(2)}, u32[]{:S(2)}) collective-permute-start(bf16[4,6272]{1,0:T(4,128)(2,1)} %get-tuple-element.12), channel_id=1, source_target_pairs={{0,2},{1,3},{2,0},{3,1},{4,6},{5,7},{6,4},{7,5},{8,10},{9,11},{10,... | collective-permute-start | bytes 150536 | tf_op jit(solution)/shard_map/ppermute | solution.py:202
  9.4 5.2 %collective-permute-start = (bf16[4,6272]{1,0:T(4,128)(2,1)}, bf16[4,6272]{1,0:T(4,128)(2,1)S(1)}, u32[]{:S(2)}, u32[]{:S(2)}) collective-permute-start(bf16[4,6272]{1,0:T(4,128)(2,1)} %get-tuple-element.12), channel_id=1, source_target_pairs={{0,1},{1,0},{2,3},{3,2},{4,5},{5,4},{6,7},{7,6},{8,9},{9,8},{10,11... | collective-permute-start | bytes 150536 | tf_op jit(solution)/shard_map/ppermute | solution.py:202
  15.6 7.4 %copy-start = (bf16[16,6272]{1,0:T(8,128)(2,1)}, bf16[16,6272]{1,0:T(8,128)(2,1)S(1)}, u32[]{:S(2)}) copy-start(bf16[16,6272]{1,0:T(8,128)(2,1)S(1)} %pad_maximum_fusion.refs_0_) | copy-start | bytes 602116
  15.6 5.9 %collective-permute-start.3 = (bf16[16,6272]{1,0:T(8,128)(2,1)S(1)}, bf16[16,6272]{1,0:T(8,128)(2,1)S(1)}, u32[]{:S(2)}, u32[]{:S(2)}) collective-permute-start(bf16[16,6272]{1,0:T(8,128)(2,1)S(1)} %pad_maximum_fusion.refs_0_), channel_id=1, source_target_pairs={{0,8},{4,12},{8,0},{12,4},{1,9},{5,13},{9,1},{13,5},{2,10},{6,14},... | collective-permute-start | bytes 602120 | tf_op jit(solution)/shard_map/ppermute | solution.py:202
  17.1 4.4 %collective-permute-start.4 = (bf16[16,6272]{1,0:T(8,128)(2,1)S(1)}, bf16[16,6272]{1,0:T(8,128)(2,1)S(1)}, u32[]{:S(2)}, u32[]{:S(2)}) collective-permute-start(bf16[16,6272]{1,0:T(8,128)(2,1)S(1)} %pad_maximum_fusion.refs_0_), channel_id=1, source_target_pairs={{0,4},{4,0},{8,12},{12,8},{1,5},{5,1},{9,13},{13,9},{2,6},{6,2},{1... | collective-permute-start | bytes 602120 | tf_op jit(solution)/shard_map/ppermute | solution.py:202
  21.5 1.5 %copy-start.1 = (bf16[16,6272]{1,0:T(8,128)(2,1)}, bf16[16,6272]{1,0:T(8,128)(2,1)S(1)}, u32[]{:S(2)}) copy-start(bf16[16,6272]{1,0:T(8,128)(2,1)S(1)} %collective-permute-done.3.refs_1_) | copy-start | bytes 602116
  21.5 1.4 %collective-permute-start.5 = (bf16[16,6272]{1,0:T(8,128)(2,1)S(1)}, bf16[16,6272]{1,0:T(8,128)(2,1)S(1)}, u32[]{:S(2)}, u32[]{:S(2)}) collective-permute-start(bf16[16,6272]{1,0:T(8,128)(2,1)S(1)} %collective-permute-done.3.refs_1_), channel_id=1, source_target_pairs={{0,4},{4,0},{8,12},{12,8},{1,5},{5,1},{9,13},{13,9},{2,6},{6,2},{1... | collective-permute-start | bytes 602120 | tf_op jit(solution)/shard_map/ppermute | solution.py:202
  21.5 1.4 %copy-start.2 = (bf16[16,6272]{1,0:T(8,128)(2,1)}, bf16[16,6272]{1,0:T(8,128)(2,1)S(1)}, u32[]{:S(2)}) copy-start(bf16[16,6272]{1,0:T(8,128)(2,1)S(1)} %collective-permute-done.4.refs_2_) | copy-start | bytes 602116
  23.0 0.7 %copy-start.3 = (bf16[16,6272]{1,0:T(8,128)(2,1)}, bf16[16,6272]{1,0:T(8,128)(2,1)S(1)}, u32[]{:S(2)}) copy-start(bf16[16,6272]{1,0:T(8,128)(2,1)S(1)} %collective-permute-done.5.refs_3_) | copy-start | bytes 602116
  45.0 1.7 %collective-permute-start.7 = (bf16[16,6144]{1,0:T(8,128)(2,1)}, bf16[16,6144]{1,0:T(8,128)(2,1)S(1)}, u32[]{:S(2)}, u32[]{:S(2)}) collective-permute-start(bf16[16,6144]{1,0:T(8,128)(2,1)} %get-tuple-element.16), channel_id=1, source_target_pairs={{0,4},{4,0},{8,12},{12,8},{1,5},{5,1},{9,13},{13,9},{2,6},{6,2},{1... | collective-permute-start | bytes 589832 | tf_op jit(solution)/shard_map/ppermute | solution.py:202
  45.2 4.1 %collective-permute-start.6 = (bf16[16,6144]{1,0:T(8,128)(2,1)}, bf16[16,6144]{1,0:T(8,128)(2,1)S(1)}, u32[]{:S(2)}, u32[]{:S(2)}) collective-permute-start(bf16[16,6144]{1,0:T(8,128)(2,1)} %get-tuple-element.14), channel_id=1, source_target_pairs={{0,4},{4,0},{8,12},{12,8},{1,5},{5,1},{9,13},{13,9},{2,6},{6,2},{1... | collective-permute-start | bytes 589832 | tf_op jit(solution)/shard_map/ppermute | solution.py:202
  47.7 7.0 %collective-permute-start.8 = (bf16[16,6144]{1,0:T(8,128)(2,1)S(1)}, bf16[16,6144]{1,0:T(8,128)(2,1)S(1)}, u32[]{:S(2)}, u32[]{:S(2)}) collective-permute-start(bf16[16,6144]{1,0:T(8,128)(2,1)S(1)} %add_convert_fusion.1), channel_id=1, source_target_pairs={{0,8},{4,12},{8,0},{12,4},{1,9},{5,13},{9,1},{13,5},{2,10},{6,14},... | collective-permute-start | bytes 589832 | tf_op jit(solution)/shard_map/ppermute | solution.py:202
  55.7 4.2 %collective-permute-start.9 = (bf16[4,6144]{1,0:T(4,128)(2,1)S(1)}, bf16[4,6144]{1,0:T(4,128)(2,1)S(1)}, u32[]{:S(2)}, u32[]{:S(2)}) collective-permute-start(bf16[4,6144]{1,0:T(4,128)(2,1)S(1)} %get-tuple-element.17), channel_id=1, source_target_pairs={{0,1},{1,0},{2,3},{3,2},{4,5},{5,4},{6,7},{7,6},{8,9},{9,8},{10,11... | collective-permute-start | bytes 147464 | tf_op jit(solution)/shard_map/ppermute | solution.py:202
  56.5 6.0 %collective-permute-start.11 = (bf16[4,6144]{1,0:T(4,128)(2,1)S(1)}, bf16[4,6144]{1,0:T(4,128)(2,1)S(1)}, u32[]{:S(2)}, u32[]{:S(2)}) collective-permute-start(bf16[4,6144]{1,0:T(4,128)(2,1)S(1)} %get-tuple-element.18), channel_id=1, source_target_pairs={{0,3},{1,2},{2,1},{3,0},{4,7},{5,6},{6,5},{7,4},{8,11},{9,10},{10,... | collective-permute-start | bytes 147464 | tf_op jit(solution)/shard_map/ppermute | solution.py:202
  59.2 5.0 %collective-permute-start.10 = (bf16[4,6144]{1,0:T(4,128)(2,1)S(1)}, bf16[4,6144]{1,0:T(4,128)(2,1)S(1)}, u32[]{:S(2)}, u32[]{:S(2)}) collective-permute-start(bf16[4,6144]{1,0:T(4,128)(2,1)S(1)} %get-tuple-element.19), channel_id=1, source_target_pairs={{0,2},{1,3},{2,0},{3,1},{4,6},{5,7},{6,4},{7,5},{8,10},{9,11},{10,... | collective-permute-start | bytes 147464 | tf_op jit(solution)/shard_map/ppermute | solution.py:202

commit v2 on v1

--- a/solution.py
+++ b/solution.py
@@ -15,8 +15,8 @@
 
 
 def attend_kernel(
-    lengths, routes, weights, tokens, queries, gain, keys_hbm, values_hbm,
-    resid_ref, row_ref, keys, values, key_sems, value_sems,
+    lengths, routes, weights, tokens, queries, gain, keys_hbm, values_hbm, ahead_hbm,
+    resid_ref, row_ref, ahead, keys, values, key_sems, value_sems, ahead_sems,
 ):
     rows, positions, kv_width = keys_hbm.shape
     width = tokens.shape[1]
@@ -29,7 +29,8 @@
         pltpu.make_async_copy(values_hbm.at[t], values.at[t], value_sems.at[t])
         for t in range(rows)
     ]
-    for copy in key_copies + value_copies:
+    ahead_copies = ahead_parts(ahead_hbm, ahead, ahead_sems, 0)
+    for copy in key_copies + value_copies + ahead_copies:
         copy.start()
     block = per * rows
     owner = lax.broadcasted_iota(jnp.int32, (block, 1), 0) % rows
@@ -92,56 +93,100 @@
             low += jnp.where(hit & (lane == routes[k, t] + LANES // 2), weights[k, t], 0.0)
     low = low - low.astype(BF16).astype(F32)
     row_ref[:, width:] = (high.astype(BF16).astype(F32) + low).astype(BF16)
-
-
-def attend(tokens, queries, keys, values, lengths, gain, routes, weights):
+    for copy in ahead_copies:
+        copy.wait()
+
+
+def thirds(hidden_units):
+    return 3 if hidden_units % 48 == 0 else 1
+
+
+def ahead_parts(source, target, sems, part):
+    size = target.shape[1]
+    return [
+        pltpu.make_async_copy(
+            source.at[i, part * size : (part + 1) * size], target.at[i], sems.at[i]
+        )
+        for i in range(2)
+    ]
+
+
+def ahead_shape(gate_up):
+    two, hidden_units, width = gate_up.shape
+    return pltpu.VMEM((two, hidden_units // thirds(hidden_units), width), gate_up.dtype)
+
+
+def ahead_kernel(part, source, target, sems):
+    copies = ahead_parts(source, target, sems, part)
+    for copy in copies:
+        copy.start()
+    for copy in copies:
+        copy.wait()
+
+
+def bring(gate_up, part):
+    shape = ahead_shape(gate_up)
+    return pl.pallas_call(
+        functools.partial(ahead_kernel, part),
+        in_specs=[pl.BlockSpec(memory_space=pltpu.HBM)],
+        out_specs=pl.BlockSpec(memory_space=pltpu.VMEM),
+        out_shape=shape,
+        scratch_shapes=[pltpu.SemaphoreType.DMA((2,))],
+        cost_estimate=pl.CostEstimate(
+            flops=0, transcendentals=0, bytes_accessed=2 * math.prod(shape.shape)
+        ),
+        compiler_params=pltpu.CompilerParams(vmem_limit_bytes=2**20),
+        name="bring",
+    )(in_hbm(gate_up))
+
+
+def attend(tokens, queries, keys, values, lengths, gain, routes, weights, gate_up):
     rows, width = tokens.shape
     smem = pl.BlockSpec(memory_space=pltpu.SMEM)
     vmem = pl.BlockSpec(memory_space=pltpu.VMEM)
-    hbm = pl.BlockSpec(memory_space=pl.ANY)
+    hbm = pl.BlockSpec(memory_space=pltpu.HBM)
     return pl.pallas_call(
         attend_kernel,
-        in_specs=[smem, smem, smem, vmem, vmem, vmem, hbm, hbm],
-        out_specs=[vmem, vmem],
+        in_specs=[smem, smem, smem, vmem, vmem, vmem, hbm, hbm, hbm],
+        out_specs=[vmem, vmem, vmem],
         out_shape=[
-            jax.ShapeDtypeStruct((rows, width), F32),
-            jax.ShapeDtypeStruct((rows, width + LANES), BF16),
+            pltpu.VMEM((rows, width), F32),
+            pltpu.VMEM((rows, width + LANES), BF16),
+            ahead_shape(gate_up),
         ],
         scratch_shapes=[
             pltpu.VMEM(keys.shape, BF16),
             pltpu.VMEM(values.shape, BF16),
             pltpu.SemaphoreType.DMA((rows,)),
             pltpu.SemaphoreType.DMA((rows,)),
+            pltpu.SemaphoreType.DMA((2,)),
         ],
+        compiler_params=pltpu.CompilerParams(vmem_limit_bytes=12 * 2**20),
         name="attend",
-    )(lengths, routes.T, weights.T, tokens, queries, gain.reshape(1, width), keys, values)
-
-
-def expert_kernel(n_pieces, chunk, wide, expert, *refs):
+    )(
+        lengths, routes.T, weights.T, tokens, queries, gain.reshape(1, width),
+        in_hbm(keys), in_hbm(values), in_hbm(gate_up),
+    )
+
+
+def expert_kernel(n_pieces, n_parts, chunk, wide, *refs):
+    expert = lax.axis_index("side").astype(jnp.int32)
     pieces = refs[:n_pieces]
-    gate_up_hbm, down_hbm = refs[n_pieces : n_pieces + 2]
-    outs = refs[n_pieces + 2 : 2 * n_pieces + 2]
-    x, gate_up, down, hidden, gate_sems, down_sems = refs[2 * n_pieces + 2 :]
+    parts = refs[n_pieces : n_pieces + n_parts]
+    down_hbm = refs[n_pieces + n_parts]
+    outs = refs[n_pieces + n_parts + 1 : 2 * n_pieces + n_parts + 1]
+    x, down, hidden, down_sems = refs[2 * n_pieces + n_parts + 1 :]
     hidden_units, width = down_hbm.shape
-    n_chunks = hidden_units // chunk
-    n_wide = width // wide
-    gate_copies = [
-        pltpu.make_async_copy(
-            gate_up_hbm.at[:, c * chunk : (c + 1) * chunk],
-            gate_up.at[:, c * chunk : (c + 1) * chunk],
-            gate_sems.at[c],
-        )
-        for c in range(n_chunks)
-    ]
+    part_units = hidden_units // n_parts
     down_copies = [
         pltpu.make_async_copy(
-            down_hbm.at[c * chunk : (c + 1) * chunk],
-            down.at[c * chunk : (c + 1) * chunk],
+            down_hbm.at[c * part_units : (c + 1) * part_units],
+            down.at[c * part_units : (c + 1) * part_units],
             down_sems.at[c],
         )
-        for c in range(n_chunks)
+        for c in range(n_parts)
     ]
-    for copy in gate_copies + down_copies:
+    for copy in down_copies:
         copy.start()
     size = pieces[0].shape[0]
     factors = []
@@ -149,22 +194,23 @@
         x[i * size : (i + 1) * size] = pieces[i][:, :width]
         meta = pieces[i][:, width:].astype(F32)
         lane = lax.broadcasted_iota(jnp.int32, meta.shape, 1)
-        mine = lane % (LANES // 2) == expert[0]
+        mine = lane % (LANES // 2) == expert
         factors.append(jnp.sum(jnp.where(mine, meta, 0.0), axis=1, keepdims=True))
-    for c in range(n_chunks):
-        gate_copies[c].wait()
-        at = slice(c * chunk, (c + 1) * chunk)
-        both = [
-            lax.dot_general(
-                gate_up[i, at], x[...], (((1,), (1,)), ((), ())), preferred_element_type=F32
-            )
-            for i in range(2)
-        ]
-        hidden[at] = both[0] / (1.0 + jnp.exp(-both[0])) * both[1]
+    for p in range(n_parts):
+        for c in range(part_units // chunk):
+            both = [
+                lax.dot_general(
+                    parts[p][i, c * chunk : (c + 1) * chunk], x[...],
+                    (((1,), (1,)), ((), ())), preferred_element_type=F32,
+                )
+                for i in range(2)
+            ]
+            first = p * part_units + c * chunk
+            hidden[first : first + chunk] = both[0] / (1.0 + jnp.exp(-both[0])) * both[1]
     turned = jnp.transpose(hidden[...]).astype(BF16)
     for copy in down_copies:
         copy.wait()
-    for c in range(n_wide):
+    for c in range(width // wide):
         at = slice(c * wide, (c + 1) * wide)
         total = jnp.dot(turned, down[:, at], preferred_element_type=F32)
         for i in range(n_pieces):
@@ -172,29 +218,54 @@
             outs[i][:, at] = part.astype(BF16)
 
 
-def experts(pieces, gate_up, down, expert):
-    n_pieces = len(pieces)
+def in_vmem(value):
+    return pltpu.with_memory_space_constraint(value, pltpu.VMEM)
+
+
+def in_hbm(value):
+    return pltpu.with_memory_space_constraint(value, pltpu.HBM)
+
+
+def join_kernel(*refs):
+    out = refs[-1]
+    out[...] = jnp.concatenate([ref[...].astype(F32) for ref in refs[:-1]], axis=0).astype(BF16)
+
+
+def join(pieces):
+    size, width = pieces[0].shape
+    vmem = pl.BlockSpec(memory_space=pltpu.VMEM)
+    return pl.pallas_call(
+        join_kernel,
+        in_specs=[vmem] * len(pieces),
+        out_specs=vmem,
+        out_shape=pltpu.VMEM((len(pieces) * size, width), BF16),
+        compiler_params=pltpu.CompilerParams(vmem_limit_bytes=2 * 2**20),
+        name="join",
+    )(*map(in_vmem, pieces))
+
+
+def experts(pieces, parts, down):
+    n_pieces, n_parts = len(pieces), len(parts)
     size, width = pieces[0].shape[0], pieces[0].shape[1] - LANES
     hidden_units = down.shape[0]
-    chunk = next((c for c in (192, 96, 64, 32, 16) if hidden_units % c == 0), hidden_units)
+    part_units = hidden_units // n_parts
+    chunk = part_units // 2 if part_units % 32 == 0 else part_units
     vmem = pl.BlockSpec(memory_space=pltpu.VMEM)
-    hbm = pl.BlockSpec(memory_space=pl.ANY)
     return pl.pallas_call(
-        functools.partial(expert_kernel, n_pieces, chunk, 768),
-        in_specs=[pl.BlockSpec(memory_space=pltpu.SMEM)] + [vmem] * n_pieces + [hbm, hbm],
+        functools.partial(expert_kernel, n_pieces, n_parts, chunk, 768),
+        in_specs=[vmem] * (n_pieces + n_parts)
+        + [pl.BlockSpec(memory_space=pltpu.HBM)],
         out_specs=[vmem] * n_pieces,
-        out_shape=[jax.ShapeDtypeStruct((size, width), BF16)] * n_pieces,
+        out_shape=[pltpu.VMEM((size, width), BF16)] * n_pieces,
         scratch_shapes=[
             pltpu.VMEM((n_pieces * size, width), BF16),
-            pltpu.VMEM(gate_up.shape, BF16),
             pltpu.VMEM(down.shape, BF16),
             pltpu.VMEM((hidden_units, n_pieces * size), F32),
-            pltpu.SemaphoreType.DMA((hidden_units // chunk,)),
-            pltpu.SemaphoreType.DMA((hidden_units // chunk,)),
+            pltpu.SemaphoreType.DMA((n_parts,)),
         ],
-        compiler_params=pltpu.CompilerParams(vmem_limit_bytes=60 * 2**20),
+        compiler_params=pltpu.CompilerParams(vmem_limit_bytes=19 * 2**20),
         name="experts",
-    )(expert, *pieces, gate_up, down)
+    )(*map(in_vmem, pieces), *map(in_vmem, parts), in_hbm(down))
 
 
 def swap(value, axis, bits):
@@ -224,24 +295,36 @@
 ):
     n_side = lax.axis_size("side")
     rows = tokens.shape[0]
-    resid, row = attend(
-        tokens, queries, stored_keys, stored_values, lengths, norm_gain, routes, route_weights
+    resid, row, first_part = attend(
+        tokens, queries, stored_keys, stored_values, lengths, norm_gain, routes, route_weights,
+        gate_up[0],
     )
+    weight_parts = [first_part]
+    waiting = list(range(1, thirds(gate_up.shape[2])))
+
+    def beside(values):
+        if not waiting:
+            return values
+        brought = bring(gate_up[0], waiting.pop(0))
+        brought, *values = lax.optimization_barrier((brought, *values))
+        weight_parts.append(brought)
+        return values
+
     tp_steps = strides(lax.axis_size("tp"))
     held = row
     for stride, radix in tp_steps:
-        held = jnp.concatenate(
-            [held] + [swap(held, "tp", stride * k) for k in range(1, radix)], axis=0
-        )
+        others = beside([swap(held, "tp", stride * k) for k in range(1, radix)])
+        held = join([held] + others)
     pieces = [held]
     side_bits = []
     bit = n_side // 2
     while bit:
         side_bits.append(bit)
-        pieces = pieces + [swap(piece, "side", bit) for piece in pieces]
+        pieces = pieces + beside([swap(piece, "side", bit) for piece in pieces])
         bit //= 2
-    expert = lax.axis_index("side").astype(jnp.int32).reshape(1)
-    parts = list(experts(pieces, gate_up[0], down_proj[0], expert))
+    while waiting:
+        weight_parts.append(bring(gate_up[0], waiting.pop(0)))
+    parts = list(experts(pieces, weight_parts, down_proj[0]))
     for bit in reversed(side_bits):
         half = len(parts) // 2
         parts = [

time: 65.2 us -> 63.7 us (0.977)
  waiting for transfers between devices: 21.8 us -> 12.5 us
  Pallas kernels: 25.6 us -> 31.5 us
  local copies, waits for them, and re-layouts: 0.75 us -> 4.41 us
  other arithmetic: 3.6 us -> 0.81 us
  starting transfers between devices: 13 us -> 14.1 us
    ppermute x12, waiting for transfers between devices: 21.8 us -> 12.5 us  [swap(): return lax.ppermute(value, axis, [(i, i ^ bits) for i in range(n)])]
    pallas_call x1 -> x4, Pallas kernels: 21.3 us -> 26 us  [the longest x1 17.4 us: experts(): pl.pallas_call(functools.partial(expert_kernel, n_pieces, n_parts, chunk,...]
    unnamed x10 -> x12, local copies, waits for them, and re-layouts: 0.69 us -> 4.34 us
    convert_element_type x2, other arithmetic: 1.99 us -> 0.12 us  [added(): return total.astype(BF16)]
    pallas_call x1, Pallas kernels: 4.3 us -> 5.45 us  [attend(): pl.pallas_call(attend_kernel, in_specs=[smem, smem, smem, vmem, vmem, vme...]
    ppermute x12, starting transfers between devices: 13 us -> 14.1 us  [swap(): return lax.ppermute(value, axis, [(i, i ^ bits) for i in range(n)])]
    concatenate x1 -> x0, other arithmetic: 0.92 us -> none  [shards(): jnp.concatenate([held] + [swap(held, 'tp', stride * k) for k in range(1,...]
  transfers between devices with their start and end apart: 12 -> 12, of which waited for: 9 -> 7; matrix products, arithmetic and copies ran while one was open for 2% -> 0% of each run, Pallas kernels for 0% -> 14%
where the time goes in v2:
time: 63.7 us; the launch traced here: 63.4 us
  Pallas kernels  31.5 us (49%)
  starting transfers between devices  14.1 us (22%)
  waiting for transfers between devices  12.5 us (20%)
  local copies, waits for them, and re-layouts  4.41 us (7%)
  other arithmetic  0.81 us (1%)
    pallas_call x1, Pallas kernels, experts(): pl.pallas_call(functools.partial(expert_kernel, n_pieces, n_parts, chunk,...  17.4 us
    ppermute x12, starting transfers between devices, swap(): return lax.ppermute(value, axis, [(i, i ^ bits) for i in range(n)])  14.1 us
    ppermute x12, waiting for transfers between devices, swap(): return lax.ppermute(value, axis, [(i, i ^ bits) for i in range(n)])  12.5 us
    pallas_call x2, Pallas kernels, bring(): pl.pallas_call(functools.partial(ahead_kernel, part), in_specs=[pl.BlockS...  8.6 us
    pallas_call x1, Pallas kernels, attend(): pl.pallas_call(attend_kernel, in_specs=[smem, smem, smem, vmem, vmem, vme...  5.45 us
    unnamed x12, local copies, waits for them, and re-layouts  4.34 us
  transfers between devices with their start and end apart: 12, of which 7 were waited for; matrix products, arithmetic and copies ran while one was open for 0% of the time, Pallas kernels for 14%

profile of v2, /device:TPU:0, one launch (start us, length us, event | category | flops | bytes accessed | tf_op | source)
XLA Modules:
  0.0 63.4 jit_solution(8754389644461496181)
XLA Ops:
  0.0 0.8 %copy-done = bf16[4,6144]{1,0:T(4,128)(2,1)S(1)} copy-done((bf16[4,6144]{1,0:T(4,128)(2,1)S(1)}, bf16[4,6144]{1,0:T(4,128)(2,1)}, u32[]{:S(2)}) %copy-start) | copy-done | bytes 49176
  0.8 0.8 %copy-done.1 = bf16[4,6144]{1,0:T(4,128)(2,1)S(1)} copy-done((bf16[4,6144]{1,0:T(4,128)(2,1)S(1)}, bf16[4,6144]{1,0:T(4,128)(2,1)}, u32[]{:S(2)}) %copy-start.1) | copy-done | bytes 49176
  1.6 0.7 %copy-done.2 = f32[6144]{0:T(1024)S(1)} copy-done((f32[6144]{0:T(1024)S(1)}, f32[6144]{0:T(1024)}, u32[]{:S(2)}) %copy-start.2) | copy-done | bytes 24600
  2.3 0.7 %copy-done.3 = s32[4,2]{0,1:T(2,128)S(1)} copy-done((s32[4,2]{0,1:T(2,128)S(1)}, s32[4,2]{0,1:T(2,128)}, u32[]{:S(2)}) %copy-start.3) | copy-done | bytes 56
  3.0 0.7 %copy-done.4 = f32[4,2]{0,1:T(2,128)S(1)} copy-done((f32[4,2]{0,1:T(2,128)S(1)}, f32[4,2]{0,1:T(2,128)}, u32[]{:S(2)}) %copy-start.4) | copy-done | bytes 56
  3.7 0.7 %copy-done.5 = s32[4]{0:T(128)S(1)} copy-done((s32[4]{0:T(128)S(1)}, s32[4]{0:T(128)}, u32[]{:S(2)}) %copy-start.5) | copy-done | bytes 40
  4.4 5.4 %attend.1 = (f32[4,6144]{1,0:T(4,128)S(1)}, bf16[4,6272]{1,0:T(4,128)(2,1)S(1)}, bf16[2,448,6144]{2,1,0:T(8,128)(2,1)S(1)}) custom-call(s32[4]{0:T(128)S(1)} %copy-done.5, s32[2,4]{1,0:T(2,128)S(1)} %bitcast.6, f32[2,4]{1,0:T(2,128)S(1)} %bitcast.7, bf16[4,6144]{1,0:T(4,128)(2,1)S(1)} %copy-done, bf16[4,6144]{1,0:T(4,128)(2,1)S(1)} %copy-done.1, ...), custom_call_target="tpu_custom_call" | custom-call | tf_op jit(solution)/shard_map/attend/pallas_call | solution.py:148
  9.8 5.1 %collective-permute-start.2 = (bf16[4,6272]{1,0:T(4,128)(2,1)S(1)}, bf16[4,6272]{1,0:T(4,128)(2,1)S(1)}, u32[]{:S(2)}, u32[]{:S(2)}) collective-permute-start(bf16[4,6272]{1,0:T(4,128)(2,1)S(1)} %get-tuple-element.19.refs_0_), channel_id=1, source_target_pairs={{0,3},{1,2},{2,1},{3,0},{4,7},{5,6},{6,5},{7,4},{8,11},{9,10},{10,... | collective-permute-start | bytes 150536 | tf_op jit(solution)/shard_map/ppermute | solution.py:273
  14.9 0.6 %collective-permute-start = (bf16[4,6272]{1,0:T(4,128)(2,1)S(1)}, bf16[4,6272]{1,0:T(4,128)(2,1)S(1)}, u32[]{:S(2)}, u32[]{:S(2)}) collective-permute-start(bf16[4,6272]{1,0:T(4,128)(2,1)S(1)} %get-tuple-element.19.refs_0_), channel_id=1, source_target_pairs={{0,1},{1,0},{2,3},{3,2},{4,5},{5,4},{6,7},{7,6},{8,9},{9,8},{10,11... | collective-permute-start | bytes 150536 | tf_op jit(solution)/shard_map/ppermute | solution.py:273
  15.6 4.4 %bring.2.refs_5_ = bf16[2,448,6144]{2,1,0:T(8,128)(2,1)S(1)} custom-call(bf16[2,1344,6144]{2,1,0:T(8,128)(2,1)} %bitcast.9), custom_call_target="tpu_custom_call" | custom-call | bytes 11010048 | tf_op jit(solution)/shard_map/bring/pallas_call | solution.py:129
  20.1 1.7 %collective-permute-start.3 = (bf16[16,6272]{1,0:T(8,128)(2,1)S(1)}, bf16[16,6272]{1,0:T(8,128)(2,1)S(1)}, u32[]{:S(2)}, u32[]{:S(2)}) collective-permute-start(bf16[16,6272]{1,0:T(8,128)(2,1)S(1)} %join.1.refs_0_), channel_id=1, source_target_pairs={{0,8},{4,12},{8,0},{12,4},{1,9},{5,13},{9,1},{13,5},{2,10},{6,14},... | collective-permute-start | bytes 602120 | tf_op jit(solution)/shard_map/ppermute | solution.py:273
  21.8 4.2 %bring.3.refs_6_ = bf16[2,448,6144]{2,1,0:T(8,128)(2,1)S(1)} custom-call(bf16[2,1344,6144]{2,1,0:T(8,128)(2,1)} %bitcast.10), custom_call_target="tpu_custom_call" | custom-call | bytes 11010048 | tf_op jit(solution)/shard_map/bring/pallas_call | solution.py:129
  26.6 0.9 %collective-permute-done.4.refs_2_ = bf16[16,6272]{1,0:T(8,128)(2,1)S(1)} collective-permute-done((bf16[16,6272]{1,0:T(8,128)(2,1)S(1)}, bf16[16,6272]{1,0:T(8,128)(2,1)S(1)}, u32[]{:S(2)}, u32[]{:S(2)}) %collective-permute-start.4) | collective-permute-done | bytes 200736 | tf_op jit(solution)/shard_map/ppermute | solution.py:273
  27.8 17.4 %experts.1 = (bf16[16,6144]{1,0:T(8,128)(2,1)S(1)}, bf16[16,6144]{1,0:T(8,128)(2,1)S(1)}, bf16[16,6144]{1,0:T(8,128)(2,1)S(1)}, bf16[16,6144]{1,0:T(8,128)(2,1)S(1)}) custom-call(bf16[16,6272]{1,0:T(8,128)(2,1)S(1)} %join.1.refs_0_, bf16[16,6272]{1,0:T(8,128)(2,1)S(1)} %collective-permute-done.3.refs_1_, ...), custom_call_target="tpu_custom_call" | custom-call | tf_op jit(solution)/shard_map/experts/pallas_call | solution.py:254
  45.2 0.3 collective-permute-start.7
  45.7 0.9 %collective-permute-done.7 = bf16[16,6144]{1,0:T(8,128)(2,1)S(1)} collective-permute-done((bf16[16,6144]{1,0:T(8,128)(2,1)S(1)}, bf16[16,6144]{1,0:T(8,128)(2,1)S(1)}, u32[]{:S(2)}, u32[]{:S(2)}) %collective-permute-start.7) | collective-permute-done | bytes 196640 | tf_op jit(solution)/shard_map/ppermute | solution.py:273
  46.7 1.5 %collective-permute-start.8 = (bf16[16,6144]{1,0:T(8,128)(2,1)S(1)}, bf16[16,6144]{1,0:T(8,128)(2,1)S(1)}, u32[]{:S(2)}, u32[]{:S(2)}) collective-permute-start(bf16[16,6144]{1,0:T(8,128)(2,1)S(1)} %add_convert_fusion.1), channel_id=1, source_target_pairs={{0,8},{4,12},{8,0},{12,4},{1,9},{5,13},{9,1},{13,5},{2,10},{6,14},... | collective-permute-start | bytes 589832 | tf_op jit(solution)/shard_map/ppermute | solution.py:273
  48.2 5.6 %collective-permute-done.8 = bf16[16,6144]{1,0:T(8,128)(2,1)S(1)} collective-permute-done((bf16[16,6144]{1,0:T(8,128)(2,1)S(1)}, bf16[16,6144]{1,0:T(8,128)(2,1)S(1)}, u32[]{:S(2)}, u32[]{:S(2)}) %collective-permute-start.8) | collective-permute-done | bytes 196640 | tf_op jit(solution)/shard_map/ppermute | solution.py:273
  54.0 1.3 %collective-permute-start.9 = (bf16[4,6144]{1,0:T(4,128)(2,1)S(1)}, bf16[4,6144]{1,0:T(4,128)(2,1)S(1)}, u32[]{:S(2)}, u32[]{:S(2)}) collective-permute-start(bf16[4,6144]{1,0:T(4,128)(2,1)S(1)} %get-tuple-element.31), channel_id=1, source_target_pairs={{0,1},{1,0},{2,3},{3,2},{4,5},{5,4},{6,7},{7,6},{8,9},{9,8},{10,11... | collective-permute-start | bytes 147464 | tf_op jit(solution)/shard_map/ppermute | solution.py:273
  55.3 2.4 %collective-permute-start.11 = (bf16[4,6144]{1,0:T(4,128)(2,1)S(1)}, bf16[4,6144]{1,0:T(4,128)(2,1)S(1)}, u32[]{:S(2)}, u32[]{:S(2)}) collective-permute-start(bf16[4,6144]{1,0:T(4,128)(2,1)S(1)} %get-tuple-element.32), channel_id=1, source_target_pairs={{0,3},{1,2},{2,1},{3,0},{4,7},{5,6},{6,5},{7,4},{8,11},{9,10},{10,... | collective-permute-start | bytes 147464 | tf_op jit(solution)/shard_map/ppermute | solution.py:273
  57.7 0.5 collective-permute-start.10
  58.2 3.5 %collective-permute-done.11 = bf16[4,6144]{1,0:T(4,128)(2,1)S(1)} collective-permute-done((bf16[4,6144]{1,0:T(4,128)(2,1)S(1)}, bf16[4,6144]{1,0:T(4,128)(2,1)S(1)}, u32[]{:S(2)}, u32[]{:S(2)}) %collective-permute-start.11) | collective-permute-done | bytes 49184 | tf_op jit(solution)/shard_map/ppermute | solution.py:273
  61.7 1.0 %collective-permute-done.10 = bf16[4,6144]{1,0:T(4,128)(2,1)S(1)} collective-permute-done((bf16[4,6144]{1,0:T(4,128)(2,1)S(1)}, bf16[4,6144]{1,0:T(4,128)(2,1)S(1)}, u32[]{:S(2)}, u32[]{:S(2)}) %collective-permute-start.10) | collective-permute-done | bytes 49184 | tf_op jit(solution)/shard_map/ppermute | solution.py:273
  62.7 0.7 %add_convert_fusion.3 = bf16[4,6144]{1,0:T(4,128)(2,1)} fusion(bf16[4,6144]{1,0:T(4,128)(2,1)S(1)} %collective-permute-done.11, bf16[4,6144]{1,0:T(4,128)(2,1)S(1)} %collective-permute-done.10, bf16[4,6144]{1,0:T(4,128)(2,1)S(1)} %collective-permute-done.9, f32[4,6144]{1,0:T(4,128)S(1)} %get-tuple-element.18, bf16[16,6144]{1,0:T(8,128)(2,1)S(1)} %add_convert_fusion), kind=kLoop, calls=%fused_computation.3 | loop fusion | flops 221184 | bytes 344064 | tf_op jit(solution)/shard_map/convert_element_type | solution.py:344
  (21 shorter events, 1.4 us)
Async XLA Ops:
  0.0 0.8 %copy-start = (bf16[4,6144]{1,0:T(4,128)(2,1)S(1)}, bf16[4,6144]{1,0:T(4,128)(2,1)}, u32[]{:S(2)}) copy-start(bf16[4,6144]{1,0:T(4,128)(2,1)} %tokens.1) | copy-start | bytes 147460
  0.8 0.8 %copy-start.1 = (bf16[4,6144]{1,0:T(4,128)(2,1)S(1)}, bf16[4,6144]{1,0:T(4,128)(2,1)}, u32[]{:S(2)}) copy-start(bf16[4,6144]{1,0:T(4,128)(2,1)} %queries.1) | copy-start | bytes 147460
  1.6 0.7 %copy-start.2 = (f32[6144]{0:T(1024)S(1)}, f32[6144]{0:T(1024)}, u32[]{:S(2)}) copy-start(f32[6144]{0:T(1024)} %param.15) | copy-start | bytes 73732
  2.3 0.7 %copy-start.3 = (s32[4,2]{0,1:T(2,128)S(1)}, s32[4,2]{0,1:T(2,128)}, u32[]{:S(2)}) copy-start(s32[4,2]{0,1:T(2,128)} %param.16) | copy-start | bytes 100
  3.0 0.7 %copy-start.4 = (f32[4,2]{0,1:T(2,128)S(1)}, f32[4,2]{0,1:T(2,128)}, u32[]{:S(2)}) copy-start(f32[4,2]{0,1:T(2,128)} %param.17) | copy-start | bytes 100
  3.7 0.7 %copy-start.5 = (s32[4]{0:T(128)S(1)}, s32[4]{0:T(128)}, u32[]{:S(2)}) copy-start(s32[4]{0:T(128)} %lengths.1) | copy-start | bytes 52
  9.8 10.2 %collective-permute-start.2 = (bf16[4,6272]{1,0:T(4,128)(2,1)S(1)}, bf16[4,6272]{1,0:T(4,128)(2,1)S(1)}, u32[]{:S(2)}, u32[]{:S(2)}) collective-permute-start(bf16[4,6272]{1,0:T(4,128)(2,1)S(1)} %get-tuple-element.19.refs_0_), channel_id=1, source_target_pairs={{0,3},{1,2},{2,1},{3,0},{4,7},{5,6},{6,5},{7,4},{8,11},{9,10},{10,... | collective-permute-start | bytes 150536 | tf_op jit(solution)/shard_map/ppermute | solution.py:273
  14.9 5.1 %collective-permute-start.1 = (bf16[4,6272]{1,0:T(4,128)(2,1)S(1)}, bf16[4,6272]{1,0:T(4,128)(2,1)S(1)}, u32[]{:S(2)}, u32[]{:S(2)}) collective-permute-start(bf16[4,6272]{1,0:T(4,128)(2,1)S(1)} %get-tuple-element.19.refs_0_), channel_id=1, source_target_pairs={{0,2},{1,3},{2,0},{3,1},{4,6},{5,7},{6,4},{7,5},{8,10},{9,11},{10,... | collective-permute-start | bytes 150536 | tf_op jit(solution)/shard_map/ppermute | solution.py:273
  14.9 5.1 %collective-permute-start = (bf16[4,6272]{1,0:T(4,128)(2,1)S(1)}, bf16[4,6272]{1,0:T(4,128)(2,1)S(1)}, u32[]{:S(2)}, u32[]{:S(2)}) collective-permute-start(bf16[4,6272]{1,0:T(4,128)(2,1)S(1)} %get-tuple-element.19.refs_0_), channel_id=1, source_target_pairs={{0,1},{1,0},{2,3},{3,2},{4,5},{5,4},{6,7},{7,6},{8,9},{9,8},{10,11... | collective-permute-start | bytes 150536 | tf_op jit(solution)/shard_map/ppermute | solution.py:273
  20.1 6.2 %collective-permute-start.3 = (bf16[16,6272]{1,0:T(8,128)(2,1)S(1)}, bf16[16,6272]{1,0:T(8,128)(2,1)S(1)}, u32[]{:S(2)}, u32[]{:S(2)}) collective-permute-start(bf16[16,6272]{1,0:T(8,128)(2,1)S(1)} %join.1.refs_0_), channel_id=1, source_target_pairs={{0,8},{4,12},{8,0},{12,4},{1,9},{5,13},{9,1},{13,5},{2,10},{6,14},... | collective-permute-start | bytes 602120 | tf_op jit(solution)/shard_map/ppermute | solution.py:273
  26.0 1.5 %collective-permute-start.4 = (bf16[16,6272]{1,0:T(8,128)(2,1)S(1)}, bf16[16,6272]{1,0:T(8,128)(2,1)S(1)}, u32[]{:S(2)}, u32[]{:S(2)}) collective-permute-start(bf16[16,6272]{1,0:T(8,128)(2,1)S(1)} %join.1.refs_0_), channel_id=1, source_target_pairs={{0,4},{4,0},{8,12},{12,8},{1,5},{5,1},{9,13},{13,9},{2,6},{6,2},{1... | collective-permute-start | bytes 602120 | tf_op jit(solution)/shard_map/ppermute | solution.py:273
  26.3 1.5 %collective-permute-start.5 = (bf16[16,6272]{1,0:T(8,128)(2,1)S(1)}, bf16[16,6272]{1,0:T(8,128)(2,1)S(1)}, u32[]{:S(2)}, u32[]{:S(2)}) collective-permute-start(bf16[16,6272]{1,0:T(8,128)(2,1)S(1)} %collective-permute-done.3.refs_1_), channel_id=1, source_target_pairs={{0,4},{4,0},{8,12},{12,8},{1,5},{5,1},{9,13},{13,9},{2,6},{6,2},{1... | collective-permute-start | bytes 602120 | tf_op jit(solution)/shard_map/ppermute | solution.py:273
  45.2 1.5 %collective-permute-start.7 = (bf16[16,6144]{1,0:T(8,128)(2,1)S(1)}, bf16[16,6144]{1,0:T(8,128)(2,1)S(1)}, u32[]{:S(2)}, u32[]{:S(2)}) collective-permute-start(bf16[16,6144]{1,0:T(8,128)(2,1)S(1)} %get-tuple-element.30), channel_id=1, source_target_pairs={{0,4},{4,0},{8,12},{12,8},{1,5},{5,1},{9,13},{13,9},{2,6},{6,2},{1... | collective-permute-start | bytes 589832 | tf_op jit(solution)/shard_map/ppermute | solution.py:273
  45.5 2.8 %collective-permute-start.6 = (bf16[16,6144]{1,0:T(8,128)(2,1)S(1)}, bf16[16,6144]{1,0:T(8,128)(2,1)S(1)}, u32[]{:S(2)}, u32[]{:S(2)}) collective-permute-start(bf16[16,6144]{1,0:T(8,128)(2,1)S(1)} %get-tuple-element.28), channel_id=1, source_target_pairs={{0,4},{4,0},{8,12},{12,8},{1,5},{5,1},{9,13},{13,9},{2,6},{6,2},{1... | collective-permute-start | bytes 589832 | tf_op jit(solution)/shard_map/ppermute | solution.py:273
  46.7 7.1 %collective-permute-start.8 = (bf16[16,6144]{1,0:T(8,128)(2,1)S(1)}, bf16[16,6144]{1,0:T(8,128)(2,1)S(1)}, u32[]{:S(2)}, u32[]{:S(2)}) collective-permute-start(bf16[16,6144]{1,0:T(8,128)(2,1)S(1)} %add_convert_fusion.1), channel_id=1, source_target_pairs={{0,8},{4,12},{8,0},{12,4},{1,9},{5,13},{9,1},{13,5},{2,10},{6,14},... | collective-permute-start | bytes 589832 | tf_op jit(solution)/shard_map/ppermute | solution.py:273
  54.0 4.2 %collective-permute-start.9 = (bf16[4,6144]{1,0:T(4,128)(2,1)S(1)}, bf16[4,6144]{1,0:T(4,128)(2,1)S(1)}, u32[]{:S(2)}, u32[]{:S(2)}) collective-permute-start(bf16[4,6144]{1,0:T(4,128)(2,1)S(1)} %get-tuple-element.31), channel_id=1, source_target_pairs={{0,1},{1,0},{2,3},{3,2},{4,5},{5,4},{6,7},{7,6},{8,9},{9,8},{10,11... | collective-permute-start | bytes 147464 | tf_op jit(solution)/shard_map/ppermute | solution.py:273
  55.3 6.4 %collective-permute-start.11 = (bf16[4,6144]{1,0:T(4,128)(2,1)S(1)}, bf16[4,6144]{1,0:T(4,128)(2,1)S(1)}, u32[]{:S(2)}, u32[]{:S(2)}) collective-permute-start(bf16[4,6144]{1,0:T(4,128)(2,1)S(1)} %get-tuple-element.32), channel_id=1, source_target_pairs={{0,3},{1,2},{2,1},{3,0},{4,7},{5,6},{6,5},{7,4},{8,11},{9,10},{10,... | collective-permute-start | bytes 147464 | tf_op jit(solution)/shard_map/ppermute | solution.py:273
  57.7 5.0 %collective-permute-start.10 = (bf16[4,6144]{1,0:T(4,128)(2,1)S(1)}, bf16[4,6144]{1,0:T(4,128)(2,1)S(1)}, u32[]{:S(2)}, u32[]{:S(2)}) collective-permute-start(bf16[4,6144]{1,0:T(4,128)(2,1)S(1)} %get-tuple-element.33), channel_id=1, source_target_pairs={{0,2},{1,3},{2,0},{3,1},{4,6},{5,7},{6,4},{7,5},{8,10},{9,11},{10,... | collective-permute-start | bytes 147464 | tf_op jit(solution)/shard_map/ppermute | solution.py:273

commit v3 on v2

--- a/solution.py
+++ b/solution.py
@@ -15,11 +15,21 @@
 
 
 def attend_kernel(
-    lengths, routes, weights, tokens, queries, gain, keys_hbm, values_hbm, ahead_hbm,
-    resid_ref, row_ref, ahead, keys, values, key_sems, value_sems, ahead_sems,
+    *refs,
 ):
+    small_hbm, (keys_hbm, values_hbm, ahead_hbm) = refs[:6], refs[6:9]
+    resid_ref, row_ref, ahead = refs[9:12]
+    small, (keys, values) = refs[12:18], refs[18:20]
+    small_sems, key_sems, value_sems, ahead_sems = refs[20:]
+    queries, tokens, gain, lengths, routes, weights = small
     rows, positions, kv_width = keys_hbm.shape
     width = tokens.shape[1]
+    small_copies = [
+        pltpu.make_async_copy(source, target, small_sems.at[i])
+        for i, (source, target) in enumerate(zip(small_hbm, small))
+    ]
+    for copy in small_copies:
+        copy.start()
     n_kv = kv_width // HEAD_SIZE
     per = width // kv_width
     key_copies = [
@@ -32,11 +42,13 @@
     ahead_copies = ahead_parts(ahead_hbm, ahead, ahead_sems, 0)
     for copy in key_copies + value_copies + ahead_copies:
         copy.start()
+    for copy in small_copies:
+        copy.wait()
     block = per * rows
     owner = lax.broadcasted_iota(jnp.int32, (block, 1), 0) % rows
     length = jnp.zeros((block, 1), jnp.int32)
     for t in range(rows):
-        length = jnp.where(owner == t, lengths[t], length)
+        length = jnp.where(owner == t, lengths[0, t], length)
     alive = lax.broadcasted_iota(jnp.int32, (block, positions), 1) < length
     q = queries[...].astype(F32)
     stacked = []
@@ -97,27 +109,28 @@
         copy.wait()
 
 
-def thirds(hidden_units):
-    return 3 if hidden_units % 48 == 0 else 1
-
-
-def ahead_parts(source, target, sems, part):
+def spans(hidden_units):
+    sizes = [hidden_units]
+    if hidden_units > 1024 and hidden_units % 16 == 0:
+        sizes = [512, 256, hidden_units - 768]
+    return [(sum(sizes[:i]), size) for i, size in enumerate(sizes)]
+
+
+def ahead_parts(source, target, sems, first):
     size = target.shape[1]
     return [
-        pltpu.make_async_copy(
-            source.at[i, part * size : (part + 1) * size], target.at[i], sems.at[i]
-        )
+        pltpu.make_async_copy(source.at[i, first : first + size], target.at[i], sems.at[i])
         for i in range(2)
     ]
 
 
-def ahead_shape(gate_up):
+def ahead_shape(gate_up, part):
     two, hidden_units, width = gate_up.shape
-    return pltpu.VMEM((two, hidden_units // thirds(hidden_units), width), gate_up.dtype)
-
-
-def ahead_kernel(part, source, target, sems):
-    copies = ahead_parts(source, target, sems, part)
+    return pltpu.VMEM((two, spans(hidden_units)[part][1], width), gate_up.dtype)
+
+
+def ahead_kernel(first, source, target, sems):
+    copies = ahead_parts(source, target, sems, first)
     for copy in copies:
         copy.start()
     for copy in copies:
@@ -125,9 +138,9 @@
 
 
 def bring(gate_up, part):
-    shape = ahead_shape(gate_up)
+    shape = ahead_shape(gate_up, part)
     return pl.pallas_call(
-        functools.partial(ahead_kernel, part),
+        functools.partial(ahead_kernel, spans(gate_up.shape[1])[part][0]),
         in_specs=[pl.BlockSpec(memory_space=pltpu.HBM)],
         out_specs=pl.BlockSpec(memory_space=pltpu.VMEM),
         out_shape=shape,
@@ -142,88 +155,95 @@
 
 def attend(tokens, queries, keys, values, lengths, gain, routes, weights, gate_up):
     rows, width = tokens.shape
-    smem = pl.BlockSpec(memory_space=pltpu.SMEM)
     vmem = pl.BlockSpec(memory_space=pltpu.VMEM)
-    hbm = pl.BlockSpec(memory_space=pltpu.HBM)
+    operands = [
+        queries, tokens, gain.reshape(1, width), lengths.reshape(1, rows), routes.T, weights.T,
+        keys, values, gate_up,
+    ]
     return pl.pallas_call(
         attend_kernel,
-        in_specs=[smem, smem, smem, vmem, vmem, vmem, hbm, hbm, hbm],
+        in_specs=[pl.BlockSpec(memory_space=pltpu.HBM)] * len(operands),
         out_specs=[vmem, vmem, vmem],
         out_shape=[
             pltpu.VMEM((rows, width), F32),
             pltpu.VMEM((rows, width + LANES), BF16),
-            ahead_shape(gate_up),
+            ahead_shape(gate_up, 0),
         ],
         scratch_shapes=[
+            pltpu.VMEM(queries.shape, BF16),
+            pltpu.VMEM(tokens.shape, BF16),
+            pltpu.VMEM((1, width), F32),
+            pltpu.SMEM((1, rows), jnp.int32),
+            pltpu.SMEM((routes.shape[1], rows), jnp.int32),
+            pltpu.SMEM((routes.shape[1], rows), F32),
             pltpu.VMEM(keys.shape, BF16),
             pltpu.VMEM(values.shape, BF16),
+            pltpu.SemaphoreType.DMA((6,)),
             pltpu.SemaphoreType.DMA((rows,)),
             pltpu.SemaphoreType.DMA((rows,)),
             pltpu.SemaphoreType.DMA((2,)),
         ],
         compiler_params=pltpu.CompilerParams(vmem_limit_bytes=12 * 2**20),
         name="attend",
-    )(
-        lengths, routes.T, weights.T, tokens, queries, gain.reshape(1, width),
-        in_hbm(keys), in_hbm(values), in_hbm(gate_up),
-    )
-
-
-def expert_kernel(n_pieces, n_parts, chunk, wide, *refs):
+    )(*map(in_hbm, operands))
+
+
+def weighted_down(turned, down, factors, outs):
+    wide = 768
+    size = outs[0].shape[0]
+    for c in range(down.shape[1] // wide):
+        at = slice(c * wide, (c + 1) * wide)
+        total = jnp.dot(turned, down[:, at], preferred_element_type=F32)
+        for i, out in enumerate(outs):
+            out[:, at] = (total[i * size : (i + 1) * size] * factors[i]).astype(BF16)
+
+
+def expert_kernel(n_pieces, n_parts, *refs):
     expert = lax.axis_index("side").astype(jnp.int32)
     pieces = refs[:n_pieces]
     parts = refs[n_pieces : n_pieces + n_parts]
     down_hbm = refs[n_pieces + n_parts]
     outs = refs[n_pieces + n_parts + 1 : 2 * n_pieces + n_parts + 1]
-    x, down, hidden, down_sems = refs[2 * n_pieces + n_parts + 1 :]
-    hidden_units, width = down_hbm.shape
-    part_units = hidden_units // n_parts
+    turned_ref, factor_ref, later = refs[2 * n_pieces + n_parts + 1 : 2 * n_pieces + n_parts + 4]
+    x, down, down_sems = refs[2 * n_pieces + n_parts + 4 :]
+    width = x.shape[1]
+    half = width // 2
     down_copies = [
-        pltpu.make_async_copy(
-            down_hbm.at[c * part_units : (c + 1) * part_units],
-            down.at[c * part_units : (c + 1) * part_units],
-            down_sems.at[c],
-        )
-        for c in range(n_parts)
+        pltpu.make_async_copy(down_hbm.at[:, :half], down, down_sems.at[0]),
+        pltpu.make_async_copy(down_hbm.at[:, half:], later, down_sems.at[1]),
     ]
     for copy in down_copies:
         copy.start()
     size = pieces[0].shape[0]
     factors = []
     for i in range(n_pieces):
-        x[i * size : (i + 1) * size] = pieces[i][:, :width]
+        at = slice(i * size, (i + 1) * size)
+        x[at] = pieces[i][:, :width]
         meta = pieces[i][:, width:].astype(F32)
         lane = lax.broadcasted_iota(jnp.int32, meta.shape, 1)
         mine = lane % (LANES // 2) == expert
         factors.append(jnp.sum(jnp.where(mine, meta, 0.0), axis=1, keepdims=True))
-    for p in range(n_parts):
-        for c in range(part_units // chunk):
-            both = [
-                lax.dot_general(
-                    parts[p][i, c * chunk : (c + 1) * chunk], x[...],
-                    (((1,), (1,)), ((), ())), preferred_element_type=F32,
-                )
-                for i in range(2)
-            ]
-            first = p * part_units + c * chunk
-            hidden[first : first + chunk] = both[0] / (1.0 + jnp.exp(-both[0])) * both[1]
-    turned = jnp.transpose(hidden[...]).astype(BF16)
-    for copy in down_copies:
-        copy.wait()
-    for c in range(width // wide):
-        at = slice(c * wide, (c + 1) * wide)
-        total = jnp.dot(turned, down[:, at], preferred_element_type=F32)
-        for i in range(n_pieces):
-            part = total[i * size : (i + 1) * size] * factors[i]
-            outs[i][:, at] = part.astype(BF16)
-
-
-def in_vmem(value):
-    return pltpu.with_memory_space_constraint(value, pltpu.VMEM)
-
-
-def in_hbm(value):
-    return pltpu.with_memory_space_constraint(value, pltpu.HBM)
+        factor_ref[at] = jnp.broadcast_to(factors[i], (size, LANES))
+    first = 0
+    for part in parts:
+        units = part.shape[1]
+        gate, up = [
+            lax.dot_general(
+                x[...], part[i], (((1,), (1,)), ((), ())), preferred_element_type=F32
+            )
+            for i in range(2)
+        ]
+        turned_ref[:, first : first + units] = (gate / (1.0 + jnp.exp(-gate)) * up).astype(BF16)
+        first += units
+    down_copies[0].wait()
+    weighted_down(turned_ref[...], down, factors, outs)
+    down_copies[1].wait()
+
+
+def later_kernel(n_pieces, turned, factor_ref, down, *outs):
+    size = outs[0].shape[0]
+    factors = [factor_ref[i * size : (i + 1) * size, :1] for i in range(n_pieces)]
+    weighted_down(turned[...], down, factors, outs)
 
 
 def join_kernel(*refs):
@@ -247,25 +267,49 @@
 def experts(pieces, parts, down):
     n_pieces, n_parts = len(pieces), len(parts)
     size, width = pieces[0].shape[0], pieces[0].shape[1] - LANES
-    hidden_units = down.shape[0]
-    part_units = hidden_units // n_parts
-    chunk = part_units // 2 if part_units % 32 == 0 else part_units
+    hidden_units, half = down.shape[0], width // 2
+    rows = n_pieces * size
     vmem = pl.BlockSpec(memory_space=pltpu.VMEM)
-    return pl.pallas_call(
-        functools.partial(expert_kernel, n_pieces, n_parts, chunk, 768),
-        in_specs=[vmem] * (n_pieces + n_parts)
-        + [pl.BlockSpec(memory_space=pltpu.HBM)],
-        out_specs=[vmem] * n_pieces,
-        out_shape=[pltpu.VMEM((size, width), BF16)] * n_pieces,
+    out_shape = [pltpu.VMEM((size, half), BF16)] * n_pieces
+    *first, turned, factor, later = pl.pallas_call(
+        functools.partial(expert_kernel, n_pieces, n_parts),
+        in_specs=[vmem] * (n_pieces + n_parts) + [pl.BlockSpec(memory_space=pltpu.HBM)],
+        out_specs=[vmem] * (n_pieces + 3),
+        out_shape=out_shape
+        + [
+            pltpu.VMEM((rows, hidden_units), BF16),
+            pltpu.VMEM((rows, LANES), F32),
+            pltpu.VMEM((hidden_units, half), BF16),
+        ],
         scratch_shapes=[
-            pltpu.VMEM((n_pieces * size, width), BF16),
-            pltpu.VMEM(down.shape, BF16),
-            pltpu.VMEM((hidden_units, n_pieces * size), F32),
-            pltpu.SemaphoreType.DMA((n_parts,)),
+            pltpu.VMEM((rows, width), BF16),
+            pltpu.VMEM((hidden_units, half), BF16),
+            pltpu.SemaphoreType.DMA((2,)),
         ],
-        compiler_params=pltpu.CompilerParams(vmem_limit_bytes=19 * 2**20),
+        compiler_params=pltpu.CompilerParams(vmem_limit_bytes=16 * 2**20),
         name="experts",
     )(*map(in_vmem, pieces), *map(in_vmem, parts), in_hbm(down))
+    second = pl.pallas_call(
+        functools.partial(later_kernel, n_pieces),
+        in_specs=[vmem] * 3,
+        out_specs=[vmem] * n_pieces,
+        out_shape=out_shape,
+        cost_estimate=pl.CostEstimate(
+            flops=2 * rows * hidden_units * half, transcendentals=0,
+            bytes_accessed=2 * hidden_units * half,
+        ),
+        compiler_params=pltpu.CompilerParams(vmem_limit_bytes=4 * 2**20),
+        name="later",
+    )(in_vmem(turned), in_vmem(factor), in_vmem(later))
+    return list(first), list(second)
+
+
+def in_vmem(value):
+    return pltpu.with_memory_space_constraint(value, pltpu.VMEM)
+
+
+def in_hbm(value):
+    return pltpu.with_memory_space_constraint(value, pltpu.HBM)
 
 
 def swap(value, axis, bits):
@@ -282,6 +326,11 @@
     return steps
 
 
+def split(parts):
+    half = len(parts) // 2
+    return parts[:half], parts[half:]
+
+
 def added(*parts):
     total = parts[0].astype(F32)
     for part in parts[1:]:
@@ -294,13 +343,12 @@
     gate_up, down_proj,
 ):
     n_side = lax.axis_size("side")
-    rows = tokens.shape[0]
     resid, row, first_part = attend(
         tokens, queries, stored_keys, stored_values, lengths, norm_gain, routes, route_weights,
         gate_up[0],
     )
     weight_parts = [first_part]
-    waiting = list(range(1, thirds(gate_up.shape[2])))
+    waiting = list(range(1, len(spans(gate_up.shape[2]))))
 
     def beside(values):
         if not waiting:
@@ -324,25 +372,30 @@
         bit //= 2
     while waiting:
         weight_parts.append(bring(gate_up[0], waiting.pop(0)))
-    parts = list(experts(pieces, weight_parts, down_proj[0]))
+    halves = experts(pieces, weight_parts, down_proj[0])
     for bit in reversed(side_bits):
-        half = len(parts) // 2
-        parts = [
-            added(parts[i], swap(parts[half + i], "side", bit)) for i in range(half)
+        halves = [
+            [added(near, swap(far, "side", bit)) for near, far in zip(*split(parts))]
+            for parts in halves
         ]
-    total = parts[0]
+    totals = [parts[0] for parts in halves]
     for stride, radix in reversed(tp_steps):
-        size = total.shape[0] // radix
-        own = total[:size]
-        other = [
-            swap(total[k * size : (k + 1) * size], "tp", stride * k) for k in range(1, radix)
-        ]
-        if size == rows:
-            mixed = resid + own.astype(F32)
-            for part in other:
-                mixed = mixed + part.astype(F32)
-            return mixed.astype(BF16)
-        total = added(own, *other)
+        size = totals[0].shape[0] // radix
+        gathered = []
+        for total in totals:
+            others = [
+                swap(total[k * size : (k + 1) * size], "tp", stride * k) for k in range(1, radix)
+            ]
+            gathered.append([total[:size]] + others)
+        totals = [added(*parts) for parts in gathered]
+    mixed = []
+    half = resid.shape[1] // 2
+    for i, parts in enumerate(gathered):
+        total = resid[:, i * half : (i + 1) * half]
+        for part in parts:
+            total = total + part.astype(F32)
+        mixed.append(total.astype(BF16))
+    return jnp.concatenate(mixed, axis=1)
 
 
 def solution(mesh):

time: 63.7 us -> 61.7 us (0.969)
  starting transfers between devices: 14.1 us -> 18.8 us
  local copies, waits for them, and re-layouts: 4.41 us -> 0.07 us
  waiting for transfers between devices: 12.5 us -> 11.3 us
  Pallas kernels: 31.5 us -> 30.4 us
    ppermute x12 -> x18, starting transfers between devices: 14.1 us -> 18.8 us  [swap(): return lax.ppermute(value, axis, [(i, i ^ bits) for i in range(n)])]
    unnamed x12 -> x0, local copies, waits for them, and re-layouts: 4.34 us -> none
    ppermute x12 -> x18, waiting for transfers between devices: 12.5 us -> 11.3 us  [swap(): return lax.ppermute(value, axis, [(i, i ^ bits) for i in range(n)])]
    pallas_call x4 -> x5, Pallas kernels: 31.4 us -> 30.4 us  [the longest x1 15.5 us: experts(): pl.pallas_call(functools.partial(expert_kernel, n_pieces, n_parts), in_sp...]
    concatenate x0 -> x1, other arithmetic: none -> 0.64 us  [shards(): return jnp.concatenate(mixed, axis=1)]
  transfers between devices with their start and end apart: 12 -> 18, of which waited for: 7 -> 8; matrix products, arithmetic and copies ran while one was open for 0% -> 0% of each run, Pallas kernels for 14% -> 15%
where the time goes in v3:
time: 61.7 us; the launch traced here: 61.6 us
  Pallas kernels  30.4 us (49%)
  starting transfers between devices  18.8 us (30%)
  waiting for transfers between devices  11.3 us (18%)
  other arithmetic  0.84 us (1%)
    ppermute x18, starting transfers between devices, swap(): return lax.ppermute(value, axis, [(i, i ^ bits) for i in range(n)])  18.8 us
    pallas_call x1, Pallas kernels, experts(): pl.pallas_call(functools.partial(expert_kernel, n_pieces, n_parts), in_sp...  15.5 us
    ppermute x18, waiting for transfers between devices, swap(): return lax.ppermute(value, axis, [(i, i ^ bits) for i in range(n)])  11.3 us
    pallas_call x2, Pallas kernels, bring(): pl.pallas_call(functools.partial(ahead_kernel, spans(gate_up.shape[1])[pa...  7.9 us
    pallas_call x1, Pallas kernels, attend(): pl.pallas_call(attend_kernel, in_specs=[pl.BlockSpec(memory_space=pltpu.H...  5.42 us
    pallas_call x1, Pallas kernels, experts(): pl.pallas_call(functools.partial(later_kernel, n_pieces), in_specs=[vmem]...  1.59 us
  transfers between devices with their start and end apart: 18, of which 8 were waited for; matrix products, arithmetic and copies ran while one was open for 0% of the time, Pallas kernels for 15%

profile of v3, /device:TPU:0, one launch (start us, length us, event | category | flops | bytes accessed | tf_op | source)
XLA Modules:
  0.0 61.6 jit_solution(5116616017867241232)
XLA Ops:
  0.0 5.4 %attend.1 = (f32[4,6144]{1,0:T(4,128)S(1)}, bf16[4,6272]{1,0:T(4,128)(2,1)S(1)}, bf16[2,512,6144]{2,1,0:T(8,128)(2,1)S(1)}) custom-call(bf16[4,6144]{1,0:T(4,128)(2,1)} %refs_0_.1, bf16[4,6144]{1,0:T(4,128)(2,1)} %refs_1_.1, f32[1,6144]{1,0:T(1,128)} %bitcast.10, s32[1,4]{1,0:T(1,128)} %bitcast.13, s32[2,4]{1,0:T(2,128)} %bitcast.11, f32[2,4]{1,0:T(2,128)} %bitcast.12, ...), custom_call_target="tpu_custom_call" | custom-call | tf_op jit(solution)/shard_map/attend/pallas_call | solution.py:163
  5.4 5.1 %collective-permute-start.2 = (bf16[4,6272]{1,0:T(4,128)(2,1)S(1)}, bf16[4,6272]{1,0:T(4,128)(2,1)S(1)}, u32[]{:S(2)}, u32[]{:S(2)}) collective-permute-start(bf16[4,6272]{1,0:T(4,128)(2,1)S(1)} %get-tuple-element.26.refs_0_), channel_id=1, source_target_pairs={{0,3},{1,2},{2,1},{3,0},{4,7},{5,6},{6,5},{7,4},{8,11},{9,10},{10,... | collective-permute-start | bytes 150536 | tf_op jit(solution)/shard_map/ppermute | solution.py:317
  10.6 0.6 %collective-permute-start = (bf16[4,6272]{1,0:T(4,128)(2,1)S(1)}, bf16[4,6272]{1,0:T(4,128)(2,1)S(1)}, u32[]{:S(2)}, u32[]{:S(2)}) collective-permute-start(bf16[4,6272]{1,0:T(4,128)(2,1)S(1)} %get-tuple-element.26.refs_0_), channel_id=1, source_target_pairs={{0,1},{1,0},{2,3},{3,2},{4,5},{5,4},{6,7},{7,6},{8,9},{9,8},{10,11... | collective-permute-start | bytes 150536 | tf_op jit(solution)/shard_map/ppermute | solution.py:317
  11.2 2.9 %bring.2.refs_5_ = bf16[2,256,6144]{2,1,0:T(8,128)(2,1)S(1)} custom-call(bf16[2,1344,6144]{2,1,0:T(8,128)(2,1)} %bitcast.7), custom_call_target="tpu_custom_call" | custom-call | bytes 6291456 | tf_op jit(solution)/shard_map/bring/pallas_call | solution.py:142
  14.1 1.5 %collective-permute-done.1.refs_2_ = bf16[4,6272]{1,0:T(4,128)(2,1)S(1)} collective-permute-done((bf16[4,6272]{1,0:T(4,128)(2,1)S(1)}, bf16[4,6272]{1,0:T(4,128)(2,1)S(1)}, u32[]{:S(2)}, u32[]{:S(2)}) %collective-permute-start.1) | collective-permute-done | bytes 50208 | tf_op jit(solution)/shard_map/ppermute | solution.py:317
  15.6 1.6 %collective-permute-start.3 = (bf16[16,6272]{1,0:T(8,128)(2,1)S(1)}, bf16[16,6272]{1,0:T(8,128)(2,1)S(1)}, u32[]{:S(2)}, u32[]{:S(2)}) collective-permute-start(bf16[16,6272]{1,0:T(8,128)(2,1)S(1)} %join.1.refs_0_), channel_id=1, source_target_pairs={{0,8},{4,12},{8,0},{12,4},{1,9},{5,13},{9,1},{13,5},{2,10},{6,14},... | collective-permute-start | bytes 602120 | tf_op jit(solution)/shard_map/ppermute | solution.py:317
  17.2 5.0 %bring.3.refs_6_ = bf16[2,576,6144]{2,1,0:T(8,128)(2,1)S(1)} custom-call(bf16[2,1344,6144]{2,1,0:T(8,128)(2,1)} %bitcast.8), custom_call_target="tpu_custom_call" | custom-call | bytes 14155776 | tf_op jit(solution)/shard_map/bring/pallas_call | solution.py:142
  22.3 0.5 collective-permute-start.5
  22.8 0.9 %collective-permute-done.4.refs_2_ = bf16[16,6272]{1,0:T(8,128)(2,1)S(1)} collective-permute-done((bf16[16,6272]{1,0:T(8,128)(2,1)S(1)}, bf16[16,6272]{1,0:T(8,128)(2,1)S(1)}, u32[]{:S(2)}, u32[]{:S(2)}) %collective-permute-start.4) | collective-permute-done | bytes 200736 | tf_op jit(solution)/shard_map/ppermute | solution.py:317
  24.0 15.5 %experts.1 = (bf16[16,3072]{1,0:T(8,128)(2,1)S(1)}, bf16[16,3072]{1,0:T(8,128)(2,1)S(1)}, bf16[16,3072]{1,0:T(8,128)(2,1)S(1)}, bf16[16,3072]{1,0:T(8,128)(2,1)S...) custom-call(bf16[16,6272]{1,0:T(8,128)(2,1)S(1)} %join.1.refs_0_, ...), custom_call_target="tpu_custom_call" | custom-call | tf_op jit(solution)/shard_map/experts/pallas_call | solution.py:274
  39.5 0.3 collective-permute-start.7
  40.1 1.6 %later.1 = (bf16[16,3072]{1,0:T(8,128)(2,1)S(1)}, bf16[16,3072]{1,0:T(8,128)(2,1)S(1)}, bf16[16,3072]{1,0:T(8,128)(2,1)S(1)}, bf16[16,3072]{1,0:T(8,128)(2,1)S(1)}) custom-call(bf16[64,1344]{1,0:T(8,128)(2,1)S(1)} %get-tuple-element.38.turned, f32[64,128]{1,0:T(8,128)S(1)} %get-tuple-element.39.factor_ref, bf16[1344,3072]{1,0:T(8,128)(2,1)S(1)} %get-tuple-element.40.down), custom_call_target="tpu_custom_call" | custom-call | flops 528482304 | bytes 8257536 | tf_op jit(solution)/shard_map/later/pallas_call | solution.py:292
  41.7 0.3 collective-permute-start.12
  42.3 0.6 collective-permute-start.8
  42.9 0.4 collective-permute-done.13
  43.3 1.2 %collective-permute-start.14 = (bf16[16,3072]{1,0:T(8,128)(2,1)S(1)}, bf16[16,3072]{1,0:T(8,128)(2,1)S(1)}, u32[]{:S(2)}, u32[]{:S(2)}) collective-permute-start(bf16[16,3072]{1,0:T(8,128)(2,1)S(1)} %add_convert_fusion.1), channel_id=1, source_target_pairs={{0,8},{4,12},{8,0},{12,4},{1,9},{5,13},{9,1},{13,5},{2,10},{6,14},... | collective-permute-start | bytes 294920 | tf_op jit(solution)/shard_map/ppermute | solution.py:317
  44.5 3.5 %collective-permute-done.8 = bf16[16,3072]{1,0:T(8,128)(2,1)S(1)} collective-permute-done((bf16[16,3072]{1,0:T(8,128)(2,1)S(1)}, bf16[16,3072]{1,0:T(8,128)(2,1)S(1)}, u32[]{:S(2)}, u32[]{:S(2)}) %collective-permute-start.8) | collective-permute-done | bytes 98336 | tf_op jit(solution)/shard_map/ppermute | solution.py:317
  48.1 0.8 %collective-permute-start.9 = (bf16[4,3072]{1,0:T(4,128)(2,1)S(1)}, bf16[4,3072]{1,0:T(4,128)(2,1)S(1)}, u32[]{:S(2)}, u32[]{:S(2)}) collective-permute-start(bf16[4,3072]{1,0:T(4,128)(2,1)S(1)} %get-tuple-element.47), channel_id=1, source_target_pairs={{0,1},{1,0},{2,3},{3,2},{4,5},{5,4},{6,7},{7,6},{8,9},{9,8},{10,11... | collective-permute-start | bytes 73736 | tf_op jit(solution)/shard_map/ppermute | solution.py:317
  48.8 2.8 %collective-permute-start.11 = (bf16[4,3072]{1,0:T(4,128)(2,1)S(1)}, bf16[4,3072]{1,0:T(4,128)(2,1)S(1)}, u32[]{:S(2)}, u32[]{:S(2)}) collective-permute-start(bf16[4,3072]{1,0:T(4,128)(2,1)S(1)} %get-tuple-element.48), channel_id=1, source_target_pairs={{0,3},{1,2},{2,1},{3,0},{4,7},{5,6},{6,5},{7,4},{8,11},{9,10},{10,... | collective-permute-start | bytes 73736 | tf_op jit(solution)/shard_map/ppermute | solution.py:317
  51.7 1.7 %collective-permute-start.15 = (bf16[4,3072]{1,0:T(4,128)(2,1)S(1)}, bf16[4,3072]{1,0:T(4,128)(2,1)S(1)}, u32[]{:S(2)}, u32[]{:S(2)}) collective-permute-start(bf16[4,3072]{1,0:T(4,128)(2,1)S(1)} %get-tuple-element.50), channel_id=1, source_target_pairs={{0,1},{1,0},{2,3},{3,2},{4,5},{5,4},{6,7},{7,6},{8,9},{9,8},{10,11... | collective-permute-start | bytes 73736 | tf_op jit(solution)/shard_map/ppermute | solution.py:317
  53.4 2.8 %collective-permute-start.17 = (bf16[4,3072]{1,0:T(4,128)(2,1)S(1)}, bf16[4,3072]{1,0:T(4,128)(2,1)S(1)}, u32[]{:S(2)}, u32[]{:S(2)}) collective-permute-start(bf16[4,3072]{1,0:T(4,128)(2,1)S(1)} %get-tuple-element.51), channel_id=1, source_target_pairs={{0,3},{1,2},{2,1},{3,0},{4,7},{5,6},{6,5},{7,4},{8,11},{9,10},{10,... | collective-permute-start | bytes 73736 | tf_op jit(solution)/shard_map/ppermute | solution.py:317
  56.4 2.6 %collective-permute-done.17 = bf16[4,3072]{1,0:T(4,128)(2,1)S(1)} collective-permute-done((bf16[4,3072]{1,0:T(4,128)(2,1)S(1)}, bf16[4,3072]{1,0:T(4,128)(2,1)S(1)}, u32[]{:S(2)}, u32[]{:S(2)}) %collective-permute-start.17) | collective-permute-done | bytes 24608 | tf_op jit(solution)/shard_map/ppermute | solution.py:317
  59.0 1.9 %collective-permute-done.16 = bf16[4,3072]{1,0:T(4,128)(2,1)S(1)} collective-permute-done((bf16[4,3072]{1,0:T(4,128)(2,1)S(1)}, bf16[4,3072]{1,0:T(4,128)(2,1)S(1)}, u32[]{:S(2)}, u32[]{:S(2)}) %collective-permute-start.16) | collective-permute-done | bytes 24608 | tf_op jit(solution)/shard_map/ppermute | solution.py:317
  60.9 0.6 %pad_maximum_fusion = bf16[4,6144]{1,0:T(4,128)(2,1)} fusion(bf16[4,3072]{1,0:T(4,128)(2,1)S(1)} %get-tuple-element.46, bf16[4,3072]{1,0:T(4,128)(2,1)S(1)} %get-tuple-element.45), kind=kLoop, calls=%fused_computation.6 | loop fusion | flops 98304 | bytes 98304 | tf_op jit(solution)/shard_map/concatenate | solution.py:398
  (26 shorter events, 1.5 us)
Async XLA Ops:
  5.4 8.6 %collective-permute-start.2 = (bf16[4,6272]{1,0:T(4,128)(2,1)S(1)}, bf16[4,6272]{1,0:T(4,128)(2,1)S(1)}, u32[]{:S(2)}, u32[]{:S(2)}) collective-permute-start(bf16[4,6272]{1,0:T(4,128)(2,1)S(1)} %get-tuple-element.26.refs_0_), channel_id=1, source_target_pairs={{0,3},{1,2},{2,1},{3,0},{4,7},{5,6},{6,5},{7,4},{8,11},{9,10},{10,... | collective-permute-start | bytes 150536 | tf_op jit(solution)/shard_map/ppermute | solution.py:317
  10.5 5.0 %collective-permute-start.1 = (bf16[4,6272]{1,0:T(4,128)(2,1)S(1)}, bf16[4,6272]{1,0:T(4,128)(2,1)S(1)}, u32[]{:S(2)}, u32[]{:S(2)}) collective-permute-start(bf16[4,6272]{1,0:T(4,128)(2,1)S(1)} %get-tuple-element.26.refs_0_), channel_id=1, source_target_pairs={{0,2},{1,3},{2,0},{3,1},{4,6},{5,7},{6,4},{7,5},{8,10},{9,11},{10,... | collective-permute-start | bytes 150536 | tf_op jit(solution)/shard_map/ppermute | solution.py:317
  10.6 5.0 %collective-permute-start = (bf16[4,6272]{1,0:T(4,128)(2,1)S(1)}, bf16[4,6272]{1,0:T(4,128)(2,1)S(1)}, u32[]{:S(2)}, u32[]{:S(2)}) collective-permute-start(bf16[4,6272]{1,0:T(4,128)(2,1)S(1)} %get-tuple-element.26.refs_0_), channel_id=1, source_target_pairs={{0,1},{1,0},{2,3},{3,2},{4,5},{5,4},{6,7},{7,6},{8,9},{9,8},{10,11... | collective-permute-start | bytes 150536 | tf_op jit(solution)/shard_map/ppermute | solution.py:317
  15.6 6.7 %collective-permute-start.3 = (bf16[16,6272]{1,0:T(8,128)(2,1)S(1)}, bf16[16,6272]{1,0:T(8,128)(2,1)S(1)}, u32[]{:S(2)}, u32[]{:S(2)}) collective-permute-start(bf16[16,6272]{1,0:T(8,128)(2,1)S(1)} %join.1.refs_0_), channel_id=1, source_target_pairs={{0,8},{4,12},{8,0},{12,4},{1,9},{5,13},{9,1},{13,5},{2,10},{6,14},... | collective-permute-start | bytes 602120 | tf_op jit(solution)/shard_map/ppermute | solution.py:317
  22.2 1.5 %collective-permute-start.4 = (bf16[16,6272]{1,0:T(8,128)(2,1)S(1)}, bf16[16,6272]{1,0:T(8,128)(2,1)S(1)}, u32[]{:S(2)}, u32[]{:S(2)}) collective-permute-start(bf16[16,6272]{1,0:T(8,128)(2,1)S(1)} %join.1.refs_0_), channel_id=1, source_target_pairs={{0,4},{4,0},{8,12},{12,8},{1,5},{5,1},{9,13},{13,9},{2,6},{6,2},{1... | collective-permute-start | bytes 602120 | tf_op jit(solution)/shard_map/ppermute | solution.py:317
  22.3 1.7 %collective-permute-start.5 = (bf16[16,6272]{1,0:T(8,128)(2,1)S(1)}, bf16[16,6272]{1,0:T(8,128)(2,1)S(1)}, u32[]{:S(2)}, u32[]{:S(2)}) collective-permute-start(bf16[16,6272]{1,0:T(8,128)(2,1)S(1)} %collective-permute-done.3.refs_1_), channel_id=1, source_target_pairs={{0,4},{4,0},{8,12},{12,8},{1,5},{5,1},{9,13},{13,9},{2,6},{6,2},{1... | collective-permute-start | bytes 602120 | tf_op jit(solution)/shard_map/ppermute | solution.py:317
  39.5 2.7 %collective-permute-start.7 = (bf16[16,3072]{1,0:T(8,128)(2,1)S(1)}, bf16[16,3072]{1,0:T(8,128)(2,1)S(1)}, u32[]{:S(2)}, u32[]{:S(2)}) collective-permute-start(bf16[16,3072]{1,0:T(8,128)(2,1)S(1)} %get-tuple-element.37), channel_id=1, source_target_pairs={{0,4},{4,0},{8,12},{12,8},{1,5},{5,1},{9,13},{13,9},{2,6},{6,2},{1... | collective-permute-start | bytes 294920 | tf_op jit(solution)/shard_map/ppermute | solution.py:317
  39.8 4.7 %collective-permute-start.6 = (bf16[16,3072]{1,0:T(8,128)(2,1)S(1)}, bf16[16,3072]{1,0:T(8,128)(2,1)S(1)}, u32[]{:S(2)}, u32[]{:S(2)}) collective-permute-start(bf16[16,3072]{1,0:T(8,128)(2,1)S(1)} %get-tuple-element.35), channel_id=1, source_target_pairs={{0,4},{4,0},{8,12},{12,8},{1,5},{5,1},{9,13},{13,9},{2,6},{6,2},{1... | collective-permute-start | bytes 294920 | tf_op jit(solution)/shard_map/ppermute | solution.py:317
  41.7 9.9 %collective-permute-start.12 = (bf16[16,3072]{1,0:T(8,128)(2,1)S(1)}, bf16[16,3072]{1,0:T(8,128)(2,1)S(1)}, u32[]{:S(2)}, u32[]{:S(2)}) collective-permute-start(bf16[16,3072]{1,0:T(8,128)(2,1)S(1)} %get-tuple-element.42), channel_id=1, source_target_pairs={{0,4},{4,0},{8,12},{12,8},{1,5},{5,1},{9,13},{13,9},{2,6},{6,2},{1... | collective-permute-start | bytes 294920 | tf_op jit(solution)/shard_map/ppermute | solution.py:317
  42.0 1.3 %collective-permute-start.13 = (bf16[16,3072]{1,0:T(8,128)(2,1)S(1)}, bf16[16,3072]{1,0:T(8,128)(2,1)S(1)}, u32[]{:S(2)}, u32[]{:S(2)}) collective-permute-start(bf16[16,3072]{1,0:T(8,128)(2,1)S(1)} %get-tuple-element.44), channel_id=1, source_target_pairs={{0,4},{4,0},{8,12},{12,8},{1,5},{5,1},{9,13},{13,9},{2,6},{6,2},{1... | collective-permute-start | bytes 294920 | tf_op jit(solution)/shard_map/ppermute | solution.py:317
  42.3 5.7 %collective-permute-start.8 = (bf16[16,3072]{1,0:T(8,128)(2,1)S(1)}, bf16[16,3072]{1,0:T(8,128)(2,1)S(1)}, u32[]{:S(2)}, u32[]{:S(2)}) collective-permute-start(bf16[16,3072]{1,0:T(8,128)(2,1)S(1)} %add_convert_fusion.4), channel_id=1, source_target_pairs={{0,8},{4,12},{8,0},{12,4},{1,9},{5,13},{9,1},{13,5},{2,10},{6,14},... | collective-permute-start | bytes 294920 | tf_op jit(solution)/shard_map/ppermute | solution.py:317
  43.3 8.3 %collective-permute-start.14 = (bf16[16,3072]{1,0:T(8,128)(2,1)S(1)}, bf16[16,3072]{1,0:T(8,128)(2,1)S(1)}, u32[]{:S(2)}, u32[]{:S(2)}) collective-permute-start(bf16[16,3072]{1,0:T(8,128)(2,1)S(1)} %add_convert_fusion.1), channel_id=1, source_target_pairs={{0,8},{4,12},{8,0},{12,4},{1,9},{5,13},{9,1},{13,5},{2,10},{6,14},... | collective-permute-start | bytes 294920 | tf_op jit(solution)/shard_map/ppermute | solution.py:317
  48.1 8.1 %collective-permute-start.9 = (bf16[4,3072]{1,0:T(4,128)(2,1)S(1)}, bf16[4,3072]{1,0:T(4,128)(2,1)S(1)}, u32[]{:S(2)}, u32[]{:S(2)}) collective-permute-start(bf16[4,3072]{1,0:T(4,128)(2,1)S(1)} %get-tuple-element.47), channel_id=1, source_target_pairs={{0,1},{1,0},{2,3},{3,2},{4,5},{5,4},{6,7},{7,6},{8,9},{9,8},{10,11... | collective-permute-start | bytes 73736 | tf_op jit(solution)/shard_map/ppermute | solution.py:317
  48.8 7.3 %collective-permute-start.11 = (bf16[4,3072]{1,0:T(4,128)(2,1)S(1)}, bf16[4,3072]{1,0:T(4,128)(2,1)S(1)}, u32[]{:S(2)}, u32[]{:S(2)}) collective-permute-start(bf16[4,3072]{1,0:T(4,128)(2,1)S(1)} %get-tuple-element.48), channel_id=1, source_target_pairs={{0,3},{1,2},{2,1},{3,0},{4,7},{5,6},{6,5},{7,4},{8,11},{9,10},{10,... | collective-permute-start | bytes 73736 | tf_op jit(solution)/shard_map/ppermute | solution.py:317
  51.6 4.8 %collective-permute-start.10 = (bf16[4,3072]{1,0:T(4,128)(2,1)S(1)}, bf16[4,3072]{1,0:T(4,128)(2,1)S(1)}, u32[]{:S(2)}, u32[]{:S(2)}) collective-permute-start(bf16[4,3072]{1,0:T(4,128)(2,1)S(1)} %get-tuple-element.49), channel_id=1, source_target_pairs={{0,2},{1,3},{2,0},{3,1},{4,6},{5,7},{6,4},{7,5},{8,10},{9,11},{10,... | collective-permute-start | bytes 73736 | tf_op jit(solution)/shard_map/ppermute | solution.py:317
  51.7 4.7 %collective-permute-start.15 = (bf16[4,3072]{1,0:T(4,128)(2,1)S(1)}, bf16[4,3072]{1,0:T(4,128)(2,1)S(1)}, u32[]{:S(2)}, u32[]{:S(2)}) collective-permute-start(bf16[4,3072]{1,0:T(4,128)(2,1)S(1)} %get-tuple-element.50), channel_id=1, source_target_pairs={{0,1},{1,0},{2,3},{3,2},{4,5},{5,4},{6,7},{7,6},{8,9},{9,8},{10,11... | collective-permute-start | bytes 73736 | tf_op jit(solution)/shard_map/ppermute | solution.py:317
  53.4 5.6 %collective-permute-start.17 = (bf16[4,3072]{1,0:T(4,128)(2,1)S(1)}, bf16[4,3072]{1,0:T(4,128)(2,1)S(1)}, u32[]{:S(2)}, u32[]{:S(2)}) collective-permute-start(bf16[4,3072]{1,0:T(4,128)(2,1)S(1)} %get-tuple-element.51), channel_id=1, source_target_pairs={{0,3},{1,2},{2,1},{3,0},{4,7},{5,6},{6,5},{7,4},{8,11},{9,10},{10,... | collective-permute-start | bytes 73736 | tf_op jit(solution)/shard_map/ppermute | solution.py:317
  56.2 4.7 %collective-permute-start.16 = (bf16[4,3072]{1,0:T(4,128)(2,1)S(1)}, bf16[4,3072]{1,0:T(4,128)(2,1)S(1)}, u32[]{:S(2)}, u32[]{:S(2)}) collective-permute-start(bf16[4,3072]{1,0:T(4,128)(2,1)S(1)} %get-tuple-element.52), channel_id=1, source_target_pairs={{0,2},{1,3},{2,0},{3,1},{4,6},{5,7},{6,4},{7,5},{8,10},{9,11},{10,... | collective-permute-start | bytes 73736 | tf_op jit(solution)/shard_map/ppermute | solution.py:317

commit v4 on v3

--- a/solution.py
+++ b/solution.py
@@ -112,7 +112,7 @@
 def spans(hidden_units):
     sizes = [hidden_units]
     if hidden_units > 1024 and hidden_units % 16 == 0:
-        sizes = [512, 256, hidden_units - 768]
+        sizes = [256, 256, 256, hidden_units - 768]
     return [(sum(sizes[:i]), size) for i, size in enumerate(sizes)]
 
 
@@ -208,12 +208,17 @@
     x, down, down_sems = refs[2 * n_pieces + n_parts + 4 :]
     width = x.shape[1]
     half = width // 2
+    quarter = half // 2
     down_copies = [
-        pltpu.make_async_copy(down_hbm.at[:, :half], down, down_sems.at[0]),
-        pltpu.make_async_copy(down_hbm.at[:, half:], later, down_sems.at[1]),
-    ]
-    for copy in down_copies:
-        copy.start()
+        pltpu.make_async_copy(
+            down_hbm.at[:, c * quarter : (c + 1) * quarter],
+            (down, later)[c // 2].at[:, c % 2 * quarter : (c % 2 + 1) * quarter],
+            down_sems.at[c],
+        )
+        for c in range(4)
+    ]
+    to_start = list(down_copies)
+    to_start.pop(0).start()
     size = pieces[0].shape[0]
     factors = []
     for i in range(n_pieces):
@@ -227,6 +232,8 @@
     first = 0
     for part in parts:
         units = part.shape[1]
+        if to_start and part is not parts[-1]:
+            to_start.pop(0).start()
         gate, up = [
             lax.dot_general(
                 x[...], part[i], (((1,), (1,)), ((), ())), preferred_element_type=F32
@@ -235,9 +242,13 @@
         ]
         turned_ref[:, first : first + units] = (gate / (1.0 + jnp.exp(-gate)) * up).astype(BF16)
         first += units
-    down_copies[0].wait()
+    for copy in to_start:
+        copy.start()
+    for copy in down_copies[:2]:
+        copy.wait()
     weighted_down(turned_ref[...], down, factors, outs)
-    down_copies[1].wait()
+    for copy in down_copies[2:]:
+        copy.wait()
 
 
 def later_kernel(n_pieces, turned, factor_ref, down, *outs):
@@ -284,7 +295,7 @@
         scratch_shapes=[
             pltpu.VMEM((rows, width), BF16),
             pltpu.VMEM((hidden_units, half), BF16),
-            pltpu.SemaphoreType.DMA((2,)),
+            pltpu.SemaphoreType.DMA((4,)),
         ],
         compiler_params=pltpu.CompilerParams(vmem_limit_bytes=16 * 2**20),
         name="experts",
@@ -318,17 +329,7 @@
 
 
 def strides(size):
-    steps, stride = [], 1
-    while stride < size:
-        radix = 4 if size // stride >= 4 else 2
-        steps.append((stride, radix))
-        stride *= radix
-    return steps
-
-
-def split(parts):
-    half = len(parts) // 2
-    return parts[:half], parts[half:]
+    return [size >> i for i in range(1, size.bit_length())]
 
 
 def added(*parts):
@@ -338,11 +339,15 @@
     return total.astype(BF16)
 
 
+def exchanged(parts, axis, stride):
+    half = len(parts) // 2
+    return [added(parts[i], swap(parts[half + i], axis, stride)) for i in range(half)]
+
+
 def shards(
     tokens, queries, stored_keys, stored_values, lengths, norm_gain, routes, route_weights,
     gate_up, down_proj,
 ):
-    n_side = lax.axis_size("side")
     resid, row, first_part = attend(
         tokens, queries, stored_keys, stored_values, lengths, norm_gain, routes, route_weights,
         gate_up[0],
@@ -359,43 +364,29 @@
         return values
 
     tp_steps = strides(lax.axis_size("tp"))
+    side_steps = strides(lax.axis_size("side"))
     held = row
-    for stride, radix in tp_steps:
-        others = beside([swap(held, "tp", stride * k) for k in range(1, radix)])
-        held = join([held] + others)
+    for stride in tp_steps:
+        held = join([held] + beside([swap(held, "tp", stride)]))
     pieces = [held]
-    side_bits = []
-    bit = n_side // 2
-    while bit:
-        side_bits.append(bit)
-        pieces = pieces + beside([swap(piece, "side", bit) for piece in pieces])
-        bit //= 2
+    for stride in side_steps:
+        pieces = pieces + beside([swap(piece, "side", stride) for piece in pieces])
     while waiting:
         weight_parts.append(bring(gate_up[0], waiting.pop(0)))
     halves = experts(pieces, weight_parts, down_proj[0])
-    for bit in reversed(side_bits):
-        halves = [
-            [added(near, swap(far, "side", bit)) for near, far in zip(*split(parts))]
-            for parts in halves
-        ]
-    totals = [parts[0] for parts in halves]
-    for stride, radix in reversed(tp_steps):
-        size = totals[0].shape[0] // radix
-        gathered = []
-        for total in totals:
-            others = [
-                swap(total[k * size : (k + 1) * size], "tp", stride * k) for k in range(1, radix)
-            ]
-            gathered.append([total[:size]] + others)
-        totals = [added(*parts) for parts in gathered]
-    mixed = []
-    half = resid.shape[1] // 2
-    for i, parts in enumerate(gathered):
-        total = resid[:, i * half : (i + 1) * half]
-        for part in parts:
-            total = total + part.astype(F32)
-        mixed.append(total.astype(BF16))
-    return jnp.concatenate(mixed, axis=1)
+    parts = [
+        jnp.concatenate(both, axis=1)
+        for both in zip(*[exchanged(half, "side", side_steps[-1]) for half in halves])
+    ]
+    for stride in reversed(side_steps[:-1]):
+        parts = exchanged(parts, "side", stride)
+    total = parts[0]
+    for stride in reversed(tp_steps[1:]):
+        half = total.shape[0] // 2
+        total = added(total[:half], swap(total[half:], "tp", stride))
+    rows = resid.shape[0]
+    last = swap(total[rows:], "tp", tp_steps[0])
+    return (resid + total[:rows].astype(F32) + last.astype(F32)).astype(BF16)
 
 
 def solution(mesh):

time: 61.7 us -> 61.4 us (level)
  starting transfers between devices: 18.8 us -> 13.7 us
  waiting for transfers between devices: 11.3 us -> 14.6 us
  Pallas kernels: 30.4 us -> 31.9 us
    ppermute x18 -> x12, starting transfers between devices: 18.8 us -> 13.7 us  [swap(): return lax.ppermute(value, axis, [(i, i ^ bits) for i in range(n)])]
    ppermute x18 -> x12, waiting for transfers between devices: 11.3 us -> 14.6 us  [swap(): return lax.ppermute(value, axis, [(i, i ^ bits) for i in range(n)])]
    pallas_call x2 -> x3, Pallas kernels: 7.9 us -> 10.8 us  [bring(): pl.pallas_call(functools.partial(ahead_kernel, spans(gate_up.shape[1])[pa...]
    pallas_call x1, Pallas kernels: 5.42 us -> 3.94 us  [attend(): pl.pallas_call(attend_kernel, in_specs=[pl.BlockSpec(memory_space=pltpu.H...]
    concatenate x1, other arithmetic: 0.64 us -> 0.02 us  [shards(): jnp.concatenate(both, axis=1)]
  transfers between devices with their start and end apart: 18 -> 12, of which waited for: 8 -> 7; matrix products, arithmetic and copies ran while one was open for 0% -> 0% of each run, Pallas kernels for 15% -> 20%
where the time goes in v4:
time: 61.4 us; the launch traced here: 61.2 us
  Pallas kernels  31.9 us (52%)
  waiting for transfers between devices  14.6 us (24%)
  starting transfers between devices  13.7 us (22%)
  other arithmetic  0.85 us (1%)
    pallas_call x1, Pallas kernels, experts(): pl.pallas_call(functools.partial(expert_kernel, n_pieces, n_parts), in_sp...  15.6 us
    ppermute x12, waiting for transfers between devices, swap(): return lax.ppermute(value, axis, [(i, i ^ bits) for i in range(n)])  14.6 us
    ppermute x12, starting transfers between devices, swap(): return lax.ppermute(value, axis, [(i, i ^ bits) for i in range(n)])  13.7 us
    pallas_call x3, Pallas kernels, bring(): pl.pallas_call(functools.partial(ahead_kernel, spans(gate_up.shape[1])[pa...  10.8 us
    pallas_call x1, Pallas kernels, attend(): pl.pallas_call(attend_kernel, in_specs=[pl.BlockSpec(memory_space=pltpu.H...  3.94 us
    pallas_call x1, Pallas kernels, experts(): pl.pallas_call(functools.partial(later_kernel, n_pieces), in_specs=[vmem]...  1.59 us
  transfers between devices with their start and end apart: 12, of which 7 were waited for; matrix products, arithmetic and copies ran while one was open for 0% of the time, Pallas kernels for 20%

profile of v4, /device:TPU:0, one launch (start us, length us, event | category | flops | bytes accessed | tf_op | source)
XLA Modules:
  0.0 61.2 jit_solution(8436330156168574960)
XLA Ops:
  0.0 3.9 %attend.1 = (f32[4,6144]{1,0:T(4,128)S(1)}, bf16[4,6272]{1,0:T(4,128)(2,1)S(1)}, bf16[2,256,6144]{2,1,0:T(8,128)(2,1)S(1)}) custom-call(bf16[4,6144]{1,0:T(4,128)(2,1)} %refs_0_.1, bf16[4,6144]{1,0:T(4,128)(2,1)} %refs_1_.1, f32[1,6144]{1,0:T(1,128)} %bitcast.11, s32[1,4]{1,0:T(1,128)} %bitcast.14, s32[2,4]{1,0:T(2,128)} %bitcast.12, f32[2,4]{1,0:T(2,128)} %bitcast.13, ...), custom_call_target="tpu_custom_call" | custom-call | tf_op jit(solution)/shard_map/attend/pallas_call | solution.py:163
  3.9 4.1 %collective-permute-start = (bf16[4,6272]{1,0:T(4,128)(2,1)S(1)}, bf16[4,6272]{1,0:T(4,128)(2,1)S(1)}, u32[]{:S(2)}, u32[]{:S(2)}) collective-permute-start(bf16[4,6272]{1,0:T(4,128)(2,1)S(1)} %get-tuple-element.26.refs_0_), channel_id=1, source_target_pairs={{0,2},{1,3},{2,0},{3,1},{4,6},{5,7},{6,4},{7,5},{8,10},{9,11},{10,... | collective-permute-start | bytes 150536 | tf_op jit(solution)/shard_map/ppermute | solution.py:328
  8.0 2.9 %bring.3.refs_5_ = bf16[2,256,6144]{2,1,0:T(8,128)(2,1)S(1)} custom-call(bf16[2,1344,6144]{2,1,0:T(8,128)(2,1)} %bitcast.7), custom_call_target="tpu_custom_call" | custom-call | bytes 6291456 | tf_op jit(solution)/shard_map/bring/pallas_call | solution.py:142
  11.0 1.6 %collective-permute-start.1 = (bf16[8,6272]{1,0:T(8,128)(2,1)S(1)}, bf16[8,6272]{1,0:T(8,128)(2,1)S(1)}, u32[]{:S(2)}, u32[]{:S(2)}) collective-permute-start(bf16[8,6272]{1,0:T(8,128)(2,1)S(1)} %join.2.refs_0_), channel_id=1, source_target_pairs={{0,1},{1,0},{2,3},{3,2},{4,5},{5,4},{6,7},{7,6},{8,9},{9,8},{10,11... | collective-permute-start | bytes 301064 | tf_op jit(solution)/shard_map/ppermute | solution.py:328
  12.6 2.9 %bring.4.refs_6_ = bf16[2,256,6144]{2,1,0:T(8,128)(2,1)S(1)} custom-call(bf16[2,1344,6144]{2,1,0:T(8,128)(2,1)} %bitcast.8), custom_call_target="tpu_custom_call" | custom-call | bytes 6291456 | tf_op jit(solution)/shard_map/bring/pallas_call | solution.py:142
  15.7 1.6 %collective-permute-start.2 = (bf16[16,6272]{1,0:T(8,128)(2,1)S(1)}, bf16[16,6272]{1,0:T(8,128)(2,1)S(1)}, u32[]{:S(2)}, u32[]{:S(2)}) collective-permute-start(bf16[16,6272]{1,0:T(8,128)(2,1)S(1)} %join.3.refs_0_), channel_id=1, source_target_pairs={{0,8},{4,12},{8,0},{12,4},{1,9},{5,13},{9,1},{13,5},{2,10},{6,14},... | collective-permute-start | bytes 602120 | tf_op jit(solution)/shard_map/ppermute | solution.py:328
  17.2 5.0 %bring.5.refs_7_ = bf16[2,576,6144]{2,1,0:T(8,128)(2,1)S(1)} custom-call(bf16[2,1344,6144]{2,1,0:T(8,128)(2,1)} %bitcast.9), custom_call_target="tpu_custom_call" | custom-call | bytes 14155776 | tf_op jit(solution)/shard_map/bring/pallas_call | solution.py:142
  22.4 0.5 collective-permute-start.4
  22.9 0.9 %collective-permute-done.3.refs_2_ = bf16[16,6272]{1,0:T(8,128)(2,1)S(1)} collective-permute-done((bf16[16,6272]{1,0:T(8,128)(2,1)S(1)}, bf16[16,6272]{1,0:T(8,128)(2,1)S(1)}, u32[]{:S(2)}, u32[]{:S(2)}) %collective-permute-start.3) | collective-permute-done | bytes 200736 | tf_op jit(solution)/shard_map/ppermute | solution.py:328
  23.8 0.3 collective-permute-done.4.refs_3_
  24.1 15.6 %experts.1 = (bf16[16,3072]{1,0:T(8,128)(2,1)S(1)}, bf16[16,3072]{1,0:T(8,128)(2,1)S(1)}, bf16[16,3072]{1,0:T(8,128)(2,1)S(1)}, bf16[16,3072]{1,0:T(8,128)(2,1)S...) custom-call(bf16[16,6272]{1,0:T(8,128)(2,1)S(1)} %join.3.refs_0_, ...), custom_call_target="tpu_custom_call" | custom-call | tf_op jit(solution)/shard_map/experts/pallas_call | solution.py:285
  39.7 0.3 collective-permute-start.7
  40.0 0.3 collective-permute-start.5
  40.3 1.6 %later.1 = (bf16[16,3072]{1,0:T(8,128)(2,1)S(1)}, bf16[16,3072]{1,0:T(8,128)(2,1)S(1)}, bf16[16,3072]{1,0:T(8,128)(2,1)S(1)}, bf16[16,3072]{1,0:T(8,128)(2,1)S(1)}) custom-call(bf16[64,1344]{1,0:T(8,128)(2,1)S(1)} %get-tuple-element.36.turned, f32[64,128]{1,0:T(8,128)S(1)} %get-tuple-element.37.factor_ref, bf16[1344,3072]{1,0:T(8,128)(2,1)S(1)} %get-tuple-element.38.down), custom_call_target="tpu_custom_call" | custom-call | flops 528482304 | bytes 8257536 | tf_op jit(solution)/shard_map/later/pallas_call | solution.py:303
  41.9 0.3 collective-permute-start.6
  42.2 0.3 collective-permute-start.8
  42.5 1.0 %collective-permute-done.8 = bf16[16,3072]{1,0:T(8,128)(2,1)S(1)} collective-permute-done((bf16[16,3072]{1,0:T(8,128)(2,1)S(1)}, bf16[16,3072]{1,0:T(8,128)(2,1)S(1)}, u32[]{:S(2)}, u32[]{:S(2)}) %collective-permute-start.8) | collective-permute-done | bytes 98336 | tf_op jit(solution)/shard_map/ppermute | solution.py:328
  43.5 0.6 collective-permute-start.9
  44.2 6.5 %collective-permute-done.9 = bf16[16,6144]{1,0:T(8,128)(2,1)S(1)} collective-permute-done((bf16[16,6144]{1,0:T(8,128)(2,1)S(1)}, bf16[16,6144]{1,0:T(8,128)(2,1)S(1)}, u32[]{:S(2)}, u32[]{:S(2)}) %collective-permute-start.9) | collective-permute-done | bytes 196640 | tf_op jit(solution)/shard_map/ppermute | solution.py:328
  50.8 1.6 %collective-permute-start.10 = (bf16[8,6144]{1,0:T(8,128)(2,1)S(1)}, bf16[8,6144]{1,0:T(8,128)(2,1)S(1)}, u32[]{:S(2)}, u32[]{:S(2)}) collective-permute-start(bf16[8,6144]{1,0:T(8,128)(2,1)S(1)} %slice.17), channel_id=1, source_target_pairs={{0,1},{1,0},{2,3},{3,2},{4,5},{5,4},{6,7},{7,6},{8,9},{9,8},{10,11... | collective-permute-start | bytes 294920 | tf_op jit(solution)/shard_map/ppermute | solution.py:328
  52.4 3.0 %collective-permute-done.10 = bf16[8,6144]{1,0:T(8,128)(2,1)S(1)} collective-permute-done((bf16[8,6144]{1,0:T(8,128)(2,1)S(1)}, bf16[8,6144]{1,0:T(8,128)(2,1)S(1)}, u32[]{:S(2)}, u32[]{:S(2)}) %collective-permute-start.10) | collective-permute-done | bytes 98336 | tf_op jit(solution)/shard_map/ppermute | solution.py:328
  55.5 2.4 %collective-permute-start.11 = (bf16[4,6144]{1,0:T(4,128)(2,1)S(1)}, bf16[4,6144]{1,0:T(4,128)(2,1)S(1)}, u32[]{:S(2)}, u32[]{:S(2)}) collective-permute-start(bf16[4,6144]{1,0:T(4,128)(2,1)S(1)} %slice.19), channel_id=1, source_target_pairs={{0,2},{1,3},{2,0},{3,1},{4,6},{5,7},{6,4},{7,5},{8,10},{9,11},{10,... | collective-permute-start | bytes 147464 | tf_op jit(solution)/shard_map/ppermute | solution.py:328
  57.9 2.6 %collective-permute-done.11 = bf16[4,6144]{1,0:T(4,128)(2,1)S(1)} collective-permute-done((bf16[4,6144]{1,0:T(4,128)(2,1)S(1)}, bf16[4,6144]{1,0:T(4,128)(2,1)S(1)}, u32[]{:S(2)}, u32[]{:S(2)}) %collective-permute-start.11) | collective-permute-done | bytes 49184 | tf_op jit(solution)/shard_map/ppermute | solution.py:328
  60.6 0.7 %add_convert_fusion.6 = bf16[4,6144]{1,0:T(4,128)(2,1)} fusion(bf16[4,6144]{1,0:T(4,128)(2,1)S(1)} %collective-permute-done.11, f32[4,6144]{1,0:T(4,128)S(1)} %get-tuple-element.25, bf16[8,6144]{1,0:T(8,128)(2,1)S(1)} %add_convert_fusion.1), kind=kLoop, calls=%fused_computation.7 | loop fusion | flops 122880 | bytes 245760 | tf_op jit(solution)/shard_map/convert_element_type | solution.py:389
  (18 shorter events, 0.6 us)
Async XLA Ops:
  3.9 7.0 %collective-permute-start = (bf16[4,6272]{1,0:T(4,128)(2,1)S(1)}, bf16[4,6272]{1,0:T(4,128)(2,1)S(1)}, u32[]{:S(2)}, u32[]{:S(2)}) collective-permute-start(bf16[4,6272]{1,0:T(4,128)(2,1)S(1)} %get-tuple-element.26.refs_0_), channel_id=1, source_target_pairs={{0,2},{1,3},{2,0},{3,1},{4,6},{5,7},{6,4},{7,5},{8,10},{9,11},{10,... | collective-permute-start | bytes 150536 | tf_op jit(solution)/shard_map/ppermute | solution.py:328
  11.0 4.7 %collective-permute-start.1 = (bf16[8,6272]{1,0:T(8,128)(2,1)S(1)}, bf16[8,6272]{1,0:T(8,128)(2,1)S(1)}, u32[]{:S(2)}, u32[]{:S(2)}) collective-permute-start(bf16[8,6272]{1,0:T(8,128)(2,1)S(1)} %join.2.refs_0_), channel_id=1, source_target_pairs={{0,1},{1,0},{2,3},{3,2},{4,5},{5,4},{6,7},{7,6},{8,9},{9,8},{10,11... | collective-permute-start | bytes 301064 | tf_op jit(solution)/shard_map/ppermute | solution.py:328
  15.7 6.7 %collective-permute-start.2 = (bf16[16,6272]{1,0:T(8,128)(2,1)S(1)}, bf16[16,6272]{1,0:T(8,128)(2,1)S(1)}, u32[]{:S(2)}, u32[]{:S(2)}) collective-permute-start(bf16[16,6272]{1,0:T(8,128)(2,1)S(1)} %join.3.refs_0_), channel_id=1, source_target_pairs={{0,8},{4,12},{8,0},{12,4},{1,9},{5,13},{9,1},{13,5},{2,10},{6,14},... | collective-permute-start | bytes 602120 | tf_op jit(solution)/shard_map/ppermute | solution.py:328
  22.3 1.5 %collective-permute-start.3 = (bf16[16,6272]{1,0:T(8,128)(2,1)S(1)}, bf16[16,6272]{1,0:T(8,128)(2,1)S(1)}, u32[]{:S(2)}, u32[]{:S(2)}) collective-permute-start(bf16[16,6272]{1,0:T(8,128)(2,1)S(1)} %join.3.refs_0_), channel_id=1, source_target_pairs={{0,4},{4,0},{8,12},{12,8},{1,5},{5,1},{9,13},{13,9},{2,6},{6,2},{1... | collective-permute-start | bytes 602120 | tf_op jit(solution)/shard_map/ppermute | solution.py:328
  22.4 1.7 %collective-permute-start.4 = (bf16[16,6272]{1,0:T(8,128)(2,1)S(1)}, bf16[16,6272]{1,0:T(8,128)(2,1)S(1)}, u32[]{:S(2)}, u32[]{:S(2)}) collective-permute-start(bf16[16,6272]{1,0:T(8,128)(2,1)S(1)} %collective-permute-done.2.refs_1_), channel_id=1, source_target_pairs={{0,4},{4,0},{8,12},{12,8},{1,5},{5,1},{9,13},{13,9},{2,6},{6,2},{1... | collective-permute-start | bytes 602120 | tf_op jit(solution)/shard_map/ppermute | solution.py:328
  39.7 2.8 %collective-permute-start.7 = (bf16[16,3072]{1,0:T(8,128)(2,1)S(1)}, bf16[16,3072]{1,0:T(8,128)(2,1)S(1)}, u32[]{:S(2)}, u32[]{:S(2)}) collective-permute-start(bf16[16,3072]{1,0:T(8,128)(2,1)S(1)} %get-tuple-element.42), channel_id=1, source_target_pairs={{0,4},{4,0},{8,12},{12,8},{1,5},{5,1},{9,13},{13,9},{2,6},{6,2},{1... | collective-permute-start | bytes 294920 | tf_op jit(solution)/shard_map/ppermute | solution.py:328
  40.0 4.1 %collective-permute-start.5 = (bf16[16,3072]{1,0:T(8,128)(2,1)S(1)}, bf16[16,3072]{1,0:T(8,128)(2,1)S(1)}, u32[]{:S(2)}, u32[]{:S(2)}) collective-permute-start(bf16[16,3072]{1,0:T(8,128)(2,1)S(1)} %get-tuple-element.35), channel_id=1, source_target_pairs={{0,4},{4,0},{8,12},{12,8},{1,5},{5,1},{9,13},{13,9},{2,6},{6,2},{1... | collective-permute-start | bytes 294920 | tf_op jit(solution)/shard_map/ppermute | solution.py:328
  41.9 2.3 %collective-permute-start.6 = (bf16[16,3072]{1,0:T(8,128)(2,1)S(1)}, bf16[16,3072]{1,0:T(8,128)(2,1)S(1)}, u32[]{:S(2)}, u32[]{:S(2)}) collective-permute-start(bf16[16,3072]{1,0:T(8,128)(2,1)S(1)} %get-tuple-element.40), channel_id=1, source_target_pairs={{0,4},{4,0},{8,12},{12,8},{1,5},{5,1},{9,13},{13,9},{2,6},{6,2},{1... | collective-permute-start | bytes 294920 | tf_op jit(solution)/shard_map/ppermute | solution.py:328
  42.2 1.3 %collective-permute-start.8 = (bf16[16,3072]{1,0:T(8,128)(2,1)S(1)}, bf16[16,3072]{1,0:T(8,128)(2,1)S(1)}, u32[]{:S(2)}, u32[]{:S(2)}) collective-permute-start(bf16[16,3072]{1,0:T(8,128)(2,1)S(1)} %get-tuple-element.44), channel_id=1, source_target_pairs={{0,4},{4,0},{8,12},{12,8},{1,5},{5,1},{9,13},{13,9},{2,6},{6,2},{1... | collective-permute-start | bytes 294920 | tf_op jit(solution)/shard_map/ppermute | solution.py:328
  43.5 7.2 %collective-permute-start.9 = (bf16[16,6144]{1,0:T(8,128)(2,1)S(1)}, bf16[16,6144]{1,0:T(8,128)(2,1)S(1)}, u32[]{:S(2)}, u32[]{:S(2)}) collective-permute-start(bf16[16,6144]{1,0:T(8,128)(2,1)S(1)} %pad_maximum_fusion), channel_id=1, source_target_pairs={{0,8},{4,12},{8,0},{12,4},{1,9},{5,13},{9,1},{13,5},{2,10},{6,14},... | collective-permute-start | bytes 589832 | tf_op jit(solution)/shard_map/ppermute | solution.py:328
  50.8 4.7 %collective-permute-start.10 = (bf16[8,6144]{1,0:T(8,128)(2,1)S(1)}, bf16[8,6144]{1,0:T(8,128)(2,1)S(1)}, u32[]{:S(2)}, u32[]{:S(2)}) collective-permute-start(bf16[8,6144]{1,0:T(8,128)(2,1)S(1)} %slice.17), channel_id=1, source_target_pairs={{0,1},{1,0},{2,3},{3,2},{4,5},{5,4},{6,7},{7,6},{8,9},{9,8},{10,11... | collective-permute-start | bytes 294920 | tf_op jit(solution)/shard_map/ppermute | solution.py:328
  55.5 5.1 %collective-permute-start.11 = (bf16[4,6144]{1,0:T(4,128)(2,1)S(1)}, bf16[4,6144]{1,0:T(4,128)(2,1)S(1)}, u32[]{:S(2)}, u32[]{:S(2)}) collective-permute-start(bf16[4,6144]{1,0:T(4,128)(2,1)S(1)} %slice.19), channel_id=1, source_target_pairs={{0,2},{1,3},{2,0},{3,1},{4,6},{5,7},{6,4},{7,5},{8,10},{9,11},{10,... | collective-permute-start | bytes 147464 | tf_op jit(solution)/shard_map/ppermute | solution.py:328

commit v5 on v4

--- a/solution.py
+++ b/solution.py
@@ -129,28 +129,33 @@
     return pltpu.VMEM((two, spans(hidden_units)[part][1], width), gate_up.dtype)
 
 
-def ahead_kernel(first, source, target, sems):
-    copies = ahead_parts(source, target, sems, first)
+def bring_kernel(cuts, *refs):
+    n = len(cuts)
+    sources, targets, sems = refs[:n], refs[n : 2 * n], refs[2 * n]
+    copies = [
+        pltpu.make_async_copy(sources[i].at[cut], targets[i], sems.at[i])
+        for i, cut in enumerate(cuts)
+    ]
     for copy in copies:
         copy.start()
     for copy in copies:
         copy.wait()
 
 
-def bring(gate_up, part):
-    shape = ahead_shape(gate_up, part)
+def bring(arrays, cuts, shapes):
+    n = len(arrays)
     return pl.pallas_call(
-        functools.partial(ahead_kernel, spans(gate_up.shape[1])[part][0]),
-        in_specs=[pl.BlockSpec(memory_space=pltpu.HBM)],
-        out_specs=pl.BlockSpec(memory_space=pltpu.VMEM),
-        out_shape=shape,
-        scratch_shapes=[pltpu.SemaphoreType.DMA((2,))],
+        functools.partial(bring_kernel, cuts),
+        in_specs=[pl.BlockSpec(memory_space=pltpu.HBM)] * n,
+        out_specs=[pl.BlockSpec(memory_space=pltpu.VMEM)] * n,
+        out_shape=[pltpu.VMEM(shape, BF16) for shape in shapes],
+        scratch_shapes=[pltpu.SemaphoreType.DMA((n,))],
         cost_estimate=pl.CostEstimate(
-            flops=0, transcendentals=0, bytes_accessed=2 * math.prod(shape.shape)
+            flops=0, transcendentals=0, bytes_accessed=2 * sum(map(math.prod, shapes))
         ),
         compiler_params=pltpu.CompilerParams(vmem_limit_bytes=2**20),
         name="bring",
-    )(in_hbm(gate_up))
+    )(*map(in_hbm, arrays))
 
 
 def attend(tokens, queries, keys, values, lengths, gain, routes, weights, gate_up):
@@ -188,34 +193,24 @@
     )(*map(in_hbm, operands))
 
 
-def weighted_down(turned, down, factors, outs):
-    wide = 768
-    size = outs[0].shape[0]
-    for c in range(down.shape[1] // wide):
-        at = slice(c * wide, (c + 1) * wide)
-        total = jnp.dot(turned, down[:, at], preferred_element_type=F32)
-        for i, out in enumerate(outs):
-            out[:, at] = (total[i * size : (i + 1) * size] * factors[i]).astype(BF16)
-
-
-def expert_kernel(n_pieces, n_parts, *refs):
+def expert_kernel(n_pieces, n_parts, n_ready, *refs):
     expert = lax.axis_index("side").astype(jnp.int32)
-    pieces = refs[:n_pieces]
-    parts = refs[n_pieces : n_pieces + n_parts]
-    down_hbm = refs[n_pieces + n_parts]
-    outs = refs[n_pieces + n_parts + 1 : 2 * n_pieces + n_parts + 1]
-    turned_ref, factor_ref, later = refs[2 * n_pieces + n_parts + 1 : 2 * n_pieces + n_parts + 4]
-    x, down, down_sems = refs[2 * n_pieces + n_parts + 4 :]
+    refs = list(refs)
+
+    def take(n):
+        taken, refs[:n] = refs[:n], []
+        return taken
+
+    pieces, parts, ready, (down_hbm,) = take(n_pieces), take(n_parts), take(n_ready), take(1)
+    outs, loaded, (x, hidden, down_sems) = take(n_pieces), take(4 - n_ready), take(3)
     width = x.shape[1]
-    half = width // 2
-    quarter = half // 2
+    quarters = ready + loaded
+    columns = width // 4
     down_copies = [
         pltpu.make_async_copy(
-            down_hbm.at[:, c * quarter : (c + 1) * quarter],
-            (down, later)[c // 2].at[:, c % 2 * quarter : (c % 2 + 1) * quarter],
-            down_sems.at[c],
+            down_hbm.at[:, c * columns : (c + 1) * columns], quarters[c], down_sems.at[c]
         )
-        for c in range(4)
+        for c in range(n_ready, 4)
     ]
     to_start = list(down_copies)
     to_start.pop(0).start()
@@ -228,11 +223,10 @@
         lane = lax.broadcasted_iota(jnp.int32, meta.shape, 1)
         mine = lane % (LANES // 2) == expert
         factors.append(jnp.sum(jnp.where(mine, meta, 0.0), axis=1, keepdims=True))
-        factor_ref[at] = jnp.broadcast_to(factors[i], (size, LANES))
     first = 0
     for part in parts:
         units = part.shape[1]
-        if to_start and part is not parts[-1]:
+        if part is parts[-1]:
             to_start.pop(0).start()
         gate, up = [
             lax.dot_general(
@@ -240,21 +234,22 @@
             )
             for i in range(2)
         ]
-        turned_ref[:, first : first + units] = (gate / (1.0 + jnp.exp(-gate)) * up).astype(BF16)
+        hidden[:, first : first + units] = (gate / (1.0 + jnp.exp(-gate)) * up).astype(BF16)
         first += units
-    for copy in to_start:
-        copy.start()
-    for copy in down_copies[:2]:
-        copy.wait()
-    weighted_down(turned_ref[...], down, factors, outs)
-    for copy in down_copies[2:]:
-        copy.wait()
-
-
-def later_kernel(n_pieces, turned, factor_ref, down, *outs):
-    size = outs[0].shape[0]
-    factors = [factor_ref[i * size : (i + 1) * size, :1] for i in range(n_pieces)]
-    weighted_down(turned[...], down, factors, outs)
+    for q, quarter in enumerate(quarters):
+        if q >= n_ready:
+            down_copies[q - n_ready].wait()
+            if to_start:
+                to_start.pop(0).start()
+        wide = columns // 2
+        for c in range(2):
+            total = jnp.dot(
+                hidden[...], quarter[:, c * wide : (c + 1) * wide], preferred_element_type=F32
+            )
+            at = slice(q * columns + c * wide, q * columns + (c + 1) * wide)
+            for i, out in enumerate(outs):
+                part = total[i * size : (i + 1) * size] * factors[i]
+                out[:, at] = part.astype(BF16)
 
 
 def join_kernel(*refs):
@@ -275,44 +270,26 @@
     )(*map(in_vmem, pieces))
 
 
-def experts(pieces, parts, down):
-    n_pieces, n_parts = len(pieces), len(parts)
+def experts(pieces, parts, ready, down):
+    n_pieces, n_parts, n_ready = len(pieces), len(parts), len(ready)
     size, width = pieces[0].shape[0], pieces[0].shape[1] - LANES
-    hidden_units, half = down.shape[0], width // 2
+    hidden_units = down.shape[0]
     rows = n_pieces * size
     vmem = pl.BlockSpec(memory_space=pltpu.VMEM)
-    out_shape = [pltpu.VMEM((size, half), BF16)] * n_pieces
-    *first, turned, factor, later = pl.pallas_call(
-        functools.partial(expert_kernel, n_pieces, n_parts),
-        in_specs=[vmem] * (n_pieces + n_parts) + [pl.BlockSpec(memory_space=pltpu.HBM)],
-        out_specs=[vmem] * (n_pieces + 3),
-        out_shape=out_shape
+    return pl.pallas_call(
+        functools.partial(expert_kernel, n_pieces, n_parts, n_ready),
+        in_specs=[vmem] * (n_pieces + n_parts + n_ready) + [pl.BlockSpec(memory_space=pltpu.HBM)],
+        out_specs=[vmem] * n_pieces,
+        out_shape=[pltpu.VMEM((size, width), BF16)] * n_pieces,
+        scratch_shapes=[pltpu.VMEM((hidden_units, width // 4), BF16)] * (4 - n_ready)
         + [
+            pltpu.VMEM((rows, width), BF16),
             pltpu.VMEM((rows, hidden_units), BF16),
-            pltpu.VMEM((rows, LANES), F32),
-            pltpu.VMEM((hidden_units, half), BF16),
-        ],
-        scratch_shapes=[
-            pltpu.VMEM((rows, width), BF16),
-            pltpu.VMEM((hidden_units, half), BF16),
             pltpu.SemaphoreType.DMA((4,)),
         ],
-        compiler_params=pltpu.CompilerParams(vmem_limit_bytes=16 * 2**20),
+        compiler_params=pltpu.CompilerParams(vmem_limit_bytes=20 * 2**20),
         name="experts",
-    )(*map(in_vmem, pieces), *map(in_vmem, parts), in_hbm(down))
-    second = pl.pallas_call(
-        functools.partial(later_kernel, n_pieces),
-        in_specs=[vmem] * 3,
-        out_specs=[vmem] * n_pieces,
-        out_shape=out_shape,
-        cost_estimate=pl.CostEstimate(
-            flops=2 * rows * hidden_units * half, transcendentals=0,
-            bytes_accessed=2 * hidden_units * half,
-        ),
-        compiler_params=pltpu.CompilerParams(vmem_limit_bytes=4 * 2**20),
-        name="later",
-    )(in_vmem(turned), in_vmem(factor), in_vmem(later))
-    return list(first), list(second)
+    )(*map(in_vmem, [*pieces, *parts, *ready]), in_hbm(down))
 
 
 def in_vmem(value):
@@ -352,41 +329,58 @@
         tokens, queries, stored_keys, stored_values, lengths, norm_gain, routes, route_weights,
         gate_up[0],
     )
-    weight_parts = [first_part]
-    waiting = list(range(1, len(spans(gate_up.shape[2]))))
-
-    def beside(values):
+    gate_up, down = gate_up[0], down_proj[0]
+    two, hidden_units, width = gate_up.shape
+    weight_parts, ready = [first_part], []
+    waiting = [
+        ((slice(None), slice(first, first + size)), (two, size, width))
+        for first, size in spans(hidden_units)[1:]
+    ]
+
+    def beside(values, down_quarter=False):
         if not waiting:
             return values
-        brought = bring(gate_up[0], waiting.pop(0))
-        brought, *values = lax.optimization_barrier((brought, *values))
-        weight_parts.append(brought)
+        cut, shape = waiting.pop(0)
+        arrays, cuts, shapes = [gate_up], [cut], [shape]
+        if down_quarter:
+            arrays.append(down)
+            cuts.append((slice(None), slice(0, width // 4)))
+            shapes.append((hidden_units, width // 4))
+        brought = bring(arrays, cuts, shapes)
+        *brought, values = lax.optimization_barrier((*brought, values))
+        weight_parts.append(brought[0])
+        ready.extend(brought[1:])
         return values
 
     tp_steps = strides(lax.axis_size("tp"))
     side_steps = strides(lax.axis_size("side"))
     held = row
-    for stride in tp_steps:
-        held = join([held] + beside([swap(held, "tp", stride)]))
+    for i, stride in enumerate(tp_steps):
+        held = join([held, beside(swap(held, "tp", stride), i == 1)])
     pieces = [held]
     for stride in side_steps:
         pieces = pieces + beside([swap(piece, "side", stride) for piece in pieces])
     while waiting:
-        weight_parts.append(bring(gate_up[0], waiting.pop(0)))
-    halves = experts(pieces, weight_parts, down_proj[0])
-    parts = [
-        jnp.concatenate(both, axis=1)
-        for both in zip(*[exchanged(half, "side", side_steps[-1]) for half in halves])
-    ]
-    for stride in reversed(side_steps[:-1]):
-        parts = exchanged(parts, "side", stride)
-    total = parts[0]
-    for stride in reversed(tp_steps[1:]):
-        half = total.shape[0] // 2
-        total = added(total[:half], swap(total[half:], "tp", stride))
-    rows = resid.shape[0]
-    last = swap(total[rows:], "tp", tp_steps[0])
-    return (resid + total[:rows].astype(F32) + last.astype(F32)).astype(BF16)
+        beside(())
+    parts = experts(pieces, weight_parts, ready, down)
+    for stride in reversed(side_steps):
+        half = len(parts) // 2
+        parts = [added(parts[i], swap(parts[half + i], "side", stride)) for i in range(half)]
+    total = parts[0].astype(F32)
+    while tp_steps:
+        near, tp_steps = tp_steps[-2:], tp_steps[:-2]
+        away = [0]
+        for stride in near:
+            away = away + [stride ^ k for k in away]
+        size = total.shape[0] // len(away)
+        sent = total.astype(BF16)
+        total = total[:size]
+        if not tp_steps:
+            total = resid + total
+        far_first = sorted(range(1, len(away)), key=lambda i: -away[i])
+        for i in far_first:
+            total = total + swap(sent[i * size : (i + 1) * size], "tp", away[i]).astype(F32)
+    return total.astype(BF16)
 
 
 def solution(mesh):

time: 61.4 us -> 58.4 us (0.951)
  waiting for transfers between devices: 14.6 us -> 12.2 us
    ppermute x12 -> x11, waiting for transfers between devices: 14.6 us -> 12.2 us  [swap(): return lax.ppermute(value, axis, [(i, i ^ bits) for i in range(n)])]
    pallas_call x5 -> x4, Pallas kernels: 28 us -> 27.4 us  [the longest x1 15.5 us: experts(): pl.pallas_call(functools.partial(expert_kernel, n_pieces, n_parts, n_read...]
    ppermute x12 -> x11, starting transfers between devices: 13.7 us -> 13.7 us  [swap(): return lax.ppermute(value, axis, [(i, i ^ bits) for i in range(n)])]
  transfers between devices with their start and end apart: 12 -> 11, of which waited for: 7 -> 7; matrix products, arithmetic and copies ran while one was open for 0% -> 0% of each run, Pallas kernels for 20% -> 20%
where the time goes in v5:
time: 58.4 us; the launch traced here: 58.2 us
  Pallas kernels  31.3 us (54%)
  starting transfers between devices  13.7 us (23%)
  waiting for transfers between devices  12.2 us (21%)
  other arithmetic  0.81 us (1%)
    pallas_call x1, Pallas kernels, experts(): pl.pallas_call(functools.partial(expert_kernel, n_pieces, n_parts, n_read...  15.5 us
    ppermute x11, starting transfers between devices, swap(): return lax.ppermute(value, axis, [(i, i ^ bits) for i in range(n)])  13.7 us
    ppermute x11, waiting for transfers between devices, swap(): return lax.ppermute(value, axis, [(i, i ^ bits) for i in range(n)])  12.2 us
    pallas_call x3, Pallas kernels, bring(): pl.pallas_call(functools.partial(bring_kernel, cuts), in_specs=[pl.BlockS...  11.8 us
    pallas_call x1, Pallas kernels, attend(): pl.pallas_call(attend_kernel, in_specs=[pl.BlockSpec(memory_space=pltpu.H...  3.94 us
  transfers between devices with their start and end apart: 11, of which 7 were waited for; matrix products, arithmetic and copies ran while one was open for 0% of the time, Pallas kernels for 20%

profile of v5, /device:TPU:0, one launch (start us, length us, event | category | flops | bytes accessed | tf_op | source)
XLA Modules:
  0.0 58.2 jit_solution(1049220811608994930)
XLA Ops:
  0.0 3.9 %attend.1 = (f32[4,6144]{1,0:T(4,128)S(1)}, bf16[4,6272]{1,0:T(4,128)(2,1)S(1)}, bf16[2,256,6144]{2,1,0:T(8,128)(2,1)S(1)}) custom-call(bf16[4,6144]{1,0:T(4,128)(2,1)} %refs_0_.1, bf16[4,6144]{1,0:T(4,128)(2,1)} %refs_1_.1, f32[1,6144]{1,0:T(1,128)} %bitcast.12, s32[1,4]{1,0:T(1,128)} %bitcast.15, s32[2,4]{1,0:T(2,128)} %bitcast.13, f32[2,4]{1,0:T(2,128)} %bitcast.14, ...), custom_call_target="tpu_custom_call" | custom-call | tf_op jit(solution)/shard_map/attend/pallas_call | solution.py:168
  3.9 4.1 %collective-permute-start = (bf16[4,6272]{1,0:T(4,128)(2,1)S(1)}, bf16[4,6272]{1,0:T(4,128)(2,1)S(1)}, u32[]{:S(2)}, u32[]{:S(2)}) collective-permute-start(bf16[4,6272]{1,0:T(4,128)(2,1)S(1)} %get-tuple-element.22.refs_0_), channel_id=1, source_target_pairs={{0,2},{1,3},{2,0},{3,1},{4,6},{5,7},{6,4},{7,5},{8,10},{9,11},{10,... | collective-permute-start | bytes 150536 | tf_op jit(solution)/shard_map/ppermute | solution.py:305
  8.0 2.8 %bring.3.refs_5_ = bf16[2,256,6144]{2,1,0:T(8,128)(2,1)S(1)} custom-call(bf16[2,1344,6144]{2,1,0:T(8,128)(2,1)} %bitcast.7), custom_call_target="tpu_custom_call" | custom-call | bytes 6291456 | tf_op jit(solution)/shard_map/bring/pallas_call | solution.py:147
  10.9 1.6 %collective-permute-start.1 = (bf16[8,6272]{1,0:T(8,128)(2,1)S(1)}, bf16[8,6272]{1,0:T(8,128)(2,1)S(1)}, u32[]{:S(2)}, u32[]{:S(2)}) collective-permute-start(bf16[8,6272]{1,0:T(8,128)(2,1)S(1)} %join.2.refs_0_), channel_id=1, source_target_pairs={{0,1},{1,0},{2,3},{3,2},{4,5},{5,4},{6,7},{7,6},{8,9},{9,8},{10,11... | collective-permute-start | bytes 301064 | tf_op jit(solution)/shard_map/ppermute | solution.py:305
  12.5 4.0 %bring.4 = (bf16[2,256,6144]{2,1,0:T(8,128)(2,1)S(1)}, bf16[1344,1536]{1,0:T(8,128)(2,1)S(1)}) custom-call(bf16[2,1344,6144]{2,1,0:T(8,128)(2,1)} %bitcast.8, bf16[1344,6144]{1,0:T(8,128)(2,1)} %bitcast.10), custom_call_target="tpu_custom_call" | custom-call | bytes 10420224 | tf_op jit(solution)/shard_map/bring/pallas_call | solution.py:147
  16.6 1.6 %collective-permute-start.2 = (bf16[16,6272]{1,0:T(8,128)(2,1)S(1)}, bf16[16,6272]{1,0:T(8,128)(2,1)S(1)}, u32[]{:S(2)}, u32[]{:S(2)}) collective-permute-start(bf16[16,6272]{1,0:T(8,128)(2,1)S(1)} %join.3.refs_0_), channel_id=1, source_target_pairs={{0,8},{4,12},{8,0},{12,4},{1,9},{5,13},{9,1},{13,5},{2,10},{6,14},... | collective-permute-start | bytes 602120 | tf_op jit(solution)/shard_map/ppermute | solution.py:305
  18.1 5.0 %bring.5.refs_7_ = bf16[2,576,6144]{2,1,0:T(8,128)(2,1)S(1)} custom-call(bf16[2,1344,6144]{2,1,0:T(8,128)(2,1)} %bitcast.9), custom_call_target="tpu_custom_call" | custom-call | bytes 14155776 | tf_op jit(solution)/shard_map/bring/pallas_call | solution.py:147
  23.3 0.5 collective-permute-start.4
  23.8 0.9 %collective-permute-done.3.refs_2_ = bf16[16,6272]{1,0:T(8,128)(2,1)S(1)} collective-permute-done((bf16[16,6272]{1,0:T(8,128)(2,1)S(1)}, bf16[16,6272]{1,0:T(8,128)(2,1)S(1)}, u32[]{:S(2)}, u32[]{:S(2)}) %collective-permute-start.3) | collective-permute-done | bytes 200736 | tf_op jit(solution)/shard_map/ppermute | solution.py:305
  24.7 0.3 collective-permute-done.4.refs_3_
  25.0 15.5 %experts.1 = (bf16[16,6144]{1,0:T(8,128)(2,1)S(1)}, bf16[16,6144]{1,0:T(8,128)(2,1)S(1)}, bf16[16,6144]{1,0:T(8,128)(2,1)S(1)}, bf16[16,6144]{1,0:T(8,128)(2,1)S(1)}) custom-call(bf16[16,6272]{1,0:T(8,128)(2,1)S(1)} %join.3.refs_0_, bf16[16,6272]{1,0:T(8,128)(2,1)S(1)} %collective-permute-done.2.refs_1_, ...), custom_call_target="tpu_custom_call" | custom-call | tf_op jit(solution)/shard_map/experts/pallas_call | solution.py:279
  40.5 0.3 collective-permute-start.6
  40.8 0.3 collective-permute-start.5
  41.1 0.9 %collective-permute-done.6 = bf16[16,6144]{1,0:T(8,128)(2,1)S(1)} collective-permute-done((bf16[16,6144]{1,0:T(8,128)(2,1)S(1)}, bf16[16,6144]{1,0:T(8,128)(2,1)S(1)}, u32[]{:S(2)}, u32[]{:S(2)}) %collective-permute-start.6) | collective-permute-done | bytes 196640 | tf_op jit(solution)/shard_map/ppermute | solution.py:305
  42.1 0.8 %collective-permute-start.7 = (bf16[16,6144]{1,0:T(8,128)(2,1)S(1)}, bf16[16,6144]{1,0:T(8,128)(2,1)S(1)}, u32[]{:S(2)}, u32[]{:S(2)}) collective-permute-start(bf16[16,6144]{1,0:T(8,128)(2,1)S(1)} %add_convert_fusion.1), channel_id=1, source_target_pairs={{0,8},{4,12},{8,0},{12,4},{1,9},{5,13},{9,1},{13,5},{2,10},{6,14},... | collective-permute-start | bytes 589832 | tf_op jit(solution)/shard_map/ppermute | solution.py:305
  42.9 6.3 %collective-permute-done.7 = bf16[16,6144]{1,0:T(8,128)(2,1)S(1)} collective-permute-done((bf16[16,6144]{1,0:T(8,128)(2,1)S(1)}, bf16[16,6144]{1,0:T(8,128)(2,1)S(1)}, u32[]{:S(2)}, u32[]{:S(2)}) %collective-permute-start.7) | collective-permute-done | bytes 196640 | tf_op jit(solution)/shard_map/ppermute | solution.py:305
  49.2 0.1 add_convert_fusion
  49.3 2.7 %collective-permute-start.8 = (bf16[4,6144]{1,0:T(4,128)(2,1)S(1)}, bf16[4,6144]{1,0:T(4,128)(2,1)S(1)}, u32[]{:S(2)}, u32[]{:S(2)}) collective-permute-start(bf16[4,6144]{1,0:T(4,128)(2,1)S(1)} %get-tuple-element.37), channel_id=1, source_target_pairs={{0,3},{1,2},{2,1},{3,0},{4,7},{5,6},{6,5},{7,4},{8,11},{9,10},{10,... | collective-permute-start | bytes 147464 | tf_op jit(solution)/shard_map/ppermute | solution.py:305
  52.1 0.5 collective-permute-start.10
  52.6 1.2 %collective-permute-start.9 = (bf16[4,6144]{1,0:T(4,128)(2,1)S(1)}, bf16[4,6144]{1,0:T(4,128)(2,1)S(1)}, u32[]{:S(2)}, u32[]{:S(2)}) collective-permute-start(bf16[4,6144]{1,0:T(4,128)(2,1)S(1)} %get-tuple-element.39), channel_id=1, source_target_pairs={{0,2},{1,3},{2,0},{3,1},{4,6},{5,7},{6,4},{7,5},{8,10},{9,11},{10,... | collective-permute-start | bytes 147464 | tf_op jit(solution)/shard_map/ppermute | solution.py:305
  53.8 1.5 %collective-permute-done.8 = bf16[4,6144]{1,0:T(4,128)(2,1)S(1)} collective-permute-done((bf16[4,6144]{1,0:T(4,128)(2,1)S(1)}, bf16[4,6144]{1,0:T(4,128)(2,1)S(1)}, u32[]{:S(2)}, u32[]{:S(2)}) %collective-permute-start.8) | collective-permute-done | bytes 49184 | tf_op jit(solution)/shard_map/ppermute | solution.py:305
  55.3 1.0 %collective-permute-done.10 = bf16[4,6144]{1,0:T(4,128)(2,1)S(1)} collective-permute-done((bf16[4,6144]{1,0:T(4,128)(2,1)S(1)}, bf16[4,6144]{1,0:T(4,128)(2,1)S(1)}, u32[]{:S(2)}, u32[]{:S(2)}) %collective-permute-start.10) | collective-permute-done | bytes 49184 | tf_op jit(solution)/shard_map/ppermute | solution.py:305
  56.3 1.2 %collective-permute-done.9 = bf16[4,6144]{1,0:T(4,128)(2,1)S(1)} collective-permute-done((bf16[4,6144]{1,0:T(4,128)(2,1)S(1)}, bf16[4,6144]{1,0:T(4,128)(2,1)S(1)}, u32[]{:S(2)}, u32[]{:S(2)}) %collective-permute-start.9) | collective-permute-done | bytes 49184 | tf_op jit(solution)/shard_map/ppermute | solution.py:305
  57.6 0.7 %add_convert_fusion.3 = bf16[4,6144]{1,0:T(4,128)(2,1)} fusion(bf16[4,6144]{1,0:T(4,128)(2,1)S(1)} %collective-permute-done.10, bf16[4,6144]{1,0:T(4,128)(2,1)S(1)} %collective-permute-done.9, bf16[4,6144]{1,0:T(4,128)(2,1)S(1)} %collective-permute-done.8, f32[4,6144]{1,0:T(4,128)S(1)} %get-tuple-element.21, bf16[16,6144]{1,0:T(8,128)(2,1)S(1)} %add_convert_fusion), kind=kLoop, calls=%fused_computation.3 | loop fusion | flops 221184 | bytes 344064 | tf_op jit(solution)/shard_map/convert_element_type | solution.py:383
  (9 shorter events, 0.2 us)
Async XLA Ops:
  3.9 6.9 %collective-permute-start = (bf16[4,6272]{1,0:T(4,128)(2,1)S(1)}, bf16[4,6272]{1,0:T(4,128)(2,1)S(1)}, u32[]{:S(2)}, u32[]{:S(2)}) collective-permute-start(bf16[4,6272]{1,0:T(4,128)(2,1)S(1)} %get-tuple-element.22.refs_0_), channel_id=1, source_target_pairs={{0,2},{1,3},{2,0},{3,1},{4,6},{5,7},{6,4},{7,5},{8,10},{9,11},{10,... | collective-permute-start | bytes 150536 | tf_op jit(solution)/shard_map/ppermute | solution.py:305
  10.9 5.7 %collective-permute-start.1 = (bf16[8,6272]{1,0:T(8,128)(2,1)S(1)}, bf16[8,6272]{1,0:T(8,128)(2,1)S(1)}, u32[]{:S(2)}, u32[]{:S(2)}) collective-permute-start(bf16[8,6272]{1,0:T(8,128)(2,1)S(1)} %join.2.refs_0_), channel_id=1, source_target_pairs={{0,1},{1,0},{2,3},{3,2},{4,5},{5,4},{6,7},{7,6},{8,9},{9,8},{10,11... | collective-permute-start | bytes 301064 | tf_op jit(solution)/shard_map/ppermute | solution.py:305
  16.6 6.7 %collective-permute-start.2 = (bf16[16,6272]{1,0:T(8,128)(2,1)S(1)}, bf16[16,6272]{1,0:T(8,128)(2,1)S(1)}, u32[]{:S(2)}, u32[]{:S(2)}) collective-permute-start(bf16[16,6272]{1,0:T(8,128)(2,1)S(1)} %join.3.refs_0_), channel_id=1, source_target_pairs={{0,8},{4,12},{8,0},{12,4},{1,9},{5,13},{9,1},{13,5},{2,10},{6,14},... | collective-permute-start | bytes 602120 | tf_op jit(solution)/shard_map/ppermute | solution.py:305
  23.2 1.5 %collective-permute-start.3 = (bf16[16,6272]{1,0:T(8,128)(2,1)S(1)}, bf16[16,6272]{1,0:T(8,128)(2,1)S(1)}, u32[]{:S(2)}, u32[]{:S(2)}) collective-permute-start(bf16[16,6272]{1,0:T(8,128)(2,1)S(1)} %join.3.refs_0_), channel_id=1, source_target_pairs={{0,4},{4,0},{8,12},{12,8},{1,5},{5,1},{9,13},{13,9},{2,6},{6,2},{1... | collective-permute-start | bytes 602120 | tf_op jit(solution)/shard_map/ppermute | solution.py:305
  23.3 1.7 %collective-permute-start.4 = (bf16[16,6272]{1,0:T(8,128)(2,1)S(1)}, bf16[16,6272]{1,0:T(8,128)(2,1)S(1)}, u32[]{:S(2)}, u32[]{:S(2)}) collective-permute-start(bf16[16,6272]{1,0:T(8,128)(2,1)S(1)} %collective-permute-done.2.refs_1_), channel_id=1, source_target_pairs={{0,4},{4,0},{8,12},{12,8},{1,5},{5,1},{9,13},{13,9},{2,6},{6,2},{1... | collective-permute-start | bytes 602120 | tf_op jit(solution)/shard_map/ppermute | solution.py:305
  40.5 1.5 %collective-permute-start.6 = (bf16[16,6144]{1,0:T(8,128)(2,1)S(1)}, bf16[16,6144]{1,0:T(8,128)(2,1)S(1)}, u32[]{:S(2)}, u32[]{:S(2)}) collective-permute-start(bf16[16,6144]{1,0:T(8,128)(2,1)S(1)} %get-tuple-element.36), channel_id=1, source_target_pairs={{0,4},{4,0},{8,12},{12,8},{1,5},{5,1},{9,13},{13,9},{2,6},{6,2},{1... | collective-permute-start | bytes 589832 | tf_op jit(solution)/shard_map/ppermute | solution.py:305
  40.8 2.1 %collective-permute-start.5 = (bf16[16,6144]{1,0:T(8,128)(2,1)S(1)}, bf16[16,6144]{1,0:T(8,128)(2,1)S(1)}, u32[]{:S(2)}, u32[]{:S(2)}) collective-permute-start(bf16[16,6144]{1,0:T(8,128)(2,1)S(1)} %get-tuple-element.34), channel_id=1, source_target_pairs={{0,4},{4,0},{8,12},{12,8},{1,5},{5,1},{9,13},{13,9},{2,6},{6,2},{1... | collective-permute-start | bytes 589832 | tf_op jit(solution)/shard_map/ppermute | solution.py:305
  42.1 7.1 %collective-permute-start.7 = (bf16[16,6144]{1,0:T(8,128)(2,1)S(1)}, bf16[16,6144]{1,0:T(8,128)(2,1)S(1)}, u32[]{:S(2)}, u32[]{:S(2)}) collective-permute-start(bf16[16,6144]{1,0:T(8,128)(2,1)S(1)} %add_convert_fusion.1), channel_id=1, source_target_pairs={{0,8},{4,12},{8,0},{12,4},{1,9},{5,13},{9,1},{13,5},{2,10},{6,14},... | collective-permute-start | bytes 589832 | tf_op jit(solution)/shard_map/ppermute | solution.py:305
  49.3 6.0 %collective-permute-start.8 = (bf16[4,6144]{1,0:T(4,128)(2,1)S(1)}, bf16[4,6144]{1,0:T(4,128)(2,1)S(1)}, u32[]{:S(2)}, u32[]{:S(2)}) collective-permute-start(bf16[4,6144]{1,0:T(4,128)(2,1)S(1)} %get-tuple-element.37), channel_id=1, source_target_pairs={{0,3},{1,2},{2,1},{3,0},{4,7},{5,6},{6,5},{7,4},{8,11},{9,10},{10,... | collective-permute-start | bytes 147464 | tf_op jit(solution)/shard_map/ppermute | solution.py:305
  52.1 4.3 %collective-permute-start.10 = (bf16[4,6144]{1,0:T(4,128)(2,1)S(1)}, bf16[4,6144]{1,0:T(4,128)(2,1)S(1)}, u32[]{:S(2)}, u32[]{:S(2)}) collective-permute-start(bf16[4,6144]{1,0:T(4,128)(2,1)S(1)} %get-tuple-element.38), channel_id=1, source_target_pairs={{0,1},{1,0},{2,3},{3,2},{4,5},{5,4},{6,7},{7,6},{8,9},{9,8},{10,11... | collective-permute-start | bytes 147464 | tf_op jit(solution)/shard_map/ppermute | solution.py:305
  52.6 5.0 %collective-permute-start.9 = (bf16[4,6144]{1,0:T(4,128)(2,1)S(1)}, bf16[4,6144]{1,0:T(4,128)(2,1)S(1)}, u32[]{:S(2)}, u32[]{:S(2)}) collective-permute-start(bf16[4,6144]{1,0:T(4,128)(2,1)S(1)} %get-tuple-element.39), channel_id=1, source_target_pairs={{0,2},{1,3},{2,0},{3,1},{4,6},{5,7},{6,4},{7,5},{8,10},{9,11},{10,... | collective-permute-start | bytes 147464 | tf_op jit(solution)/shard_map/ppermute | solution.py:305

commit v6 on v5

--- a/solution.py
+++ b/solution.py
@@ -10,6 +10,8 @@
 
 HEAD_SIZE = 128
 LANES = 128
+EARLY_BLOCKS = (3, 1)
+BLOCKS = 8
 F32 = jnp.float32
 BF16 = jnp.bfloat16
 
@@ -110,10 +112,9 @@
 
 
 def spans(hidden_units):
-    sizes = [hidden_units]
-    if hidden_units > 1024 and hidden_units % 16 == 0:
-        sizes = [256, 256, 256, hidden_units - 768]
-    return [(sum(sizes[:i]), size) for i, size in enumerate(sizes)]
+    n = 3 if hidden_units > 1024 and hidden_units % 48 == 0 else 1
+    size = hidden_units // n
+    return [(i * size, size) for i in range(n)]
 
 
 def ahead_parts(source, target, sems, first):
@@ -202,18 +203,20 @@
         return taken
 
     pieces, parts, ready, (down_hbm,) = take(n_pieces), take(n_parts), take(n_ready), take(1)
-    outs, loaded, (x, hidden, down_sems) = take(n_pieces), take(4 - n_ready), take(3)
+    outs, (loaded, x, hidden, down_sems) = take(n_pieces), take(4)
     width = x.shape[1]
-    quarters = ready + loaded
-    columns = width // 4
+    wide = width // BLOCKS
+    skip, half = width - loaded.shape[1], loaded.shape[1] // 2
     down_copies = [
         pltpu.make_async_copy(
-            down_hbm.at[:, c * columns : (c + 1) * columns], quarters[c], down_sems.at[c]
+            down_hbm.at[:, skip + c * half : skip + (c + 1) * half],
+            loaded.at[:, c * half : (c + 1) * half],
+            down_sems.at[c],
         )
-        for c in range(n_ready, 4)
-    ]
-    to_start = list(down_copies)
-    to_start.pop(0).start()
+        for c in range(2)
+    ]
+    for copy in down_copies:
+        copy.start()
     size = pieces[0].shape[0]
     factors = []
     for i in range(n_pieces):
@@ -226,8 +229,6 @@
     first = 0
     for part in parts:
         units = part.shape[1]
-        if part is parts[-1]:
-            to_start.pop(0).start()
         gate, up = [
             lax.dot_general(
                 x[...], part[i], (((1,), (1,)), ((), ())), preferred_element_type=F32
@@ -236,20 +237,17 @@
         ]
         hidden[:, first : first + units] = (gate / (1.0 + jnp.exp(-gate)) * up).astype(BF16)
         first += units
-    for q, quarter in enumerate(quarters):
-        if q >= n_ready:
-            down_copies[q - n_ready].wait()
-            if to_start:
-                to_start.pop(0).start()
-        wide = columns // 2
-        for c in range(2):
-            total = jnp.dot(
-                hidden[...], quarter[:, c * wide : (c + 1) * wide], preferred_element_type=F32
-            )
-            at = slice(q * columns + c * wide, q * columns + (c + 1) * wide)
+    first = 0
+    for down in ready + [loaded]:
+        for c in range(down.shape[1] // wide):
+            if down is loaded and c * wide % half == 0:
+                down_copies[c * wide // half].wait()
+            block = down[:, c * wide : (c + 1) * wide]
+            total = jnp.dot(hidden[...], block, preferred_element_type=F32)
             for i, out in enumerate(outs):
                 part = total[i * size : (i + 1) * size] * factors[i]
-                out[:, at] = part.astype(BF16)
+                out[:, first : first + wide] = part.astype(BF16)
+            first += wide
 
 
 def join_kernel(*refs):
@@ -281,11 +279,11 @@
         in_specs=[vmem] * (n_pieces + n_parts + n_ready) + [pl.BlockSpec(memory_space=pltpu.HBM)],
         out_specs=[vmem] * n_pieces,
         out_shape=[pltpu.VMEM((size, width), BF16)] * n_pieces,
-        scratch_shapes=[pltpu.VMEM((hidden_units, width // 4), BF16)] * (4 - n_ready)
-        + [
+        scratch_shapes=[
+            pltpu.VMEM((hidden_units, width - sum(early.shape[1] for early in ready)), BF16),
             pltpu.VMEM((rows, width), BF16),
             pltpu.VMEM((rows, hidden_units), BF16),
-            pltpu.SemaphoreType.DMA((4,)),
+            pltpu.SemaphoreType.DMA((2,)),
         ],
         compiler_params=pltpu.CompilerParams(vmem_limit_bytes=20 * 2**20),
         name="experts",
@@ -332,31 +330,40 @@
     gate_up, down = gate_up[0], down_proj[0]
     two, hidden_units, width = gate_up.shape
     weight_parts, ready = [first_part], []
-    waiting = [
-        ((slice(None), slice(first, first + size)), (two, size, width))
-        for first, size in spans(hidden_units)[1:]
-    ]
-
-    def beside(values, down_quarter=False):
+
+    def gate_part(first, size):
+        return (weight_parts, gate_up, (slice(None), slice(first, first + size)), (two, size, width))
+
+    def down_blocks(first, n):
+        wide = width // BLOCKS
+        cut = (slice(None), slice(first * wide, (first + n) * wide))
+        return (ready, down, cut, (hidden_units, n * wide))
+
+    waiting = []
+    if len(spans(hidden_units)) == 3:
+        second, third = spans(hidden_units)[1:]
+        early, more = EARLY_BLOCKS
+        waiting = [
+            [down_blocks(0, early)],
+            [gate_part(*second)],
+            [gate_part(*third), down_blocks(early, more)],
+        ]
+
+    def beside(values):
         if not waiting:
             return values
-        cut, shape = waiting.pop(0)
-        arrays, cuts, shapes = [gate_up], [cut], [shape]
-        if down_quarter:
-            arrays.append(down)
-            cuts.append((slice(None), slice(0, width // 4)))
-            shapes.append((hidden_units, width // 4))
+        kept, arrays, cuts, shapes = zip(*waiting.pop(0))
         brought = bring(arrays, cuts, shapes)
         *brought, values = lax.optimization_barrier((*brought, values))
-        weight_parts.append(brought[0])
-        ready.extend(brought[1:])
+        for where, part in zip(kept, brought):
+            where.append(part)
         return values
 
     tp_steps = strides(lax.axis_size("tp"))
     side_steps = strides(lax.axis_size("side"))
     held = row
-    for i, stride in enumerate(tp_steps):
-        held = join([held, beside(swap(held, "tp", stride), i == 1)])
+    for stride in tp_steps:
+        held = join([held, beside(swap(held, "tp", stride))])
     pieces = [held]
     for stride in side_steps:
         pieces = pieces + beside([swap(piece, "side", stride) for piece in pieces])

time: 58.4 us -> 57.9 us (level)
    pallas_call x1, Pallas kernels: 15.5 us -> 13.9 us  [experts(): pl.pallas_call(functools.partial(expert_kernel, n_pieces, n_parts, n_read...]
    pallas_call x1, Pallas kernels: 3.94 us -> 4.98 us  [attend(): pl.pallas_call(attend_kernel, in_specs=[pl.BlockSpec(memory_space=pltpu.H...]
  transfers between devices with their start and end apart: 11 -> 11, of which waited for: 7 -> 7; matrix products, arithmetic and copies ran while one was open for 0% -> 0% of each run, Pallas kernels for 20% -> 21%
where the time goes in v6:
time: 57.9 us; the launch traced here: 57.7 us
  Pallas kernels  30.8 us (53%)
  starting transfers between devices  14 us (24%)
  waiting for transfers between devices  11.9 us (21%)
  other arithmetic  0.81 us (1%)
    ppermute x11, starting transfers between devices, swap(): return lax.ppermute(value, axis, [(i, i ^ bits) for i in range(n)])  14 us
    pallas_call x1, Pallas kernels, experts(): pl.pallas_call(functools.partial(expert_kernel, n_pieces, n_parts, n_read...  13.9 us
    ppermute x11, waiting for transfers between devices, swap(): return lax.ppermute(value, axis, [(i, i ^ bits) for i in range(n)])  11.9 us
    pallas_call x3, Pallas kernels, bring(): pl.pallas_call(functools.partial(bring_kernel, cuts), in_specs=[pl.BlockS...  11.9 us
    pallas_call x1, Pallas kernels, attend(): pl.pallas_call(attend_kernel, in_specs=[pl.BlockSpec(memory_space=pltpu.H...  4.98 us
  transfers between devices with their start and end apart: 11, of which 7 were waited for; matrix products, arithmetic and copies ran while one was open for 0% of the time, Pallas kernels for 21%

profile of v6, /device:TPU:0, one launch (start us, length us, event | category | flops | bytes accessed | tf_op | source)
XLA Modules:
  0.0 57.7 jit_solution(366050166593784942)
XLA Ops:
  0.0 5.0 %attend.1 = (f32[4,6144]{1,0:T(4,128)S(1)}, bf16[4,6272]{1,0:T(4,128)(2,1)S(1)}, bf16[2,448,6144]{2,1,0:T(8,128)(2,1)S(1)}) custom-call(bf16[4,6144]{1,0:T(4,128)(2,1)} %refs_0_.1, bf16[4,6144]{1,0:T(4,128)(2,1)} %refs_1_.1, f32[1,6144]{1,0:T(1,128)} %bitcast.12, s32[1,4]{1,0:T(1,128)} %bitcast.15, s32[2,4]{1,0:T(2,128)} %bitcast.13, f32[2,4]{1,0:T(2,128)} %bitcast.14, ...), custom_call_target="tpu_custom_call" | custom-call | tf_op jit(solution)/shard_map/attend/pallas_call | solution.py:169
  5.0 4.1 %collective-permute-start = (bf16[4,6272]{1,0:T(4,128)(2,1)S(1)}, bf16[4,6272]{1,0:T(4,128)(2,1)S(1)}, u32[]{:S(2)}, u32[]{:S(2)}) collective-permute-start(bf16[4,6272]{1,0:T(4,128)(2,1)S(1)} %get-tuple-element.22.refs_0_), channel_id=1, source_target_pairs={{0,2},{1,3},{2,0},{3,1},{4,6},{5,7},{6,4},{7,5},{8,10},{9,11},{10,... | collective-permute-start | bytes 150536 | tf_op jit(solution)/shard_map/ppermute | solution.py:303
  9.1 2.8 %bring.3.refs_7_ = bf16[1344,2304]{1,0:T(8,128)(2,1)S(1)} custom-call(bf16[1344,6144]{1,0:T(8,128)(2,1)} %bitcast.9), custom_call_target="tpu_custom_call" | custom-call | bytes 6193152 | tf_op jit(solution)/shard_map/bring/pallas_call | solution.py:148
  11.9 1.6 %collective-permute-start.1 = (bf16[8,6272]{1,0:T(8,128)(2,1)S(1)}, bf16[8,6272]{1,0:T(8,128)(2,1)S(1)}, u32[]{:S(2)}, u32[]{:S(2)}) collective-permute-start(bf16[8,6272]{1,0:T(8,128)(2,1)S(1)} %join.2.refs_0_), channel_id=1, source_target_pairs={{0,1},{1,0},{2,3},{3,2},{4,5},{5,4},{6,7},{7,6},{8,9},{9,8},{10,11... | collective-permute-start | bytes 301064 | tf_op jit(solution)/shard_map/ppermute | solution.py:303
  13.5 4.4 %bring.4.refs_5_ = bf16[2,448,6144]{2,1,0:T(8,128)(2,1)S(1)} custom-call(bf16[2,1344,6144]{2,1,0:T(8,128)(2,1)} %bitcast.7), custom_call_target="tpu_custom_call" | custom-call | bytes 11010048 | tf_op jit(solution)/shard_map/bring/pallas_call | solution.py:148
  18.0 1.6 %collective-permute-start.2 = (bf16[16,6272]{1,0:T(8,128)(2,1)S(1)}, bf16[16,6272]{1,0:T(8,128)(2,1)S(1)}, u32[]{:S(2)}, u32[]{:S(2)}) collective-permute-start(bf16[16,6272]{1,0:T(8,128)(2,1)S(1)} %join.3.refs_0_), channel_id=1, source_target_pairs={{0,8},{4,12},{8,0},{12,4},{1,9},{5,13},{9,1},{13,5},{2,10},{6,14},... | collective-permute-start | bytes 602120 | tf_op jit(solution)/shard_map/ppermute | solution.py:303
  19.5 4.7 %bring.5 = (bf16[2,448,6144]{2,1,0:T(8,128)(2,1)S(1)}, bf16[1344,768]{1,0:T(8,128)(2,1)S(1)}) custom-call(bf16[2,1344,6144]{2,1,0:T(8,128)(2,1)} %bitcast.8, bf16[1344,6144]{1,0:T(8,128)(2,1)} %bitcast.10), custom_call_target="tpu_custom_call" | custom-call | bytes 13074432 | tf_op jit(solution)/shard_map/bring/pallas_call | solution.py:148
  24.4 0.5 collective-permute-start.4
  24.8 0.9 %collective-permute-done.3.refs_2_ = bf16[16,6272]{1,0:T(8,128)(2,1)S(1)} collective-permute-done((bf16[16,6272]{1,0:T(8,128)(2,1)S(1)}, bf16[16,6272]{1,0:T(8,128)(2,1)S(1)}, u32[]{:S(2)}, u32[]{:S(2)}) %collective-permute-start.3) | collective-permute-done | bytes 200736 | tf_op jit(solution)/shard_map/ppermute | solution.py:303
  25.8 0.3 collective-permute-done.4.refs_3_
  26.1 13.9 %experts.1 = (bf16[16,6144]{1,0:T(8,128)(2,1)S(1)}, bf16[16,6144]{1,0:T(8,128)(2,1)S(1)}, bf16[16,6144]{1,0:T(8,128)(2,1)S(1)}, bf16[16,6144]{1,0:T(8,128)(2,1)S(1)}) custom-call(bf16[16,6272]{1,0:T(8,128)(2,1)S(1)} %join.3.refs_0_, bf16[16,6272]{1,0:T(8,128)(2,1)S(1)} %collective-permute-done.2.refs_1_, ...), custom_call_target="tpu_custom_call" | custom-call | tf_op jit(solution)/shard_map/experts/pallas_call | solution.py:277
  40.0 0.3 collective-permute-start.6
  40.3 0.3 collective-permute-start.5
  40.6 0.9 %collective-permute-done.6 = bf16[16,6144]{1,0:T(8,128)(2,1)S(1)} collective-permute-done((bf16[16,6144]{1,0:T(8,128)(2,1)S(1)}, bf16[16,6144]{1,0:T(8,128)(2,1)S(1)}, u32[]{:S(2)}, u32[]{:S(2)}) %collective-permute-start.6) | collective-permute-done | bytes 196640 | tf_op jit(solution)/shard_map/ppermute | solution.py:303
  41.5 1.2 %collective-permute-start.7 = (bf16[16,6144]{1,0:T(8,128)(2,1)S(1)}, bf16[16,6144]{1,0:T(8,128)(2,1)S(1)}, u32[]{:S(2)}, u32[]{:S(2)}) collective-permute-start(bf16[16,6144]{1,0:T(8,128)(2,1)S(1)} %add_convert_fusion.1), channel_id=1, source_target_pairs={{0,8},{4,12},{8,0},{12,4},{1,9},{5,13},{9,1},{13,5},{2,10},{6,14},... | collective-permute-start | bytes 589832 | tf_op jit(solution)/shard_map/ppermute | solution.py:303
  42.7 6.0 %collective-permute-done.7 = bf16[16,6144]{1,0:T(8,128)(2,1)S(1)} collective-permute-done((bf16[16,6144]{1,0:T(8,128)(2,1)S(1)}, bf16[16,6144]{1,0:T(8,128)(2,1)S(1)}, u32[]{:S(2)}, u32[]{:S(2)}) %collective-permute-start.7) | collective-permute-done | bytes 196640 | tf_op jit(solution)/shard_map/ppermute | solution.py:303
  48.6 0.1 add_convert_fusion
  48.8 2.4 %collective-permute-start.8 = (bf16[4,6144]{1,0:T(4,128)(2,1)S(1)}, bf16[4,6144]{1,0:T(4,128)(2,1)S(1)}, u32[]{:S(2)}, u32[]{:S(2)}) collective-permute-start(bf16[4,6144]{1,0:T(4,128)(2,1)S(1)} %get-tuple-element.37), channel_id=1, source_target_pairs={{0,3},{1,2},{2,1},{3,0},{4,7},{5,6},{6,5},{7,4},{8,11},{9,10},{10,... | collective-permute-start | bytes 147464 | tf_op jit(solution)/shard_map/ppermute | solution.py:303
  51.2 0.9 %collective-permute-start.10 = (bf16[4,6144]{1,0:T(4,128)(2,1)S(1)}, bf16[4,6144]{1,0:T(4,128)(2,1)S(1)}, u32[]{:S(2)}, u32[]{:S(2)}) collective-permute-start(bf16[4,6144]{1,0:T(4,128)(2,1)S(1)} %get-tuple-element.38), channel_id=1, source_target_pairs={{0,1},{1,0},{2,3},{3,2},{4,5},{5,4},{6,7},{7,6},{8,9},{9,8},{10,11... | collective-permute-start | bytes 147464 | tf_op jit(solution)/shard_map/ppermute | solution.py:303
  52.1 1.2 %collective-permute-start.9 = (bf16[4,6144]{1,0:T(4,128)(2,1)S(1)}, bf16[4,6144]{1,0:T(4,128)(2,1)S(1)}, u32[]{:S(2)}, u32[]{:S(2)}) collective-permute-start(bf16[4,6144]{1,0:T(4,128)(2,1)S(1)} %get-tuple-element.39), channel_id=1, source_target_pairs={{0,2},{1,3},{2,0},{3,1},{4,6},{5,7},{6,4},{7,5},{8,10},{9,11},{10,... | collective-permute-start | bytes 147464 | tf_op jit(solution)/shard_map/ppermute | solution.py:303
  53.2 1.5 %collective-permute-done.8 = bf16[4,6144]{1,0:T(4,128)(2,1)S(1)} collective-permute-done((bf16[4,6144]{1,0:T(4,128)(2,1)S(1)}, bf16[4,6144]{1,0:T(4,128)(2,1)S(1)}, u32[]{:S(2)}, u32[]{:S(2)}) %collective-permute-start.8) | collective-permute-done | bytes 49184 | tf_op jit(solution)/shard_map/ppermute | solution.py:303
  54.8 1.0 %collective-permute-done.10 = bf16[4,6144]{1,0:T(4,128)(2,1)S(1)} collective-permute-done((bf16[4,6144]{1,0:T(4,128)(2,1)S(1)}, bf16[4,6144]{1,0:T(4,128)(2,1)S(1)}, u32[]{:S(2)}, u32[]{:S(2)}) %collective-permute-start.10) | collective-permute-done | bytes 49184 | tf_op jit(solution)/shard_map/ppermute | solution.py:303
  55.8 1.2 %collective-permute-done.9 = bf16[4,6144]{1,0:T(4,128)(2,1)S(1)} collective-permute-done((bf16[4,6144]{1,0:T(4,128)(2,1)S(1)}, bf16[4,6144]{1,0:T(4,128)(2,1)S(1)}, u32[]{:S(2)}, u32[]{:S(2)}) %collective-permute-start.9) | collective-permute-done | bytes 49184 | tf_op jit(solution)/shard_map/ppermute | solution.py:303
  57.0 0.7 %add_convert_fusion.3 = bf16[4,6144]{1,0:T(4,128)(2,1)} fusion(bf16[4,6144]{1,0:T(4,128)(2,1)S(1)} %collective-permute-done.10, bf16[4,6144]{1,0:T(4,128)(2,1)S(1)} %collective-permute-done.9, bf16[4,6144]{1,0:T(4,128)(2,1)S(1)} %collective-permute-done.8, f32[4,6144]{1,0:T(4,128)S(1)} %get-tuple-element.21, bf16[16,6144]{1,0:T(8,128)(2,1)S(1)} %add_convert_fusion), kind=kLoop, calls=%fused_computation.3 | loop fusion | flops 221184 | bytes 344064 | tf_op jit(solution)/shard_map/convert_element_type | solution.py:390
  (9 shorter events, 0.2 us)
Async XLA Ops:
  5.0 6.9 %collective-permute-start = (bf16[4,6272]{1,0:T(4,128)(2,1)S(1)}, bf16[4,6272]{1,0:T(4,128)(2,1)S(1)}, u32[]{:S(2)}, u32[]{:S(2)}) collective-permute-start(bf16[4,6272]{1,0:T(4,128)(2,1)S(1)} %get-tuple-element.22.refs_0_), channel_id=1, source_target_pairs={{0,2},{1,3},{2,0},{3,1},{4,6},{5,7},{6,4},{7,5},{8,10},{9,11},{10,... | collective-permute-start | bytes 150536 | tf_op jit(solution)/shard_map/ppermute | solution.py:303
  11.9 6.0 %collective-permute-start.1 = (bf16[8,6272]{1,0:T(8,128)(2,1)S(1)}, bf16[8,6272]{1,0:T(8,128)(2,1)S(1)}, u32[]{:S(2)}, u32[]{:S(2)}) collective-permute-start(bf16[8,6272]{1,0:T(8,128)(2,1)S(1)} %join.2.refs_0_), channel_id=1, source_target_pairs={{0,1},{1,0},{2,3},{3,2},{4,5},{5,4},{6,7},{7,6},{8,9},{9,8},{10,11... | collective-permute-start | bytes 301064 | tf_op jit(solution)/shard_map/ppermute | solution.py:303
  18.0 6.4 %collective-permute-start.2 = (bf16[16,6272]{1,0:T(8,128)(2,1)S(1)}, bf16[16,6272]{1,0:T(8,128)(2,1)S(1)}, u32[]{:S(2)}, u32[]{:S(2)}) collective-permute-start(bf16[16,6272]{1,0:T(8,128)(2,1)S(1)} %join.3.refs_0_), channel_id=1, source_target_pairs={{0,8},{4,12},{8,0},{12,4},{1,9},{5,13},{9,1},{13,5},{2,10},{6,14},... | collective-permute-start | bytes 602120 | tf_op jit(solution)/shard_map/ppermute | solution.py:303
  24.3 1.5 %collective-permute-start.3 = (bf16[16,6272]{1,0:T(8,128)(2,1)S(1)}, bf16[16,6272]{1,0:T(8,128)(2,1)S(1)}, u32[]{:S(2)}, u32[]{:S(2)}) collective-permute-start(bf16[16,6272]{1,0:T(8,128)(2,1)S(1)} %join.3.refs_0_), channel_id=1, source_target_pairs={{0,4},{4,0},{8,12},{12,8},{1,5},{5,1},{9,13},{13,9},{2,6},{6,2},{1... | collective-permute-start | bytes 602120 | tf_op jit(solution)/shard_map/ppermute | solution.py:303
  24.4 1.7 %collective-permute-start.4 = (bf16[16,6272]{1,0:T(8,128)(2,1)S(1)}, bf16[16,6272]{1,0:T(8,128)(2,1)S(1)}, u32[]{:S(2)}, u32[]{:S(2)}) collective-permute-start(bf16[16,6272]{1,0:T(8,128)(2,1)S(1)} %collective-permute-done.2.refs_1_), channel_id=1, source_target_pairs={{0,4},{4,0},{8,12},{12,8},{1,5},{5,1},{9,13},{13,9},{2,6},{6,2},{1... | collective-permute-start | bytes 602120 | tf_op jit(solution)/shard_map/ppermute | solution.py:303
  40.0 1.5 %collective-permute-start.6 = (bf16[16,6144]{1,0:T(8,128)(2,1)S(1)}, bf16[16,6144]{1,0:T(8,128)(2,1)S(1)}, u32[]{:S(2)}, u32[]{:S(2)}) collective-permute-start(bf16[16,6144]{1,0:T(8,128)(2,1)S(1)} %get-tuple-element.36), channel_id=1, source_target_pairs={{0,4},{4,0},{8,12},{12,8},{1,5},{5,1},{9,13},{13,9},{2,6},{6,2},{1... | collective-permute-start | bytes 589832 | tf_op jit(solution)/shard_map/ppermute | solution.py:303
  40.3 2.4 %collective-permute-start.5 = (bf16[16,6144]{1,0:T(8,128)(2,1)S(1)}, bf16[16,6144]{1,0:T(8,128)(2,1)S(1)}, u32[]{:S(2)}, u32[]{:S(2)}) collective-permute-start(bf16[16,6144]{1,0:T(8,128)(2,1)S(1)} %get-tuple-element.34), channel_id=1, source_target_pairs={{0,4},{4,0},{8,12},{12,8},{1,5},{5,1},{9,13},{13,9},{2,6},{6,2},{1... | collective-permute-start | bytes 589832 | tf_op jit(solution)/shard_map/ppermute | solution.py:303
  41.5 7.1 %collective-permute-start.7 = (bf16[16,6144]{1,0:T(8,128)(2,1)S(1)}, bf16[16,6144]{1,0:T(8,128)(2,1)S(1)}, u32[]{:S(2)}, u32[]{:S(2)}) collective-permute-start(bf16[16,6144]{1,0:T(8,128)(2,1)S(1)} %add_convert_fusion.1), channel_id=1, source_target_pairs={{0,8},{4,12},{8,0},{12,4},{1,9},{5,13},{9,1},{13,5},{2,10},{6,14},... | collective-permute-start | bytes 589832 | tf_op jit(solution)/shard_map/ppermute | solution.py:303
  48.8 6.0 %collective-permute-start.8 = (bf16[4,6144]{1,0:T(4,128)(2,1)S(1)}, bf16[4,6144]{1,0:T(4,128)(2,1)S(1)}, u32[]{:S(2)}, u32[]{:S(2)}) collective-permute-start(bf16[4,6144]{1,0:T(4,128)(2,1)S(1)} %get-tuple-element.37), channel_id=1, source_target_pairs={{0,3},{1,2},{2,1},{3,0},{4,7},{5,6},{6,5},{7,4},{8,11},{9,10},{10,... | collective-permute-start | bytes 147464 | tf_op jit(solution)/shard_map/ppermute | solution.py:303
  51.2 4.6 %collective-permute-start.10 = (bf16[4,6144]{1,0:T(4,128)(2,1)S(1)}, bf16[4,6144]{1,0:T(4,128)(2,1)S(1)}, u32[]{:S(2)}, u32[]{:S(2)}) collective-permute-start(bf16[4,6144]{1,0:T(4,128)(2,1)S(1)} %get-tuple-element.38), channel_id=1, source_target_pairs={{0,1},{1,0},{2,3},{3,2},{4,5},{5,4},{6,7},{7,6},{8,9},{9,8},{10,11... | collective-permute-start | bytes 147464 | tf_op jit(solution)/shard_map/ppermute | solution.py:303
  52.1 5.0 %collective-permute-start.9 = (bf16[4,6144]{1,0:T(4,128)(2,1)S(1)}, bf16[4,6144]{1,0:T(4,128)(2,1)S(1)}, u32[]{:S(2)}, u32[]{:S(2)}) collective-permute-start(bf16[4,6144]{1,0:T(4,128)(2,1)S(1)} %get-tuple-element.39), channel_id=1, source_target_pairs={{0,2},{1,3},{2,0},{3,1},{4,6},{5,7},{6,4},{7,5},{8,10},{9,11},{10,... | collective-permute-start | bytes 147464 | tf_op jit(solution)/shard_map/ppermute | solution.py:303

commit v7 on v6

--- a/solution.py
+++ b/solution.py
@@ -206,16 +206,17 @@
     outs, (loaded, x, hidden, down_sems) = take(n_pieces), take(4)
     width = x.shape[1]
     wide = width // BLOCKS
-    skip, half = width - loaded.shape[1], loaded.shape[1] // 2
+    skip = width - loaded.shape[1]
     down_copies = [
         pltpu.make_async_copy(
-            down_hbm.at[:, skip + c * half : skip + (c + 1) * half],
-            loaded.at[:, c * half : (c + 1) * half],
+            down_hbm.at[:, skip + c * wide : skip + (c + 1) * wide],
+            loaded.at[:, c * wide : (c + 1) * wide],
             down_sems.at[c],
         )
-        for c in range(2)
-    ]
-    for copy in down_copies:
+        for c in range(loaded.shape[1] // wide)
+    ]
+    at_head = len(down_copies) // 2
+    for copy in down_copies[:at_head]:
         copy.start()
     size = pieces[0].shape[0]
     factors = []
@@ -237,11 +238,14 @@
         ]
         hidden[:, first : first + units] = (gate / (1.0 + jnp.exp(-gate)) * up).astype(BF16)
         first += units
+        if part is parts[0]:
+            for copy in down_copies[at_head:]:
+                copy.start()
     first = 0
     for down in ready + [loaded]:
         for c in range(down.shape[1] // wide):
-            if down is loaded and c * wide % half == 0:
-                down_copies[c * wide // half].wait()
+            if down is loaded:
+                down_copies[c].wait()
             block = down[:, c * wide : (c + 1) * wide]
             total = jnp.dot(hidden[...], block, preferred_element_type=F32)
             for i, out in enumerate(outs):
@@ -283,7 +287,7 @@
             pltpu.VMEM((hidden_units, width - sum(early.shape[1] for early in ready)), BF16),
             pltpu.VMEM((rows, width), BF16),
             pltpu.VMEM((rows, hidden_units), BF16),
-            pltpu.SemaphoreType.DMA((2,)),
+            pltpu.SemaphoreType.DMA((BLOCKS,)),
         ],
         compiler_params=pltpu.CompilerParams(vmem_limit_bytes=20 * 2**20),
         name="experts",
@@ -370,23 +374,30 @@
     while waiting:
         beside(())
     parts = experts(pieces, weight_parts, ready, down)
-    for stride in reversed(side_steps):
+    for stride in reversed(side_steps[1:]):
         half = len(parts) // 2
         parts = [added(parts[i], swap(parts[half + i], "side", stride)) for i in range(half)]
-    total = parts[0].astype(F32)
+    blocks = 4 if len(tp_steps) > 1 else 2
+    near, far = [part.reshape(blocks, part.shape[0] // blocks, width) for part in parts]
+    moving = added(near[1:], swap(far[1:], "side", side_steps[0]))
+    moving, staying = lax.optimization_barrier((moving, far[0]))
+    sent = [None] + [moving[i] for i in range(blocks - 1)]
+    total = near[0].astype(F32) + swap(staying, "side", side_steps[0]).astype(F32)
     while tp_steps:
-        near, tp_steps = tp_steps[-2:], tp_steps[:-2]
+        steps, tp_steps = tp_steps[-2:], tp_steps[:-2]
         away = [0]
-        for stride in near:
+        for stride in steps:
             away = away + [stride ^ k for k in away]
-        size = total.shape[0] // len(away)
-        sent = total.astype(BF16)
-        total = total[:size]
+        if sent is None:
+            size = total.shape[0] // len(away)
+            whole = total.astype(BF16)
+            sent = [whole[i * size : (i + 1) * size] for i in range(len(away))]
+            total = total[:size]
         if not tp_steps:
             total = resid + total
-        far_first = sorted(range(1, len(away)), key=lambda i: -away[i])
-        for i in far_first:
-            total = total + swap(sent[i * size : (i + 1) * size], "tp", away[i]).astype(F32)
+        for i in sorted(range(1, len(away)), key=lambda i: -away[i]):
+            total = total + swap(sent[i], "tp", away[i]).astype(F32)
+        sent = None
     return total.astype(BF16)
 
 

time: 57.9 us -> 57.4 us (level)
  waiting for transfers between devices: 11.9 us -> 10.2 us
  starting transfers between devices: 14 us -> 15.1 us
    ppermute x11 -> x12, waiting for transfers between devices: 11.9 us -> 10.2 us  [swap(): return lax.ppermute(value, axis, [(i, i ^ bits) for i in range(n)])]
    ppermute x11 -> x12, starting transfers between devices: 14 us -> 15.1 us  [swap(): return lax.ppermute(value, axis, [(i, i ^ bits) for i in range(n)])]
  transfers between devices with their start and end apart: 11 -> 12, of which waited for: 7 -> 6; matrix products, arithmetic and copies ran while one was open for 0% -> 1% of each run, Pallas kernels for 21% -> 21%
where the time goes in v7:
time: 57.4 us; the launch traced here: 57.2 us
  Pallas kernels  30.6 us (53%)
  starting transfers between devices  15.1 us (26%)
  waiting for transfers between devices  10.2 us (18%)
  other arithmetic  0.92 us (2%)
    ppermute x12, starting transfers between devices, swap(): return lax.ppermute(value, axis, [(i, i ^ bits) for i in range(n)])  15.1 us
    pallas_call x1, Pallas kernels, experts(): pl.pallas_call(functools.partial(expert_kernel, n_pieces, n_parts, n_read...  13.7 us
    pallas_call x3, Pallas kernels, bring(): pl.pallas_call(functools.partial(bring_kernel, cuts), in_specs=[pl.BlockS...  11.9 us
    ppermute x12, waiting for transfers between devices, swap(): return lax.ppermute(value, axis, [(i, i ^ bits) for i in range(n)])  10.2 us
    pallas_call x1, Pallas kernels, attend(): pl.pallas_call(attend_kernel, in_specs=[pl.BlockSpec(memory_space=pltpu.H...  4.98 us
  transfers between devices with their start and end apart: 12, of which 6 were waited for; matrix products, arithmetic and copies ran while one was open for 1% of the time, Pallas kernels for 21%

profile of v7, /device:TPU:0, one launch (start us, length us, event | category | flops | bytes accessed | tf_op | source)
XLA Modules:
  0.0 57.2 jit_solution(1834388475171501236)
XLA Ops:
  0.0 5.0 %attend.1 = (f32[4,6144]{1,0:T(4,128)S(1)}, bf16[4,6272]{1,0:T(4,128)(2,1)S(1)}, bf16[2,448,6144]{2,1,0:T(8,128)(2,1)S(1)}) custom-call(bf16[4,6144]{1,0:T(4,128)(2,1)} %refs_0_.1, bf16[4,6144]{1,0:T(4,128)(2,1)} %refs_1_.1, f32[1,6144]{1,0:T(1,128)} %bitcast.18, s32[1,4]{1,0:T(1,128)} %bitcast.21, s32[2,4]{1,0:T(2,128)} %bitcast.19, f32[2,4]{1,0:T(2,128)} %bitcast.20, ...), custom_call_target="tpu_custom_call" | custom-call | tf_op jit(solution)/shard_map/attend/pallas_call | solution.py:169
  5.0 4.1 %collective-permute-start = (bf16[4,6272]{1,0:T(4,128)(2,1)S(1)}, bf16[4,6272]{1,0:T(4,128)(2,1)S(1)}, u32[]{:S(2)}, u32[]{:S(2)}) collective-permute-start(bf16[4,6272]{1,0:T(4,128)(2,1)S(1)} %get-tuple-element.24.refs_0_), channel_id=1, source_target_pairs={{0,2},{1,3},{2,0},{3,1},{4,6},{5,7},{6,4},{7,5},{8,10},{9,11},{10,... | collective-permute-start | bytes 150536 | tf_op jit(solution)/shard_map/ppermute | solution.py:307
  9.1 2.8 %bring.3.refs_7_ = bf16[1344,2304]{1,0:T(8,128)(2,1)S(1)} custom-call(bf16[1344,6144]{1,0:T(8,128)(2,1)} %bitcast.15), custom_call_target="tpu_custom_call" | custom-call | bytes 6193152 | tf_op jit(solution)/shard_map/bring/pallas_call | solution.py:148
  11.9 1.6 %collective-permute-start.1 = (bf16[8,6272]{1,0:T(8,128)(2,1)S(1)}, bf16[8,6272]{1,0:T(8,128)(2,1)S(1)}, u32[]{:S(2)}, u32[]{:S(2)}) collective-permute-start(bf16[8,6272]{1,0:T(8,128)(2,1)S(1)} %join.2.refs_0_), channel_id=1, source_target_pairs={{0,1},{1,0},{2,3},{3,2},{4,5},{5,4},{6,7},{7,6},{8,9},{9,8},{10,11... | collective-permute-start | bytes 301064 | tf_op jit(solution)/shard_map/ppermute | solution.py:307
  13.5 4.4 %bring.4.refs_5_ = bf16[2,448,6144]{2,1,0:T(8,128)(2,1)S(1)} custom-call(bf16[2,1344,6144]{2,1,0:T(8,128)(2,1)} %bitcast.13), custom_call_target="tpu_custom_call" | custom-call | bytes 11010048 | tf_op jit(solution)/shard_map/bring/pallas_call | solution.py:148
  18.0 1.6 %collective-permute-start.2 = (bf16[16,6272]{1,0:T(8,128)(2,1)S(1)}, bf16[16,6272]{1,0:T(8,128)(2,1)S(1)}, u32[]{:S(2)}, u32[]{:S(2)}) collective-permute-start(bf16[16,6272]{1,0:T(8,128)(2,1)S(1)} %join.3.refs_0_), channel_id=1, source_target_pairs={{0,8},{4,12},{8,0},{12,4},{1,9},{5,13},{9,1},{13,5},{2,10},{6,14},... | collective-permute-start | bytes 602120 | tf_op jit(solution)/shard_map/ppermute | solution.py:307
  19.5 4.7 %bring.5 = (bf16[2,448,6144]{2,1,0:T(8,128)(2,1)S(1)}, bf16[1344,768]{1,0:T(8,128)(2,1)S(1)}) custom-call(bf16[2,1344,6144]{2,1,0:T(8,128)(2,1)} %bitcast.14, bf16[1344,6144]{1,0:T(8,128)(2,1)} %bitcast.16), custom_call_target="tpu_custom_call" | custom-call | bytes 13074432 | tf_op jit(solution)/shard_map/bring/pallas_call | solution.py:148
  24.4 0.5 collective-permute-start.4
  24.8 0.9 %collective-permute-done.3.refs_2_ = bf16[16,6272]{1,0:T(8,128)(2,1)S(1)} collective-permute-done((bf16[16,6272]{1,0:T(8,128)(2,1)S(1)}, bf16[16,6272]{1,0:T(8,128)(2,1)S(1)}, u32[]{:S(2)}, u32[]{:S(2)}) %collective-permute-start.3) | collective-permute-done | bytes 200736 | tf_op jit(solution)/shard_map/ppermute | solution.py:307
  25.8 0.3 collective-permute-done.4.refs_3_
  26.1 13.7 %experts.1 = (bf16[16,6144]{1,0:T(8,128)(2,1)S(1)}, bf16[16,6144]{1,0:T(8,128)(2,1)S(1)}, bf16[16,6144]{1,0:T(8,128)(2,1)S(1)}, bf16[16,6144]{1,0:T(8,128)(2,1)S(1)}) custom-call(bf16[16,6272]{1,0:T(8,128)(2,1)S(1)} %join.3.refs_0_, bf16[16,6272]{1,0:T(8,128)(2,1)S(1)} %collective-permute-done.2.refs_1_, ...), custom_call_target="tpu_custom_call" | custom-call | tf_op jit(solution)/shard_map/experts/pallas_call | solution.py:281
  39.8 0.3 collective-permute-start.6
  40.1 0.3 collective-permute-start.5
  40.4 0.9 %collective-permute-done.6 = bf16[16,6144]{1,0:T(8,128)(2,1)S(1)} collective-permute-done((bf16[16,6144]{1,0:T(8,128)(2,1)S(1)}, bf16[16,6144]{1,0:T(8,128)(2,1)S(1)}, u32[]{:S(2)}, u32[]{:S(2)}) %collective-permute-start.6) | collective-permute-done | bytes 196640 | tf_op jit(solution)/shard_map/ppermute | solution.py:307
  41.5 1.1 %collective-permute-start.7 = (bf16[3,4,6144]{2,1,0:T(4,128)(2,1)S(1)}, bf16[3,4,6144]{2,1,0:T(4,128)(2,1)S(1)}, u32[]{:S(2)}, u32[]{:S(2)}) collective-permute-start(bf16[3,4,6144]{2,1,0:T(4,128)(2,1)S(1)} %slice.30), channel_id=1, source_target_pairs={{0,8},{4,12},{8,0},{12,4},{1,9},{5,13},{9,1},{13,5},{2,10},{6,14},... | collective-permute-start | bytes 442376 | tf_op jit(solution)/shard_map/ppermute | solution.py:307
  42.8 0.1 reshape.18
  42.9 4.7 %collective-permute-done.7 = bf16[3,4,6144]{2,1,0:T(4,128)(2,1)S(1)} collective-permute-done((bf16[3,4,6144]{2,1,0:T(4,128)(2,1)S(1)}, bf16[3,4,6144]{2,1,0:T(4,128)(2,1)S(1)}, u32[]{:S(2)}, u32[]{:S(2)}) %collective-permute-start.7) | collective-permute-done | bytes 147488 | tf_op jit(solution)/shard_map/ppermute | solution.py:307
  47.6 1.1 %collective-permute-start.8 = (bf16[4,6144]{1,0:T(4,128)(2,1)S(1)}, bf16[4,6144]{1,0:T(4,128)(2,1)S(1)}, u32[]{:S(2)}, u32[]{:S(2)}) collective-permute-start(bf16[4,6144]{1,0:T(4,128)(2,1)S(1)} %slice.38), channel_id=1, source_target_pairs={{0,8},{4,12},{8,0},{12,4},{1,9},{5,13},{9,1},{13,5},{2,10},{6,14},... | collective-permute-start | bytes 147464 | tf_op jit(solution)/shard_map/ppermute | solution.py:307
  48.7 1.9 %collective-permute-start.9 = (bf16[4,6144]{1,0:T(4,128)(2,1)S(1)}, bf16[4,6144]{1,0:T(4,128)(2,1)S(1)}, u32[]{:S(2)}, u32[]{:S(2)}) collective-permute-start(bf16[4,6144]{1,0:T(4,128)(2,1)S(1)} %get-tuple-element.41), channel_id=1, source_target_pairs={{0,3},{1,2},{2,1},{3,0},{4,7},{5,6},{6,5},{7,4},{8,11},{9,10},{10,... | collective-permute-start | bytes 147464 | tf_op jit(solution)/shard_map/ppermute | solution.py:307
  50.7 0.9 %collective-permute-start.11 = (bf16[4,6144]{1,0:T(4,128)(2,1)S(1)}, bf16[4,6144]{1,0:T(4,128)(2,1)S(1)}, u32[]{:S(2)}, u32[]{:S(2)}) collective-permute-start(bf16[4,6144]{1,0:T(4,128)(2,1)S(1)} %get-tuple-element.42), channel_id=1, source_target_pairs={{0,1},{1,0},{2,3},{3,2},{4,5},{5,4},{6,7},{7,6},{8,9},{9,8},{10,11... | collective-permute-start | bytes 147464 | tf_op jit(solution)/shard_map/ppermute | solution.py:307
  51.5 1.6 %collective-permute-start.10 = (bf16[4,6144]{1,0:T(4,128)(2,1)S(1)}, bf16[4,6144]{1,0:T(4,128)(2,1)S(1)}, u32[]{:S(2)}, u32[]{:S(2)}) collective-permute-start(bf16[4,6144]{1,0:T(4,128)(2,1)S(1)} %get-tuple-element.43), channel_id=1, source_target_pairs={{0,2},{1,3},{2,0},{3,1},{4,6},{5,7},{6,4},{7,5},{8,10},{9,11},{10,... | collective-permute-start | bytes 147464 | tf_op jit(solution)/shard_map/ppermute | solution.py:307
  53.2 2.0 %collective-permute-done.9 = bf16[4,6144]{1,0:T(4,128)(2,1)S(1)} collective-permute-done((bf16[4,6144]{1,0:T(4,128)(2,1)S(1)}, bf16[4,6144]{1,0:T(4,128)(2,1)S(1)}, u32[]{:S(2)}, u32[]{:S(2)}) %collective-permute-start.9) | collective-permute-done | bytes 49184 | tf_op jit(solution)/shard_map/ppermute | solution.py:307
  55.2 1.3 %collective-permute-done.10 = bf16[4,6144]{1,0:T(4,128)(2,1)S(1)} collective-permute-done((bf16[4,6144]{1,0:T(4,128)(2,1)S(1)}, bf16[4,6144]{1,0:T(4,128)(2,1)S(1)}, u32[]{:S(2)}, u32[]{:S(2)}) %collective-permute-start.10) | collective-permute-done | bytes 49184 | tf_op jit(solution)/shard_map/ppermute | solution.py:307
  56.5 0.7 %add_convert_fusion.3 = bf16[4,6144]{1,0:T(4,128)(2,1)} fusion(bf16[4,6144]{1,0:T(4,128)(2,1)S(1)} %collective-permute-done.11, bf16[4,6144]{1,0:T(4,128)(2,1)S(1)} %collective-permute-done.10, bf16[4,6144]{1,0:T(4,128)(2,1)S(1)} %collective-permute-done.9, f32[4,6144]{1,0:T(4,128)S(1)} %get-tuple-element.23, bf16[4,6144]{1,0:T(4,128)(2,1)S(1)} %collective-permute-done.8, ...), kind=kLoop, calls=%fused_computation.4 | loop fusion | flops 270336 | bytes 393216 | tf_op jit(solution)/shard_map/convert_element_type | solution.py:401
  (17 shorter events, 0.5 us)
Async XLA Ops:
  5.0 6.9 %collective-permute-start = (bf16[4,6272]{1,0:T(4,128)(2,1)S(1)}, bf16[4,6272]{1,0:T(4,128)(2,1)S(1)}, u32[]{:S(2)}, u32[]{:S(2)}) collective-permute-start(bf16[4,6272]{1,0:T(4,128)(2,1)S(1)} %get-tuple-element.24.refs_0_), channel_id=1, source_target_pairs={{0,2},{1,3},{2,0},{3,1},{4,6},{5,7},{6,4},{7,5},{8,10},{9,11},{10,... | collective-permute-start | bytes 150536 | tf_op jit(solution)/shard_map/ppermute | solution.py:307
  11.9 6.0 %collective-permute-start.1 = (bf16[8,6272]{1,0:T(8,128)(2,1)S(1)}, bf16[8,6272]{1,0:T(8,128)(2,1)S(1)}, u32[]{:S(2)}, u32[]{:S(2)}) collective-permute-start(bf16[8,6272]{1,0:T(8,128)(2,1)S(1)} %join.2.refs_0_), channel_id=1, source_target_pairs={{0,1},{1,0},{2,3},{3,2},{4,5},{5,4},{6,7},{7,6},{8,9},{9,8},{10,11... | collective-permute-start | bytes 301064 | tf_op jit(solution)/shard_map/ppermute | solution.py:307
  18.0 6.4 %collective-permute-start.2 = (bf16[16,6272]{1,0:T(8,128)(2,1)S(1)}, bf16[16,6272]{1,0:T(8,128)(2,1)S(1)}, u32[]{:S(2)}, u32[]{:S(2)}) collective-permute-start(bf16[16,6272]{1,0:T(8,128)(2,1)S(1)} %join.3.refs_0_), channel_id=1, source_target_pairs={{0,8},{4,12},{8,0},{12,4},{1,9},{5,13},{9,1},{13,5},{2,10},{6,14},... | collective-permute-start | bytes 602120 | tf_op jit(solution)/shard_map/ppermute | solution.py:307
  24.3 1.5 %collective-permute-start.3 = (bf16[16,6272]{1,0:T(8,128)(2,1)S(1)}, bf16[16,6272]{1,0:T(8,128)(2,1)S(1)}, u32[]{:S(2)}, u32[]{:S(2)}) collective-permute-start(bf16[16,6272]{1,0:T(8,128)(2,1)S(1)} %join.3.refs_0_), channel_id=1, source_target_pairs={{0,4},{4,0},{8,12},{12,8},{1,5},{5,1},{9,13},{13,9},{2,6},{6,2},{1... | collective-permute-start | bytes 602120 | tf_op jit(solution)/shard_map/ppermute | solution.py:307
  24.4 1.7 %collective-permute-start.4 = (bf16[16,6272]{1,0:T(8,128)(2,1)S(1)}, bf16[16,6272]{1,0:T(8,128)(2,1)S(1)}, u32[]{:S(2)}, u32[]{:S(2)}) collective-permute-start(bf16[16,6272]{1,0:T(8,128)(2,1)S(1)} %collective-permute-done.2.refs_1_), channel_id=1, source_target_pairs={{0,4},{4,0},{8,12},{12,8},{1,5},{5,1},{9,13},{13,9},{2,6},{6,2},{1... | collective-permute-start | bytes 602120 | tf_op jit(solution)/shard_map/ppermute | solution.py:307
  39.8 1.5 %collective-permute-start.6 = (bf16[16,6144]{1,0:T(8,128)(2,1)S(1)}, bf16[16,6144]{1,0:T(8,128)(2,1)S(1)}, u32[]{:S(2)}, u32[]{:S(2)}) collective-permute-start(bf16[16,6144]{1,0:T(8,128)(2,1)S(1)} %get-tuple-element.38), channel_id=1, source_target_pairs={{0,4},{4,0},{8,12},{12,8},{1,5},{5,1},{9,13},{13,9},{2,6},{6,2},{1... | collective-permute-start | bytes 589832 | tf_op jit(solution)/shard_map/ppermute | solution.py:307
  40.1 2.5 %collective-permute-start.5 = (bf16[16,6144]{1,0:T(8,128)(2,1)S(1)}, bf16[16,6144]{1,0:T(8,128)(2,1)S(1)}, u32[]{:S(2)}, u32[]{:S(2)}) collective-permute-start(bf16[16,6144]{1,0:T(8,128)(2,1)S(1)} %get-tuple-element.36), channel_id=1, source_target_pairs={{0,4},{4,0},{8,12},{12,8},{1,5},{5,1},{9,13},{13,9},{2,6},{6,2},{1... | collective-permute-start | bytes 589832 | tf_op jit(solution)/shard_map/ppermute | solution.py:307
  41.5 6.1 %collective-permute-start.7 = (bf16[3,4,6144]{2,1,0:T(4,128)(2,1)S(1)}, bf16[3,4,6144]{2,1,0:T(4,128)(2,1)S(1)}, u32[]{:S(2)}, u32[]{:S(2)}) collective-permute-start(bf16[3,4,6144]{2,1,0:T(4,128)(2,1)S(1)} %slice.30), channel_id=1, source_target_pairs={{0,8},{4,12},{8,0},{12,4},{1,9},{5,13},{9,1},{13,5},{2,10},{6,14},... | collective-permute-start | bytes 442376 | tf_op jit(solution)/shard_map/ppermute | solution.py:307
  47.6 5.6 %collective-permute-start.8 = (bf16[4,6144]{1,0:T(4,128)(2,1)S(1)}, bf16[4,6144]{1,0:T(4,128)(2,1)S(1)}, u32[]{:S(2)}, u32[]{:S(2)}) collective-permute-start(bf16[4,6144]{1,0:T(4,128)(2,1)S(1)} %slice.38), channel_id=1, source_target_pairs={{0,8},{4,12},{8,0},{12,4},{1,9},{5,13},{9,1},{13,5},{2,10},{6,14},... | collective-permute-start | bytes 147464 | tf_op jit(solution)/shard_map/ppermute | solution.py:307
  48.7 6.5 %collective-permute-start.9 = (bf16[4,6144]{1,0:T(4,128)(2,1)S(1)}, bf16[4,6144]{1,0:T(4,128)(2,1)S(1)}, u32[]{:S(2)}, u32[]{:S(2)}) collective-permute-start(bf16[4,6144]{1,0:T(4,128)(2,1)S(1)} %get-tuple-element.41), channel_id=1, source_target_pairs={{0,3},{1,2},{2,1},{3,0},{4,7},{5,6},{6,5},{7,4},{8,11},{9,10},{10,... | collective-permute-start | bytes 147464 | tf_op jit(solution)/shard_map/ppermute | solution.py:307
  50.7 4.6 %collective-permute-start.11 = (bf16[4,6144]{1,0:T(4,128)(2,1)S(1)}, bf16[4,6144]{1,0:T(4,128)(2,1)S(1)}, u32[]{:S(2)}, u32[]{:S(2)}) collective-permute-start(bf16[4,6144]{1,0:T(4,128)(2,1)S(1)} %get-tuple-element.42), channel_id=1, source_target_pairs={{0,1},{1,0},{2,3},{3,2},{4,5},{5,4},{6,7},{7,6},{8,9},{9,8},{10,11... | collective-permute-start | bytes 147464 | tf_op jit(solution)/shard_map/ppermute | solution.py:307
  51.5 5.0 %collective-permute-start.10 = (bf16[4,6144]{1,0:T(4,128)(2,1)S(1)}, bf16[4,6144]{1,0:T(4,128)(2,1)S(1)}, u32[]{:S(2)}, u32[]{:S(2)}) collective-permute-start(bf16[4,6144]{1,0:T(4,128)(2,1)S(1)} %get-tuple-element.43), channel_id=1, source_target_pairs={{0,2},{1,3},{2,0},{3,1},{4,6},{5,7},{6,4},{7,5},{8,10},{9,11},{10,... | collective-permute-start | bytes 147464 | tf_op jit(solution)/shard_map/ppermute | solution.py:307

commit v8 on v7

--- a/solution.py
+++ b/solution.py
@@ -10,7 +10,7 @@
 
 HEAD_SIZE = 128
 LANES = 128
-EARLY_BLOCKS = (3, 1)
+EARLY_BLOCKS = (1, 1)
 BLOCKS = 8
 F32 = jnp.float32
 BF16 = jnp.bfloat16
@@ -348,8 +348,7 @@
         second, third = spans(hidden_units)[1:]
         early, more = EARLY_BLOCKS
         waiting = [
-            [down_blocks(0, early)],
-            [gate_part(*second)],
+            [gate_part(*second), down_blocks(0, early)],
             [gate_part(*third), down_blocks(early, more)],
         ]
 
@@ -366,8 +365,13 @@
     tp_steps = strides(lax.axis_size("tp"))
     side_steps = strides(lax.axis_size("side"))
     held = row
-    for stride in tp_steps:
-        held = join([held, beside(swap(held, "tp", stride))])
+    for steps in [tp_steps[i : i + 2] for i in range(0, len(tp_steps), 2)]:
+        away = [0]
+        for stride in steps:
+            away = away + [stride ^ k for k in away]
+        far_first = sorted(range(1, len(away)), key=lambda i: -away[i])
+        got = beside([swap(held, "tp", away[i]) for i in far_first])
+        held = join([held] + [got[far_first.index(i)] for i in range(1, len(away))])
     pieces = [held]
     for stride in side_steps:
         pieces = pieces + beside([swap(piece, "side", stride) for piece in pieces])

time: 57.4 us -> 57.2 us (level)
  waiting for transfers between devices: 10.2 us -> 11.9 us
  starting transfers between devices: 15.1 us -> 14.1 us
  Pallas kernels: 30.6 us -> 29.8 us
    pallas_call x3 -> x2, Pallas kernels: 11.9 us -> 9.7 us  [bring(): pl.pallas_call(functools.partial(bring_kernel, cuts), in_specs=[pl.BlockS...]
    ppermute x12 -> x13, waiting for transfers between devices: 10.2 us -> 11.9 us  [swap(): return lax.ppermute(value, axis, [(i, i ^ bits) for i in range(n)])]
    pallas_call x1, Pallas kernels: 13.7 us -> 15 us  [experts(): pl.pallas_call(functools.partial(expert_kernel, n_pieces, n_parts, n_read...]
    ppermute x12 -> x13, starting transfers between devices: 15.1 us -> 14.1 us  [swap(): return lax.ppermute(value, axis, [(i, i ^ bits) for i in range(n)])]
  transfers between devices with their start and end apart: 12 -> 13, of which waited for: 6 -> 8; matrix products, arithmetic and copies ran while one was open for 1% -> 1% of each run, Pallas kernels for 21% -> 17%
where the time goes in v8:
time: 57.2 us; the launch traced here: 57.1 us
  Pallas kernels  29.8 us (52%)
  starting transfers between devices  14.1 us (25%)
  waiting for transfers between devices  11.9 us (21%)
  other arithmetic  0.92 us (2%)
    pallas_call x1, Pallas kernels, experts(): pl.pallas_call(functools.partial(expert_kernel, n_pieces, n_parts, n_read...  15 us
    ppermute x13, starting transfers between devices, swap(): return lax.ppermute(value, axis, [(i, i ^ bits) for i in range(n)])  14.1 us
    ppermute x13, waiting for transfers between devices, swap(): return lax.ppermute(value, axis, [(i, i ^ bits) for i in range(n)])  11.9 us
    pallas_call x2, Pallas kernels, bring(): pl.pallas_call(functools.partial(bring_kernel, cuts), in_specs=[pl.BlockS...  9.7 us
    pallas_call x1, Pallas kernels, attend(): pl.pallas_call(attend_kernel, in_specs=[pl.BlockSpec(memory_space=pltpu.H...  4.98 us
  transfers between devices with their start and end apart: 13, of which 8 were waited for; matrix products, arithmetic and copies ran while one was open for 1% of the time, Pallas kernels for 17%

profile of v8, /device:TPU:0, one launch (start us, length us, event | category | flops | bytes accessed | tf_op | source)
XLA Modules:
  0.0 57.1 jit_solution(3753602689681985211)
XLA Ops:
  0.0 5.0 %attend.1 = (f32[4,6144]{1,0:T(4,128)S(1)}, bf16[4,6272]{1,0:T(4,128)(2,1)S(1)}, bf16[2,448,6144]{2,1,0:T(8,128)(2,1)S(1)}) custom-call(bf16[4,6144]{1,0:T(4,128)(2,1)} %refs_0_.1, bf16[4,6144]{1,0:T(4,128)(2,1)} %refs_1_.1, f32[1,6144]{1,0:T(1,128)} %bitcast.18, s32[1,4]{1,0:T(1,128)} %bitcast.21, s32[2,4]{1,0:T(2,128)} %bitcast.19, f32[2,4]{1,0:T(2,128)} %bitcast.20, ...), custom_call_target="tpu_custom_call" | custom-call | tf_op jit(solution)/shard_map/attend/pallas_call | solution.py:169
  5.0 3.1 %collective-permute-start.2 = (bf16[4,6272]{1,0:T(4,128)(2,1)S(1)}, bf16[4,6272]{1,0:T(4,128)(2,1)S(1)}, u32[]{:S(2)}, u32[]{:S(2)}) collective-permute-start(bf16[4,6272]{1,0:T(4,128)(2,1)S(1)} %get-tuple-element.27.refs_0_), channel_id=1, source_target_pairs={{0,1},{1,0},{2,3},{3,2},{4,5},{5,4},{6,7},{7,6},{8,9},{9,8},{10,11... | collective-permute-start | bytes 150536 | tf_op jit(solution)/shard_map/ppermute | solution.py:307
  8.1 2.6 %collective-permute-start.1 = (bf16[4,6272]{1,0:T(4,128)(2,1)S(1)}, bf16[4,6272]{1,0:T(4,128)(2,1)S(1)}, u32[]{:S(2)}, u32[]{:S(2)}) collective-permute-start(bf16[4,6272]{1,0:T(4,128)(2,1)S(1)} %get-tuple-element.27.refs_0_), channel_id=1, source_target_pairs={{0,2},{1,3},{2,0},{3,1},{4,6},{5,7},{6,4},{7,5},{8,10},{9,11},{10,... | collective-permute-start | bytes 150536 | tf_op jit(solution)/shard_map/ppermute | solution.py:307
  10.7 5.0 %bring.2 = (bf16[2,448,6144]{2,1,0:T(8,128)(2,1)S(1)}, bf16[1344,768]{1,0:T(8,128)(2,1)S(1)}) custom-call(bf16[2,1344,6144]{2,1,0:T(8,128)(2,1)} %bitcast.13, bf16[1344,6144]{1,0:T(8,128)(2,1)} %bitcast.15), custom_call_target="tpu_custom_call" | custom-call | bytes 13074432 | tf_op jit(solution)/shard_map/bring/pallas_call | solution.py:148
  15.6 0.9 %collective-permute-done.refs_3_ = bf16[4,6272]{1,0:T(4,128)(2,1)S(1)} collective-permute-done((bf16[4,6272]{1,0:T(4,128)(2,1)S(1)}, bf16[4,6272]{1,0:T(4,128)(2,1)S(1)}, u32[]{:S(2)}, u32[]{:S(2)}) %collective-permute-start) | collective-permute-done | bytes 50208 | tf_op jit(solution)/shard_map/ppermute | solution.py:307
  16.6 1.6 %collective-permute-start.3 = (bf16[16,6272]{1,0:T(8,128)(2,1)S(1)}, bf16[16,6272]{1,0:T(8,128)(2,1)S(1)}, u32[]{:S(2)}, u32[]{:S(2)}) collective-permute-start(bf16[16,6272]{1,0:T(8,128)(2,1)S(1)} %join.1.refs_0_), channel_id=1, source_target_pairs={{0,8},{4,12},{8,0},{12,4},{1,9},{5,13},{9,1},{13,5},{2,10},{6,14},... | collective-permute-start | bytes 602120 | tf_op jit(solution)/shard_map/ppermute | solution.py:307
  18.2 4.7 %bring.3 = (bf16[2,448,6144]{2,1,0:T(8,128)(2,1)S(1)}, bf16[1344,768]{1,0:T(8,128)(2,1)S(1)}) custom-call(bf16[2,1344,6144]{2,1,0:T(8,128)(2,1)} %bitcast.14, bf16[1344,6144]{1,0:T(8,128)(2,1)} %bitcast.16), custom_call_target="tpu_custom_call" | custom-call | bytes 13074432 | tf_op jit(solution)/shard_map/bring/pallas_call | solution.py:148
  23.0 0.5 collective-permute-start.5
  23.5 0.9 %collective-permute-done.4.refs_2_ = bf16[16,6272]{1,0:T(8,128)(2,1)S(1)} collective-permute-done((bf16[16,6272]{1,0:T(8,128)(2,1)S(1)}, bf16[16,6272]{1,0:T(8,128)(2,1)S(1)}, u32[]{:S(2)}, u32[]{:S(2)}) %collective-permute-start.4) | collective-permute-done | bytes 200736 | tf_op jit(solution)/shard_map/ppermute | solution.py:307
  24.4 0.3 collective-permute-done.5.refs_3_
  24.7 15.0 %experts.1 = (bf16[16,6144]{1,0:T(8,128)(2,1)S(1)}, bf16[16,6144]{1,0:T(8,128)(2,1)S(1)}, bf16[16,6144]{1,0:T(8,128)(2,1)S(1)}, bf16[16,6144]{1,0:T(8,128)(2,1)S(1)}) custom-call(bf16[16,6272]{1,0:T(8,128)(2,1)S(1)} %join.1.refs_0_, bf16[16,6272]{1,0:T(8,128)(2,1)S(1)} %collective-permute-done.3.refs_1_, ...), custom_call_target="tpu_custom_call" | custom-call | tf_op jit(solution)/shard_map/experts/pallas_call | solution.py:281
  39.8 0.3 collective-permute-start.7
  40.1 0.3 collective-permute-start.6
  40.4 0.9 %collective-permute-done.7 = bf16[16,6144]{1,0:T(8,128)(2,1)S(1)} collective-permute-done((bf16[16,6144]{1,0:T(8,128)(2,1)S(1)}, bf16[16,6144]{1,0:T(8,128)(2,1)S(1)}, u32[]{:S(2)}, u32[]{:S(2)}) %collective-permute-start.7) | collective-permute-done | bytes 196640 | tf_op jit(solution)/shard_map/ppermute | solution.py:307
  41.5 0.7 %collective-permute-start.8 = (bf16[3,4,6144]{2,1,0:T(4,128)(2,1)S(1)}, bf16[3,4,6144]{2,1,0:T(4,128)(2,1)S(1)}, u32[]{:S(2)}, u32[]{:S(2)}) collective-permute-start(bf16[3,4,6144]{2,1,0:T(4,128)(2,1)S(1)} %slice.30), channel_id=1, source_target_pairs={{0,8},{4,12},{8,0},{12,4},{1,9},{5,13},{9,1},{13,5},{2,10},{6,14},... | collective-permute-start | bytes 442376 | tf_op jit(solution)/shard_map/ppermute | solution.py:307
  42.3 0.1 reshape.18
  42.4 5.2 %collective-permute-done.8 = bf16[3,4,6144]{2,1,0:T(4,128)(2,1)S(1)} collective-permute-done((bf16[3,4,6144]{2,1,0:T(4,128)(2,1)S(1)}, bf16[3,4,6144]{2,1,0:T(4,128)(2,1)S(1)}, u32[]{:S(2)}, u32[]{:S(2)}) %collective-permute-start.8) | collective-permute-done | bytes 147488 | tf_op jit(solution)/shard_map/ppermute | solution.py:307
  47.6 0.6 %collective-permute-start.9 = (bf16[4,6144]{1,0:T(4,128)(2,1)S(1)}, bf16[4,6144]{1,0:T(4,128)(2,1)S(1)}, u32[]{:S(2)}, u32[]{:S(2)}) collective-permute-start(bf16[4,6144]{1,0:T(4,128)(2,1)S(1)} %slice.38), channel_id=1, source_target_pairs={{0,8},{4,12},{8,0},{12,4},{1,9},{5,13},{9,1},{13,5},{2,10},{6,14},... | collective-permute-start | bytes 147464 | tf_op jit(solution)/shard_map/ppermute | solution.py:307
  48.3 3.1 %collective-permute-start.10 = (bf16[4,6144]{1,0:T(4,128)(2,1)S(1)}, bf16[4,6144]{1,0:T(4,128)(2,1)S(1)}, u32[]{:S(2)}, u32[]{:S(2)}) collective-permute-start(bf16[4,6144]{1,0:T(4,128)(2,1)S(1)} %get-tuple-element.47), channel_id=1, source_target_pairs={{0,3},{1,2},{2,1},{3,0},{4,7},{5,6},{6,5},{7,4},{8,11},{9,10},{10,... | collective-permute-start | bytes 147464 | tf_op jit(solution)/shard_map/ppermute | solution.py:307
  51.4 1.3 %collective-permute-start.11 = (bf16[4,6144]{1,0:T(4,128)(2,1)S(1)}, bf16[4,6144]{1,0:T(4,128)(2,1)S(1)}, u32[]{:S(2)}, u32[]{:S(2)}) collective-permute-start(bf16[4,6144]{1,0:T(4,128)(2,1)S(1)} %get-tuple-element.49), channel_id=1, source_target_pairs={{0,2},{1,3},{2,0},{3,1},{4,6},{5,7},{6,4},{7,5},{8,10},{9,11},{10,... | collective-permute-start | bytes 147464 | tf_op jit(solution)/shard_map/ppermute | solution.py:307
  52.7 1.6 %collective-permute-done.10 = bf16[4,6144]{1,0:T(4,128)(2,1)S(1)} collective-permute-done((bf16[4,6144]{1,0:T(4,128)(2,1)S(1)}, bf16[4,6144]{1,0:T(4,128)(2,1)S(1)}, u32[]{:S(2)}, u32[]{:S(2)}) %collective-permute-start.10) | collective-permute-done | bytes 49184 | tf_op jit(solution)/shard_map/ppermute | solution.py:307
  54.3 1.2 %collective-permute-done.12 = bf16[4,6144]{1,0:T(4,128)(2,1)S(1)} collective-permute-done((bf16[4,6144]{1,0:T(4,128)(2,1)S(1)}, bf16[4,6144]{1,0:T(4,128)(2,1)S(1)}, u32[]{:S(2)}, u32[]{:S(2)}) %collective-permute-start.12) | collective-permute-done | bytes 49184 | tf_op jit(solution)/shard_map/ppermute | solution.py:307
  55.5 0.9 %collective-permute-done.11 = bf16[4,6144]{1,0:T(4,128)(2,1)S(1)} collective-permute-done((bf16[4,6144]{1,0:T(4,128)(2,1)S(1)}, bf16[4,6144]{1,0:T(4,128)(2,1)S(1)}, u32[]{:S(2)}, u32[]{:S(2)}) %collective-permute-start.11) | collective-permute-done | bytes 49184 | tf_op jit(solution)/shard_map/ppermute | solution.py:307
  56.4 0.7 %add_convert_fusion.3 = bf16[4,6144]{1,0:T(4,128)(2,1)} fusion(bf16[4,6144]{1,0:T(4,128)(2,1)S(1)} %collective-permute-done.12, bf16[4,6144]{1,0:T(4,128)(2,1)S(1)} %collective-permute-done.11, bf16[4,6144]{1,0:T(4,128)(2,1)S(1)} %collective-permute-done.10, f32[4,6144]{1,0:T(4,128)S(1)} %get-tuple-element.26, bf16[4,6144]{1,0:T(4,128)(2,1)S(1)} %collective-permute-done.9, ...), kind=kLoop, calls=%fused_computation.4 | loop fusion | flops 270336 | bytes 393216 | tf_op jit(solution)/shard_map/convert_element_type | solution.py:405
  (17 shorter events, 0.6 us)
Async XLA Ops:
  5.0 10.6 %collective-permute-start.2 = (bf16[4,6272]{1,0:T(4,128)(2,1)S(1)}, bf16[4,6272]{1,0:T(4,128)(2,1)S(1)}, u32[]{:S(2)}, u32[]{:S(2)}) collective-permute-start(bf16[4,6272]{1,0:T(4,128)(2,1)S(1)} %get-tuple-element.27.refs_0_), channel_id=1, source_target_pairs={{0,1},{1,0},{2,3},{3,2},{4,5},{5,4},{6,7},{7,6},{8,9},{9,8},{10,11... | collective-permute-start | bytes 150536 | tf_op jit(solution)/shard_map/ppermute | solution.py:307
  8.1 7.6 %collective-permute-start.1 = (bf16[4,6272]{1,0:T(4,128)(2,1)S(1)}, bf16[4,6272]{1,0:T(4,128)(2,1)S(1)}, u32[]{:S(2)}, u32[]{:S(2)}) collective-permute-start(bf16[4,6272]{1,0:T(4,128)(2,1)S(1)} %get-tuple-element.27.refs_0_), channel_id=1, source_target_pairs={{0,2},{1,3},{2,0},{3,1},{4,6},{5,7},{6,4},{7,5},{8,10},{9,11},{10,... | collective-permute-start | bytes 150536 | tf_op jit(solution)/shard_map/ppermute | solution.py:307
  10.7 5.9 %collective-permute-start = (bf16[4,6272]{1,0:T(4,128)(2,1)S(1)}, bf16[4,6272]{1,0:T(4,128)(2,1)S(1)}, u32[]{:S(2)}, u32[]{:S(2)}) collective-permute-start(bf16[4,6272]{1,0:T(4,128)(2,1)S(1)} %get-tuple-element.27.refs_0_), channel_id=1, source_target_pairs={{0,3},{1,2},{2,1},{3,0},{4,7},{5,6},{6,5},{7,4},{8,11},{9,10},{10,... | collective-permute-start | bytes 150536 | tf_op jit(solution)/shard_map/ppermute | solution.py:307
  16.6 6.4 %collective-permute-start.3 = (bf16[16,6272]{1,0:T(8,128)(2,1)S(1)}, bf16[16,6272]{1,0:T(8,128)(2,1)S(1)}, u32[]{:S(2)}, u32[]{:S(2)}) collective-permute-start(bf16[16,6272]{1,0:T(8,128)(2,1)S(1)} %join.1.refs_0_), channel_id=1, source_target_pairs={{0,8},{4,12},{8,0},{12,4},{1,9},{5,13},{9,1},{13,5},{2,10},{6,14},... | collective-permute-start | bytes 602120 | tf_op jit(solution)/shard_map/ppermute | solution.py:307
  22.9 1.5 %collective-permute-start.4 = (bf16[16,6272]{1,0:T(8,128)(2,1)S(1)}, bf16[16,6272]{1,0:T(8,128)(2,1)S(1)}, u32[]{:S(2)}, u32[]{:S(2)}) collective-permute-start(bf16[16,6272]{1,0:T(8,128)(2,1)S(1)} %join.1.refs_0_), channel_id=1, source_target_pairs={{0,4},{4,0},{8,12},{12,8},{1,5},{5,1},{9,13},{13,9},{2,6},{6,2},{1... | collective-permute-start | bytes 602120 | tf_op jit(solution)/shard_map/ppermute | solution.py:307
  23.0 1.7 %collective-permute-start.5 = (bf16[16,6272]{1,0:T(8,128)(2,1)S(1)}, bf16[16,6272]{1,0:T(8,128)(2,1)S(1)}, u32[]{:S(2)}, u32[]{:S(2)}) collective-permute-start(bf16[16,6272]{1,0:T(8,128)(2,1)S(1)} %collective-permute-done.3.refs_1_), channel_id=1, source_target_pairs={{0,4},{4,0},{8,12},{12,8},{1,5},{5,1},{9,13},{13,9},{2,6},{6,2},{1... | collective-permute-start | bytes 602120 | tf_op jit(solution)/shard_map/ppermute | solution.py:307
  39.8 1.5 %collective-permute-start.7 = (bf16[16,6144]{1,0:T(8,128)(2,1)S(1)}, bf16[16,6144]{1,0:T(8,128)(2,1)S(1)}, u32[]{:S(2)}, u32[]{:S(2)}) collective-permute-start(bf16[16,6144]{1,0:T(8,128)(2,1)S(1)} %get-tuple-element.44), channel_id=1, source_target_pairs={{0,4},{4,0},{8,12},{12,8},{1,5},{5,1},{9,13},{13,9},{2,6},{6,2},{1... | collective-permute-start | bytes 589832 | tf_op jit(solution)/shard_map/ppermute | solution.py:307
  40.1 2.1 %collective-permute-start.6 = (bf16[16,6144]{1,0:T(8,128)(2,1)S(1)}, bf16[16,6144]{1,0:T(8,128)(2,1)S(1)}, u32[]{:S(2)}, u32[]{:S(2)}) collective-permute-start(bf16[16,6144]{1,0:T(8,128)(2,1)S(1)} %get-tuple-element.42), channel_id=1, source_target_pairs={{0,4},{4,0},{8,12},{12,8},{1,5},{5,1},{9,13},{13,9},{2,6},{6,2},{1... | collective-permute-start | bytes 589832 | tf_op jit(solution)/shard_map/ppermute | solution.py:307
  41.5 6.1 %collective-permute-start.8 = (bf16[3,4,6144]{2,1,0:T(4,128)(2,1)S(1)}, bf16[3,4,6144]{2,1,0:T(4,128)(2,1)S(1)}, u32[]{:S(2)}, u32[]{:S(2)}) collective-permute-start(bf16[3,4,6144]{2,1,0:T(4,128)(2,1)S(1)} %slice.30), channel_id=1, source_target_pairs={{0,8},{4,12},{8,0},{12,4},{1,9},{5,13},{9,1},{13,5},{2,10},{6,14},... | collective-permute-start | bytes 442376 | tf_op jit(solution)/shard_map/ppermute | solution.py:307
  47.6 5.1 %collective-permute-start.9 = (bf16[4,6144]{1,0:T(4,128)(2,1)S(1)}, bf16[4,6144]{1,0:T(4,128)(2,1)S(1)}, u32[]{:S(2)}, u32[]{:S(2)}) collective-permute-start(bf16[4,6144]{1,0:T(4,128)(2,1)S(1)} %slice.38), channel_id=1, source_target_pairs={{0,8},{4,12},{8,0},{12,4},{1,9},{5,13},{9,1},{13,5},{2,10},{6,14},... | collective-permute-start | bytes 147464 | tf_op jit(solution)/shard_map/ppermute | solution.py:307
  48.3 6.1 %collective-permute-start.10 = (bf16[4,6144]{1,0:T(4,128)(2,1)S(1)}, bf16[4,6144]{1,0:T(4,128)(2,1)S(1)}, u32[]{:S(2)}, u32[]{:S(2)}) collective-permute-start(bf16[4,6144]{1,0:T(4,128)(2,1)S(1)} %get-tuple-element.47), channel_id=1, source_target_pairs={{0,3},{1,2},{2,1},{3,0},{4,7},{5,6},{6,5},{7,4},{8,11},{9,10},{10,... | collective-permute-start | bytes 147464 | tf_op jit(solution)/shard_map/ppermute | solution.py:307
  51.4 4.1 %collective-permute-start.12 = (bf16[4,6144]{1,0:T(4,128)(2,1)S(1)}, bf16[4,6144]{1,0:T(4,128)(2,1)S(1)}, u32[]{:S(2)}, u32[]{:S(2)}) collective-permute-start(bf16[4,6144]{1,0:T(4,128)(2,1)S(1)} %get-tuple-element.48), channel_id=1, source_target_pairs={{0,1},{1,0},{2,3},{3,2},{4,5},{5,4},{6,7},{7,6},{8,9},{9,8},{10,11... | collective-permute-start | bytes 147464 | tf_op jit(solution)/shard_map/ppermute | solution.py:307
  51.4 5.0 %collective-permute-start.11 = (bf16[4,6144]{1,0:T(4,128)(2,1)S(1)}, bf16[4,6144]{1,0:T(4,128)(2,1)S(1)}, u32[]{:S(2)}, u32[]{:S(2)}) collective-permute-start(bf16[4,6144]{1,0:T(4,128)(2,1)S(1)} %get-tuple-element.49), channel_id=1, source_target_pairs={{0,2},{1,3},{2,0},{3,1},{4,6},{5,7},{6,4},{7,5},{8,10},{9,11},{10,... | collective-permute-start | bytes 147464 | tf_op jit(solution)/shard_map/ppermute | solution.py:307
